TPU v7x, 32 devices: a whole 2x2x4 slice. The times are simulated.
32 devices in a mesh: gx: 4 (over z), gy: 4 (over y, x), comp: 2 (over core).
Axes of the slice: x: 2, y: 2, z: 4, core: 2. Of those that a mesh axis runs over, the one named last changes fastest.
Arguments:
- spectrum: bfloat16 [64, 512, 1024], P('gx', 'gy', 'comp'), may hold values from -6 to 6
- sea_mask: int32 [64, 512], P('gx', 'gy'), may hold values 0 or 1
- courant: float32 [2, 1024], P(None, 'comp'), may hold values from -0.45 to 0.45
- interaction: bfloat16 [1024, 1024], replicated, may hold values from -0.1875 to 0.1875
- stokes_proj: bfloat16 [2, 1024, 64], replicated, may hold values from -0.1875 to 0.1875
- currents: float32 [2, 64, 64, 512], P(None, 'comp', 'gx', 'gy'), may hold values from -6 to 6
- level_drag: float32 [64], P('comp'), may hold values from 0.05 to 0.5
Outputs:
- wave_out: bfloat16 [64, 512, 1024], P('gx', 'gy', 'comp')
- currents_out: float32 [2, 64, 64, 512], P(None, 'comp', 'gx', 'gy')
All inputs are finite; a program needn't handle non-finite values. No bound on the sum of `sea_mask` on one device may be relied on, other than what follows from the above.
Results may differ from a plain program's by a relative error of at most 0.0049.
Values may be sent and summed in bfloat16 or wider, within the bound.
No kernel may reach another device: no remote copies, remote signals or barrier semaphores. Data moves between devices by JAX's collectives and lax.ppermute only.
A program may use at most 64 MiB of HBM per device.

v0:
```python
import jax
import jax.numpy as jnp
from jax import lax
from jax.sharding import PartitionSpec as P

SUBSTEPS = 3


time_step = 0.5
viscosity = 0.4


def padded_2(block, sides, width, periodic):
    for axis, dim in sides:
        count = lax.axis_size(axis)
        forward = [(i, i + 1) for i in range(count - 1)]
        if periodic:
            forward.append((count - 1, 0))
        backward = [(target, source) for source, target in forward]
        low = lax.ppermute(
            lax.slice_in_dim(block, block.shape[dim] - width, None, axis=dim), axis, forward
        )
        high = lax.ppermute(lax.slice_in_dim(block, 0, width, axis=dim), axis, backward)
        block = jnp.concatenate([low, block, high], axis=dim)
    return block


def upwind(centre, west_cell, east_cell, south_cell, north_cell, courant):
    cour_x = courant[0]
    cour_y = courant[1]
    return (
        centre
        - jnp.maximum(cour_x, 0.0) * (centre - west_cell)
        - jnp.minimum(cour_x, 0.0) * (east_cell - centre)
        - jnp.maximum(cour_y, 0.0) * (centre - south_cell)
        - jnp.minimum(cour_y, 0.0) * (north_cell - centre)
    )


def substep(u_pad, v_pad, stokes_u, stokes_v, coriolis, sea_cells, level_drag):
    u_mid = u_pad[:, 1:-1, 1:-1]
    v_mid = v_pad[:, 1:-1, 1:-1]
    vorticity = 0.5 * (v_pad[:, 2:, 1:-1] - v_pad[:, :-2, 1:-1]) - 0.5 * (
        u_pad[:, 1:-1, 2:] - u_pad[:, 1:-1, :-2]
    )
    lap_u = (
        u_pad[:, 2:, 1:-1]
        + u_pad[:, :-2, 1:-1]
        + u_pad[:, 1:-1, 2:]
        + u_pad[:, 1:-1, :-2]
        - 4.0 * u_mid
    )
    lap_v = (
        v_pad[:, 2:, 1:-1]
        + v_pad[:, :-2, 1:-1]
        + v_pad[:, 1:-1, 2:]
        + v_pad[:, 1:-1, :-2]
        - 4.0 * v_mid
    )
    abs_vort = coriolis + vorticity
    drag_col = level_drag[:, None, None]
    u_next = u_mid + time_step * (
        abs_vort * (v_mid + stokes_v) - drag_col * u_mid + viscosity * lap_u
    )
    v_next = v_mid + time_step * (
        -abs_vort * (u_mid + stokes_u) - drag_col * v_mid + viscosity * lap_v
    )
    return (u_next * sea_cells, v_next * sea_cells)


def crop_cells(field, margin):
    return field[..., margin : field.shape[-2] - margin, margin : field.shape[-1] - margin]


def lat_coriolis(cells_y, margin):
    ny_total = lax.axis_size("gy") * cells_y
    lat_index = lax.axis_index("gy") * cells_y + jnp.arange(-margin, cells_y + margin)
    return jnp.sin(jnp.pi * ((lat_index.astype(jnp.float32) + 0.5) / ny_total - 0.5))[None, :]


def local(spectrum, sea_mask, courant, interaction, stokes_proj, currents, level_drag):
    sea_cells = sea_mask.astype(jnp.float32)
    lon_padded = padded_2(spectrum, (("gx", 0),), 1, True)
    padded = padded_2(lon_padded, (("gy", 1),), 1, False)
    centre = padded[1:-1, 1:-1].astype(jnp.float32)
    west_cell = padded[:-2, 1:-1].astype(jnp.float32)
    east_cell = padded[2:, 1:-1].astype(jnp.float32)
    south_cell = padded[1:-1, :-2].astype(jnp.float32)
    north_cell = padded[1:-1, 2:].astype(jnp.float32)
    advected = (
        upwind(centre, west_cell, east_cell, south_cell, north_cell, courant)
        * sea_cells[:, :, None]
    ).astype(jnp.bfloat16)
    cells_x, cells_y, bins_own = advected.shape
    lev_own = currents.shape[1]
    core_index = lax.axis_index("comp")
    w_cols = lax.dynamic_slice_in_dim(interaction, core_index * bins_own, bins_own, 1)
    proj_own = lax.dynamic_slice_in_dim(stokes_proj, core_index * lev_own, lev_own, 2)
    block_piece = lax.all_gather(advected, "comp", axis=2, tiled=True)
    count = block_piece.shape[2]
    flat_rows = block_piece.reshape(-1, count)
    gain_sum = jnp.dot(flat_rows, w_cols, preferred_element_type=jnp.float32)
    stokes_sum = jnp.einsum(
        "xyk,ckl->clxy", block_piece, proj_own, preferred_element_type=jnp.float32
    )
    wave_out = (
        (advected.astype(jnp.float32) + gain_sum.reshape(cells_x, cells_y, bins_own))
        * sea_cells[:, :, None]
    ).astype(jnp.bfloat16)
    stacked = jnp.concatenate(
        [
            currents.reshape(2 * lev_own, cells_x, cells_y),
            stokes_sum.reshape(2 * lev_own, cells_x, cells_y),
            sea_cells[None],
        ],
        0,
    )
    lon_state = padded_2(stacked, (("gx", 1),), SUBSTEPS, True)
    state_ext = padded_2(lon_state, (("gy", 2),), SUBSTEPS, False)
    flow = state_ext[: 2 * lev_own]
    stokes_ext = state_ext[2 * lev_own : 4 * lev_own]
    mask_ext = state_ext[4 * lev_own]
    coriolis_ext = lat_coriolis(cells_y, SUBSTEPS)
    for sub_index in range(SUBSTEPS):
        inner = sub_index + 1
        cor_now = coriolis_ext[:, inner : coriolis_ext.shape[1] - inner]
        u_next, v_next = substep(
            flow[:lev_own],
            flow[lev_own:],
            crop_cells(stokes_ext[:lev_own], inner),
            crop_cells(stokes_ext[lev_own:], inner),
            cor_now,
            crop_cells(mask_ext, inner),
            level_drag,
        )
        flow = jnp.concatenate([u_next, v_next], 0)
    currents_out = flow.reshape(2, lev_own, cells_x, cells_y)
    return (wave_out, currents_out)


def solution(mesh):
    in_specs = (
        P("gx", "gy", "comp"),
        P("gx", "gy"),
        P(None, "comp"),
        P(),
        P(),
        P(None, "comp", "gx", "gy"),
        P("comp"),
    )
    out_specs = (P("gx", "gy", "comp"), P(None, "comp", "gx", "gy"))
    return jax.shard_map(local, mesh=mesh, in_specs=in_specs, out_specs=out_specs, check_vma=False)
```

profile of v0, /device:TPU:0, one launch (start us, length us, event | category | flops | bytes accessed | tf_op | source)
XLA Modules:
  0.0 113.2 jit_solution(1719781579728695428)
XLA Ops:
  7.3 1.1 %fusion.74 = (bf16[1,128,512]{2,1,0:T(8,128)(2,1)S(1)}, bf16[1,128,512]{2,1,0:T(8,128)(2,1)S(1)}) fusion(bf16[16,128,512]{2,1,0:T(8,128)(2,1)} %param.7), kind=kLoop, calls=%fused_computation.119 | loop fusion | bytes 524288 | tf_op jit(solution)/shard_map/slice | solution.py:23
  8.4 3.1 %collective-permute-start = (bf16[1,128,512]{2,1,0:T(8,128)(2,1)S(1)}, bf16[1,128,512]{2,1,0:T(8,128)(2,1)S(1)}, u32[]{:S(2)}, u32[]{:S(2)}) collective-permute-start(bf16[1,128,512]{2,1,0:T(8,128)(2,1)S(1)} %get-tuple-element.11), channel_id=1, source_target_pairs={{0,8},{8,16},{16,24},{24,0},{1,9},{9,17},{17,25},{25,1},{2,10},{10... | collective-permute-start | bytes 393224 | tf_op jit(solution)/shard_map/ppermute | solution.py:20
  11.5 2.1 %collective-permute-start.1 = (bf16[1,128,512]{2,1,0:T(8,128)(2,1)S(1)}, bf16[1,128,512]{2,1,0:T(8,128)(2,1)S(1)}, u32[]{:S(2)}, u32[]{:S(2)}) collective-permute-start(bf16[1,128,512]{2,1,0:T(8,128)(2,1)S(1)} %get-tuple-element.10), channel_id=1, source_target_pairs={{8,0},{16,8},{24,16},{0,24},{9,1},{17,9},{25,17},{1,25},{10,2},{18... | collective-permute-start | bytes 393224 | tf_op jit(solution)/shard_map/ppermute | solution.py:23
  13.6 4.3 %collective-permute-done = bf16[1,128,512]{2,1,0:T(8,128)(2,1)S(1)} collective-permute-done((bf16[1,128,512]{2,1,0:T(8,128)(2,1)S(1)}, bf16[1,128,512]{2,1,0:T(8,128)(2,1)S(1)}, u32[]{:S(2)}, u32[]{:S(2)}) %collective-permute-start) | collective-permute-done | bytes 131104 | tf_op jit(solution)/shard_map/ppermute | solution.py:20
  17.8 1.8 %constant_dynamic-update-slice_fusion.1 = bf16[18,128,512]{2,1,0:T(8,128)(2,1)S(1)} fusion(bf16[18,128,512]{2,1,0:T(8,128)(2,1)S(1)} %constant_dynamic-update-slice_fusion.2, bf16[16,128,512]{2,1,0:T(8,128)(2,1)} %param.7), kind=kLoop, calls=%fused_computation.108 | loop fusion | bytes 4194304
  19.7 1.3 %collective-permute-start.3 = (bf16[18,1,512]{2,1,0:T(2,128)(2,1)S(1)}, bf16[18,1,512]{2,1,0:T(2,128)(2,1)S(1)}, u32[]{:S(2)}, u32[]{:S(2)}) collective-permute-start(bf16[18,1,512]{2,1,0:T(2,128)(2,1)S(1)} %get-tuple-element.9), channel_id=1, source_target_pairs={{2,0},{4,2},{6,4},{3,1},{5,3},{7,5},{10,8},{12,10},{14,12},{11,9},... | collective-permute-start | bytes 55304 | tf_op jit(solution)/shard_map/ppermute | solution.py:23
  21.0 4.5 %collective-permute-start.2 = (bf16[18,1,512]{2,1,0:T(2,128)(2,1)S(1)}, bf16[18,1,512]{2,1,0:T(2,128)(2,1)S(1)}, u32[]{:S(2)}, u32[]{:S(2)}) collective-permute-start(bf16[18,1,512]{2,1,0:T(2,128)(2,1)S(1)} %get-tuple-element.8), channel_id=1, source_target_pairs={{0,2},{2,4},{4,6},{1,3},{3,5},{5,7},{8,10},{10,12},{12,14},{9,11},... | collective-permute-start | bytes 55304 | tf_op jit(solution)/shard_map/ppermute | solution.py:20
  25.7 1.6 %collective-permute-done.2 = bf16[18,1,512]{2,1,0:T(2,128)(2,1)S(1)} collective-permute-done((bf16[18,1,512]{2,1,0:T(2,128)(2,1)S(1)}, bf16[18,1,512]{2,1,0:T(2,128)(2,1)S(1)}, u32[]{:S(2)}, u32[]{:S(2)}) %collective-permute-start.2) | collective-permute-done | bytes 18464 | tf_op jit(solution)/shard_map/ppermute | solution.py:20
  27.2 7.7 %fusion.5 = bf16[16,128,512]{2,1,0:T(8,128)(2,1)} fusion(bf16[16,128,512]{2,1,0:T(8,128)(2,1)S(1)} %copy-done.3, bf16[18,1,512]{2,1,0:T(2,128)(2,1)S(1)} %collective-permute-done.3, bf16[18,128,512]{2,1,0:T(8,128)(2,1)S(1)} %constant_dynamic-update-slice_fusion, bf16[18,1,512]{2,1,0:T(2,128)(2,1)S(1)} %collective-permute-done.2, ...), kind=kLoop, calls=%fused_computation.10 | loop fusion | flops 32505856 | bytes 6868992 | tf_op jit(solution)/shard_map/convert_element_type | solution.py:93
  35.4 16.5 %all-gather.2.cloned.1.call-done = bf16[16,128,1024]{2,1,0:T(8,128)(2,1)} async-done(((bf16[16,128,512]{2,1,0:T(8,128)(2,1)}), bf16[16,128,1024]{2,1,0:T(8,128)(2,1)}) %all-gather.2.cloned.1.call-update) | async-done | bytes 4194320 | tf_op jit(solution)/shard_map/all_gather | solution.py:99
  51.9 3.7 %fusion.9 = f32[2,32,16,128]{3,1,2,0:T(8,128)S(1)} fusion(bf16[16,128,1024]{2,1,0:T(8,128)(2,1)} %all-gather.2.cloned.1.call-done, bf16[2,1024,64]{1,2,0:T(8,128)(2,1)} %param.11, s32[]{:T(128)S(6)} %select_n.7), kind=kOutput, calls=%fused_computation.14 | convolution fusion | flops 268435456 | bytes 4849668 | tf_op jit(solution)/shard_map/xyk,ckl->clxy/dot_general | solution.py:103
  56.1 3.6 %collective-permute-start.5 = (f32[129,3,128]{2,0,1:T(8,128)S(1)}, f32[129,3,128]{2,0,1:T(8,128)S(1)}, u32[]{:S(2)}, u32[]{:S(2)}) collective-permute-start(f32[129,3,128]{2,0,1:T(8,128)S(1)} %get-tuple-element.15), channel_id=1, source_target_pairs={{8,0},{16,8},{24,16},{0,24},{9,1},{17,9},{25,17},{1,25},{10,2},{18... | collective-permute-start | bytes 594440 | tf_op jit(solution)/shard_map/ppermute | solution.py:23
  59.8 5.5 %collective-permute-done.5 = f32[129,3,128]{2,0,1:T(8,128)S(1)} collective-permute-done((f32[129,3,128]{2,0,1:T(8,128)S(1)}, f32[129,3,128]{2,0,1:T(8,128)S(1)}, u32[]{:S(2)}, u32[]{:S(2)}) %collective-permute-start.5) | collective-permute-done | bytes 198176 | tf_op jit(solution)/shard_map/ppermute | solution.py:23
  65.2 4.8 %collective-permute-done.4 = f32[129,3,128]{2,0,1:T(8,128)S(1)} collective-permute-done((f32[129,3,128]{2,0,1:T(8,128)S(1)}, f32[129,3,128]{2,0,1:T(8,128)S(1)}, u32[]{:S(2)}, u32[]{:S(2)}) %collective-permute-start.4) | collective-permute-done | bytes 198176 | tf_op jit(solution)/shard_map/ppermute | solution.py:20
  70.1 0.7 copy-done.6
  70.9 2.1 %fusion.75 = (f32[129,22,3]{2,0,1:T(8,128)}, f32[129,22,3]{2,0,1:T(8,128)}) fusion(f32[129,22,128]{2,0,1:T(8,128)S(1)} %pad_maximum_fusion.5), kind=kLoop, calls=%fused_computation.120 | loop fusion | bytes 136224 | tf_op jit(solution)/shard_map/slice | solution.py:21
  73.0 2.3 %copy.19 = f32[129,22,3]{0,1,2:T(8,128)S(1)} copy(f32[129,22,3]{2,0,1:T(8,128)} %get-tuple-element.13) | data formatting | bytes 68112 | tf_op jit(solution)/shard_map/slice | solution.py:23
  75.2 1.3 %collective-permute-start.7 = (f32[129,22,3]{0,1,2:T(8,128)S(1)}, f32[129,22,3]{0,1,2:T(8,128)S(1)}, u32[]{:S(2)}, u32[]{:S(2)}) collective-permute-start(f32[129,22,3]{0,1,2:T(8,128)S(1)} %copy.19), channel_id=1, source_target_pairs={{2,0},{4,2},{6,4},{3,1},{5,3},{7,5},{10,8},{12,10},{14,12},{11,9},... | collective-permute-start | bytes 102176 | tf_op jit(solution)/shard_map/ppermute | solution.py:23
  76.5 2.9 %copy.18 = f32[129,22,3]{0,1,2:T(8,128)} copy(f32[129,22,3]{2,0,1:T(8,128)} %get-tuple-element.12) | data formatting | bytes 68112 | tf_op jit(solution)/shard_map/slice | solution.py:21
  79.5 5.2 %collective-permute-start.6 = (f32[129,22,3]{0,1,2:T(8,128)}, f32[129,22,3]{0,1,2:T(8,128)}, u32[]{:S(2)}, u32[]{:S(2)}) collective-permute-start(f32[129,22,3]{0,1,2:T(8,128)} %copy.18), channel_id=1, source_target_pairs={{0,2},{2,4},{4,6},{1,3},{3,5},{5,7},{8,10},{10,12},{12,14},{9,11},... | collective-permute-start | bytes 102176 | tf_op jit(solution)/shard_map/ppermute | solution.py:20
  84.6 6.7 %multiply_convert_fusion = bf16[16,128,512]{2,1,0:T(8,128)(2,1)} fusion(bf16[16,128,512]{2,1,0:T(8,128)(2,1)} %fusion.5, f32[16,128]{1,0:T(8,128)S(1)} %convert_element_type.42, bf16[16,128,1024]{2,1,0:T(8,128)(2,1)} %all-gather.2.cloned.1.call-done, bf16[1024,1024]{1,0:T(8,128)(2,1)S(1)} %copy-done, s32[]{:T(128)S(6)} %select_n.6), kind=kOutput, calls=%fused_computation.16 | convolution fusion | flops 2151677952 | bytes 9445380 | tf_op jit(solution)/shard_map/dot_general | solution.py:102
  91.3 1.7 %copy.21 = f32[129,22,3]{2,0,1:T(8,128)} copy(f32[129,22,3]{0,1,2:T(8,128)S(1)} %collective-permute-done.7) | data formatting | bytes 68112 | tf_op jit(solution)/shard_map/ppermute | solution.py:23
  93.0 2.6 %copy.20 = f32[129,22,3]{2,0,1:T(8,128)} copy(f32[129,22,3]{0,1,2:T(8,128)} %collective-permute-done.6) | data formatting | bytes 68112 | tf_op jit(solution)/shard_map/ppermute | solution.py:20
  95.6 1.2 %pad_maximum_fusion.10 = f32[1,22,134]{2,0,1:T(1,128)S(1)} fusion(f32[129,22,3]{2,0,1:T(8,128)} %copy.21, f32[129,22,3]{2,0,1:T(8,128)} %copy.20, f32[129,3,128]{2,0,1:T(8,128)S(1)} %collective-permute-done.5, f32[129,3,128]{2,0,1:T(8,128)} %copy-done.6, f32[1,16,128]{2,0,1:T(1,128)S(1)} %bitcast.55, f32[64,16,128]{2,0,1:T(8,128)S(1)} %copy.17, ...), kind=kLoop, calls=%fused_computation.106 | loop fusion | flops 17688 | bytes 1532960 | tf_op jit(solution)/shard_map/slice | solution.py:122
  97.5 1.3 %pad_maximum_fusion = f32[129,22,134]{2,0,1:T(8,128)S(1)} fusion(f32[129,22,3]{2,0,1:T(8,128)S(1)} %copy-done.1, f32[129,3,128]{2,0,1:T(8,128)S(1)} %collective-permute-done.5, f32[1,16,128]{2,0,1:T(1,128)S(1)} %bitcast.56, f32[64,16,128]{2,0,1:T(8,128)S(1)} %copy.17, f32[64,16,128]{2,0,1:T(8,128)S(1)} %bitcast.50, f32[129,3,128]{2,0,1:T(8,128)S(1)} %copy-done.7, ...), kind=kLoop, calls=%fused_computation.17 | loop fusion | flops 2281752 | bytes 3042336 | tf_op jit(solution)/shard_map/concatenate | solution.py:24
  98.8 1.3 %fusion.18 = f32[32,20,132]{2,0,1:T(8,128)S(1)} fusion(f32[129,22,134]{2,0,1:T(8,128)S(1)} %pad_maximum_fusion, f32[20,132]{1,0:T(8,128)S(1)} %slice.302, f32[32]{0:T(128)S(1)} %copy-done.9, f32[132]{0:T(256)S(1)} %bitcast.62), kind=kLoop, calls=%fused_computation.31 | loop fusion | flops 1774080 | bytes 3390416 | tf_op jit(solution)/shard_map/mul | solution.py:68
  100.1 1.4 %fusion.28 = f32[32,20,132]{2,0,1:T(8,128)S(1)} fusion(f32[129,22,134]{2,0,1:T(8,128)S(1)} %pad_maximum_fusion, f32[20,132]{1,0:T(8,128)S(1)} %slice.302, f32[32]{0:T(128)S(1)} %copy-done.9, f32[132]{0:T(256)S(1)} %bitcast.63), kind=kLoop, calls=%fused_computation.44 | loop fusion | flops 1689600 | bytes 3390416 | tf_op jit(solution)/shard_map/mul | solution.py:68
  101.6 1.2 %fusion.36 = f32[32,18,130]{2,0,1:T(8,128)S(1)} fusion(f32[32,20,132]{2,0,1:T(8,128)S(1)} %fusion.18, f32[129,22,134]{2,0,1:T(8,128)S(1)} %pad_maximum_fusion, f32[32,20,132]{2,0,1:T(8,128)S(1)} %fusion.28, f32[18,130]{1,0:T(8,128)S(1)} %slice.316, f32[32]{0:T(128)S(1)} %copy-done.9, f32[130]{0:T(256)S(1)} %bitcast.60), kind=kLoop, calls=%fused_computation.55 | loop fusion | flops 1572480 | bytes 3005208 | tf_op jit(solution)/shard_map/mul | solution.py:68
  102.8 1.3 %fusion.46 = f32[32,18,130]{2,0,1:T(8,128)S(1)} fusion(f32[32,20,132]{2,0,1:T(8,128)S(1)} %fusion.28, f32[129,22,134]{2,0,1:T(8,128)S(1)} %pad_maximum_fusion, f32[32,20,132]{2,0,1:T(8,128)S(1)} %fusion.18, f32[18,130]{1,0:T(8,128)S(1)} %slice.316, f32[32]{0:T(128)S(1)} %copy-done.9, f32[130]{0:T(256)S(1)} %bitcast.61), kind=kLoop, calls=%fused_computation.68 | loop fusion | flops 1497600 | bytes 3005208 | tf_op jit(solution)/shard_map/mul | solution.py:68
  104.1 0.5 fusion.54
  104.6 0.6 fusion.65
  105.2 1.1 copy.22
  (49 shorter events, 2.2 us)
Async XLA Ops:
  7.2 77.5 %copy-start = (bf16[1024,1024]{1,0:T(8,128)(2,1)S(1)}, bf16[1024,1024]{1,0:T(8,128)(2,1)}, u32[]{:S(2)}) copy-start(bf16[1024,1024]{1,0:T(8,128)(2,1)} %param.10) | copy-start | bytes 6291460
  7.2 18.4 %copy-start.11 = (f32[2,512]{1,0:T(2,128)S(1)}, f32[2,512]{1,0:T(2,128)}, u32[]{:S(2)}) copy-start(f32[2,512]{1,0:T(2,128)} %param.9) | copy-start | bytes 12292
  7.2 18.4 %copy-start.10 = (s32[16,128]{1,0:T(8,128)S(1)}, s32[16,128]{1,0:T(8,128)}, u32[]{:S(2)}) copy-start(s32[16,128]{1,0:T(8,128)} %param.8) | copy-start | bytes 24580
  7.2 44.7 %all-gather.2.cloned.1.call-start = ((), (), s32[]{:S(2)}) async-start(), calls=%async_computation | async-start | bytes 6291456 | tf_op jit(solution)/shard_map/all_gather | solution.py:99
  7.2 20.0 %copy-start.3 = (bf16[16,128,512]{2,1,0:T(8,128)(2,1)S(1)}, bf16[16,128,512]{2,1,0:T(8,128)(2,1)}, u32[]{:S(2)}) copy-start(bf16[16,128,512]{2,1,0:T(8,128)(2,1)} %param.7) | copy-start | bytes 6291460
  8.4 9.4 %collective-permute-start = (bf16[1,128,512]{2,1,0:T(8,128)(2,1)S(1)}, bf16[1,128,512]{2,1,0:T(8,128)(2,1)S(1)}, u32[]{:S(2)}, u32[]{:S(2)}) collective-permute-start(bf16[1,128,512]{2,1,0:T(8,128)(2,1)S(1)} %get-tuple-element.11), channel_id=1, source_target_pairs={{0,8},{8,16},{16,24},{24,0},{1,9},{9,17},{17,25},{25,1},{2,10},{10... | collective-permute-start | bytes 393224 | tf_op jit(solution)/shard_map/ppermute | solution.py:20
  11.5 8.2 %collective-permute-start.1 = (bf16[1,128,512]{2,1,0:T(8,128)(2,1)S(1)}, bf16[1,128,512]{2,1,0:T(8,128)(2,1)S(1)}, u32[]{:S(2)}, u32[]{:S(2)}) collective-permute-start(bf16[1,128,512]{2,1,0:T(8,128)(2,1)S(1)} %get-tuple-element.10), channel_id=1, source_target_pairs={{8,0},{16,8},{24,16},{0,24},{9,1},{17,9},{25,17},{1,25},{10,2},{18... | collective-permute-start | bytes 393224 | tf_op jit(solution)/shard_map/ppermute | solution.py:23
  19.7 5.9 %collective-permute-start.3 = (bf16[18,1,512]{2,1,0:T(2,128)(2,1)S(1)}, bf16[18,1,512]{2,1,0:T(2,128)(2,1)S(1)}, u32[]{:S(2)}, u32[]{:S(2)}) collective-permute-start(bf16[18,1,512]{2,1,0:T(2,128)(2,1)S(1)} %get-tuple-element.9), channel_id=1, source_target_pairs={{2,0},{4,2},{6,4},{3,1},{5,3},{7,5},{10,8},{12,10},{14,12},{11,9},... | collective-permute-start | bytes 55304 | tf_op jit(solution)/shard_map/ppermute | solution.py:23
  21.0 6.2 %collective-permute-start.2 = (bf16[18,1,512]{2,1,0:T(2,128)(2,1)S(1)}, bf16[18,1,512]{2,1,0:T(2,128)(2,1)S(1)}, u32[]{:S(2)}, u32[]{:S(2)}) collective-permute-start(bf16[18,1,512]{2,1,0:T(2,128)(2,1)S(1)} %get-tuple-element.8), channel_id=1, source_target_pairs={{0,2},{2,4},{4,6},{1,3},{3,5},{5,7},{8,10},{10,12},{12,14},{9,11},... | collective-permute-start | bytes 55304 | tf_op jit(solution)/shard_map/ppermute | solution.py:20
  27.2 8.0 %copy-start.8 = (f32[2,32,16,128]{3,2,1,0:T(8,128)S(1)}, f32[2,32,16,128]{3,2,1,0:T(8,128)}, u32[]{:S(2)}) copy-start(f32[2,32,16,128]{3,2,1,0:T(8,128)} %param.12) | copy-start | bytes 1572868
  55.5 15.3 %copy-start.4 = (f32[2,32,16,128]{3,1,2,0:T(8,128)}, f32[2,32,16,128]{3,1,2,0:T(8,128)S(1)}, u32[]{:S(2)}) copy-start(f32[2,32,16,128]{3,1,2,0:T(8,128)S(1)} %fusion.9) | copy-start | bytes 1572868
  56.1 9.2 %collective-permute-start.5 = (f32[129,3,128]{2,0,1:T(8,128)S(1)}, f32[129,3,128]{2,0,1:T(8,128)S(1)}, u32[]{:S(2)}, u32[]{:S(2)}) collective-permute-start(f32[129,3,128]{2,0,1:T(8,128)S(1)} %get-tuple-element.15), channel_id=1, source_target_pairs={{8,0},{16,8},{24,16},{0,24},{9,1},{17,9},{25,17},{1,25},{10,2},{18... | collective-permute-start | bytes 594440 | tf_op jit(solution)/shard_map/ppermute | solution.py:23
  59.7 10.4 %collective-permute-start.4 = (f32[129,3,128]{2,0,1:T(8,128)S(1)}, f32[129,3,128]{2,0,1:T(8,128)S(1)}, u32[]{:S(2)}, u32[]{:S(2)}) collective-permute-start(f32[129,3,128]{2,0,1:T(8,128)S(1)} %get-tuple-element.14), channel_id=1, source_target_pairs={{0,8},{8,16},{16,24},{24,0},{1,9},{9,17},{17,25},{25,1},{2,10},{10... | collective-permute-start | bytes 594440 | tf_op jit(solution)/shard_map/ppermute | solution.py:20
  70.1 0.7 copy-start.6
  75.2 16.1 %collective-permute-start.7 = (f32[129,22,3]{0,1,2:T(8,128)S(1)}, f32[129,22,3]{0,1,2:T(8,128)S(1)}, u32[]{:S(2)}, u32[]{:S(2)}) collective-permute-start(f32[129,22,3]{0,1,2:T(8,128)S(1)} %copy.19), channel_id=1, source_target_pairs={{2,0},{4,2},{6,4},{3,1},{5,3},{7,5},{10,8},{12,10},{14,12},{11,9},... | collective-permute-start | bytes 102176 | tf_op jit(solution)/shard_map/ppermute | solution.py:23
  79.5 13.5 %collective-permute-start.6 = (f32[129,22,3]{0,1,2:T(8,128)}, f32[129,22,3]{0,1,2:T(8,128)}, u32[]{:S(2)}, u32[]{:S(2)}) collective-permute-start(f32[129,22,3]{0,1,2:T(8,128)} %copy.18), channel_id=1, source_target_pairs={{0,2},{2,4},{4,6},{1,3},{3,5},{5,7},{8,10},{10,12},{12,14},{9,11},... | collective-permute-start | bytes 102176 | tf_op jit(solution)/shard_map/ppermute | solution.py:20
  95.6 1.5 %copy-start.1 = (f32[129,22,3]{2,0,1:T(8,128)S(1)}, f32[129,22,3]{2,0,1:T(8,128)}, u32[]{:S(2)}) copy-start(f32[129,22,3]{2,0,1:T(8,128)} %copy.21) | copy-start | bytes 102172
  95.6 2.0 %copy-start.2 = (f32[129,22,3]{2,0,1:T(8,128)S(1)}, f32[129,22,3]{2,0,1:T(8,128)}, u32[]{:S(2)}) copy-start(f32[129,22,3]{2,0,1:T(8,128)} %copy.20) | copy-start | bytes 102172
  95.6 2.0 %copy-start.7 = (f32[129,3,128]{2,0,1:T(8,128)S(1)}, f32[129,3,128]{2,0,1:T(8,128)}, u32[]{:S(2)}) copy-start(f32[129,3,128]{2,0,1:T(8,128)} %copy-done.6) | copy-start | bytes 594436
  97.5 1.3 %copy-start.9 = (f32[32]{0:T(128)S(1)}, f32[32]{0:T(128)}, u32[]{:S(2)}) copy-start(f32[32]{0:T(128)} %param.13) | copy-start | bytes 388
  102.7 1.4 %copy-start.5 = (f32[2,32,16,128]{3,1,2,0:T(8,128)S(1)}, f32[2,32,16,128]{3,1,2,0:T(8,128)}, u32[]{:S(2)}) copy-start(f32[2,32,16,128]{3,1,2,0:T(8,128)} %copy-done.4) | copy-start | bytes 1572868
Sparse Core Ops, SparseCore 0:
  35.1 16.7 all-gather.1
where the time goes:
time: 114 us; the launch traced here: 113 us
  waiting for transfers between devices  32.6 us (29%)
  starting transfers between devices  21.1 us (19%)
  local copies, waits for them, and re-layouts  18.2 us (16%)
  other arithmetic  16.6 us (15%)
  between operations  14.3 us (13%)
  matrix products  10.3 us (9%)
    all_gather x1, waiting for transfers between devices, local(): block_piece = lax.all_gather(advected, 'comp', axis=2, tiled=True)  16.5 us
    ppermute x4, starting transfers between devices, padded_2(): lax.ppermute(lax.slice_in_dim(block, block.shape[dim] - width, None, axis...  12.8 us
    ppermute x4, waiting for transfers between devices, padded_2(): lax.ppermute(lax.slice_in_dim(block, block.shape[dim] - width, None, axis...  10.6 us
    ppermute x4, starting transfers between devices, padded_2(): lax.ppermute(lax.slice_in_dim(block, 0, width, axis=dim), axis, backward)  8.32 us
    convert_element_type x1, other arithmetic, local(): advected = (upwind(centre, west_cell, east_cell, south_cell, north_cell,...  7.72 us
    dot_general x1, matrix products, local(): gain_sum = jnp.dot(flat_rows, w_cols, preferred_element_type=jnp.float32)  6.66 us
    mul x6, other arithmetic, substep(): return (u_next * sea_cells, v_next * sea_cells)  6.19 us
    ppermute x4, waiting for transfers between devices, padded_2(): lax.ppermute(lax.slice_in_dim(block, 0, width, axis=dim), axis, backward)  5.49 us
  transfers between devices with their start and end apart: 9, of which 5 were waited for; matrix products, arithmetic and copies ran while one was open for 12% of the time, Pallas kernels for 0%

commit v1 on v0

--- a/solution.py
+++ b/solution.py
@@ -96,13 +96,24 @@
     core_index = lax.axis_index("comp")
     w_cols = lax.dynamic_slice_in_dim(interaction, core_index * bins_own, bins_own, 1)
     proj_own = lax.dynamic_slice_in_dim(stokes_proj, core_index * lev_own, lev_own, 2)
-    block_piece = lax.all_gather(advected, "comp", axis=2, tiled=True)
-    count = block_piece.shape[2]
-    flat_rows = block_piece.reshape(-1, count)
-    gain_sum = jnp.dot(flat_rows, w_cols, preferred_element_type=jnp.float32)
-    stokes_sum = jnp.einsum(
-        "xyk,ckl->clxy", block_piece, proj_own, preferred_element_type=jnp.float32
-    )
+    cores = lax.axis_size("comp")
+    gain_sum = 0.0
+    stokes_sum = 0.0
+    block = advected
+    for hop in range(cores):
+        owner = lax.rem(core_index + cores - hop, cores) * bins_own
+        rows = lax.dynamic_slice_in_dim(w_cols, owner, bins_own, 0)
+        proj_rows = lax.dynamic_slice_in_dim(proj_own, owner, bins_own, 1)
+        following = block
+        if hop + 1 < cores:
+            following = lax.ppermute(block, "comp", [(i, (i + 1) % cores) for i in range(cores)])
+        gain_sum = gain_sum + jnp.dot(
+            block.reshape(-1, bins_own), rows, preferred_element_type=jnp.float32
+        )
+        stokes_sum = stokes_sum + jnp.einsum(
+            "xyk,ckl->clxy", block, proj_rows, preferred_element_type=jnp.float32
+        )
+        block = following
     wave_out = (
         (advected.astype(jnp.float32) + gain_sum.reshape(cells_x, cells_y, bins_own))
         * sea_cells[:, :, None]

time: 114 us -> 87.2 us (0.76)
  the two profiles are of different devices: /device:TPU:0 before, /device:TPU:5 now
where the time goes in v1:
time: 87.2 us; the launch traced here: 85.6 us
  other arithmetic  21.4 us (25%)
  starting transfers between devices  20.8 us (24%)
  local copies, waits for them, and re-layouts  17.7 us (20%)
  matrix products  12.8 us (15%)
  waiting for transfers between devices  12 us (14%)
  between operations  0.91 us (1%)
    ppermute x4, starting transfers between devices, padded_2(): lax.ppermute(lax.slice_in_dim(block, 0, width, axis=dim), axis, backward)  10.3 us
    dot_general x2, matrix products, local(): jnp.dot(block.reshape(-1, bins_own), rows, preferred_element_type=jnp.flo...  8.01 us
    ppermute x4, waiting for transfers between devices, padded_2(): lax.ppermute(lax.slice_in_dim(block, block.shape[dim] - width, None, axis...  7.74 us
    convert_element_type x1, other arithmetic, local(): advected = (upwind(centre, west_cell, east_cell, south_cell, north_cell,...  7.72 us
    ppermute x4, starting transfers between devices, padded_2(): lax.ppermute(lax.slice_in_dim(block, block.shape[dim] - width, None, axis...  7.1 us
    mul x6, other arithmetic, substep(): return (u_next * sea_cells, v_next * sea_cells)  6.19 us
    slice x3, local copies, waits for them, and re-layouts, padded_2(): lax.slice_in_dim(block, block.shape[dim] - width, None, axis=dim)  5.11 us
    dot_general x2, matrix products, local(): jnp.einsum('xyk,ckl->clxy', block, proj_rows, preferred_element_type=jnp....  4.81 us
  transfers between devices with their start and end apart: 9, of which 5 were waited for; matrix products, arithmetic and copies ran while one was open for 23% of the time, Pallas kernels for 0%

profile of v1, /device:TPU:5, one launch (start us, length us, event | category | flops | bytes accessed | tf_op | source)
XLA Modules:
  0.0 85.6 jit_solution(12074219779254844086)
XLA Ops:
  0.6 1.1 %fusion.86 = (bf16[1,128,512]{2,1,0:T(8,128)(2,1)S(1)}, bf16[1,128,512]{2,1,0:T(8,128)(2,1)S(1)}) fusion(bf16[16,128,512]{2,1,0:T(8,128)(2,1)} %param.7), kind=kLoop, calls=%fused_computation.127 | loop fusion | bytes 524288 | tf_op jit(solution)/shard_map/slice | solution.py:23
  1.8 1.3 %collective-permute-start = (bf16[1,128,512]{2,1,0:T(8,128)(2,1)S(1)}, bf16[1,128,512]{2,1,0:T(8,128)(2,1)S(1)}, u32[]{:S(2)}, u32[]{:S(2)}) collective-permute-start(bf16[1,128,512]{2,1,0:T(8,128)(2,1)S(1)} %get-tuple-element.11), channel_id=1, source_target_pairs={{0,8},{8,16},{16,24},{24,0},{1,9},{9,17},{17,25},{25,1},{2,10},{10... | collective-permute-start | bytes 393224 | tf_op jit(solution)/shard_map/ppermute | solution.py:20
  3.1 2.1 %collective-permute-start.1 = (bf16[1,128,512]{2,1,0:T(8,128)(2,1)S(1)}, bf16[1,128,512]{2,1,0:T(8,128)(2,1)S(1)}, u32[]{:S(2)}, u32[]{:S(2)}) collective-permute-start(bf16[1,128,512]{2,1,0:T(8,128)(2,1)S(1)} %get-tuple-element.10), channel_id=1, source_target_pairs={{8,0},{16,8},{24,16},{0,24},{9,1},{17,9},{25,17},{1,25},{10,2},{18... | collective-permute-start | bytes 393224 | tf_op jit(solution)/shard_map/ppermute | solution.py:23
  5.2 2.9 %collective-permute-done = bf16[1,128,512]{2,1,0:T(8,128)(2,1)S(1)} collective-permute-done((bf16[1,128,512]{2,1,0:T(8,128)(2,1)S(1)}, bf16[1,128,512]{2,1,0:T(8,128)(2,1)S(1)}, u32[]{:S(2)}, u32[]{:S(2)}) %collective-permute-start) | collective-permute-done | bytes 131104 | tf_op jit(solution)/shard_map/ppermute | solution.py:20
  8.2 1.9 %constant_dynamic-update-slice_fusion.1 = bf16[18,128,512]{2,1,0:T(8,128)(2,1)S(1)} fusion(bf16[18,128,512]{2,1,0:T(8,128)(2,1)S(1)} %constant_dynamic-update-slice_fusion.2, bf16[16,128,512]{2,1,0:T(8,128)(2,1)} %param.7), kind=kLoop, calls=%fused_computation.116 | loop fusion | bytes 4194304
  10.8 3.1 %collective-permute-start.3 = (bf16[18,1,512]{2,1,0:T(2,128)(2,1)S(1)}, bf16[18,1,512]{2,1,0:T(2,128)(2,1)S(1)}, u32[]{:S(2)}, u32[]{:S(2)}) collective-permute-start(bf16[18,1,512]{2,1,0:T(2,128)(2,1)S(1)} %get-tuple-element.9), channel_id=1, source_target_pairs={{2,0},{4,2},{6,4},{3,1},{5,3},{7,5},{10,8},{12,10},{14,12},{11,9},... | collective-permute-start | bytes 55304 | tf_op jit(solution)/shard_map/ppermute | solution.py:23
  13.9 2.2 %collective-permute-start.2 = (bf16[18,1,512]{2,1,0:T(2,128)(2,1)S(1)}, bf16[18,1,512]{2,1,0:T(2,128)(2,1)S(1)}, u32[]{:S(2)}, u32[]{:S(2)}) collective-permute-start(bf16[18,1,512]{2,1,0:T(2,128)(2,1)S(1)} %get-tuple-element.8), channel_id=1, source_target_pairs={{0,2},{2,4},{4,6},{1,3},{3,5},{5,7},{8,10},{10,12},{12,14},{9,11},... | collective-permute-start | bytes 55304 | tf_op jit(solution)/shard_map/ppermute | solution.py:20
  16.2 3.3 %collective-permute-done.2 = bf16[18,1,512]{2,1,0:T(2,128)(2,1)S(1)} collective-permute-done((bf16[18,1,512]{2,1,0:T(2,128)(2,1)S(1)}, bf16[18,1,512]{2,1,0:T(2,128)(2,1)S(1)}, u32[]{:S(2)}, u32[]{:S(2)}) %collective-permute-start.2) | collective-permute-done | bytes 18464 | tf_op jit(solution)/shard_map/ppermute | solution.py:20
  19.5 7.7 %fusion.5 = bf16[16,128,512]{2,1,0:T(8,128)(2,1)} fusion(bf16[16,128,512]{2,1,0:T(8,128)(2,1)S(1)} %copy-done.3, bf16[18,1,512]{2,1,0:T(2,128)(2,1)S(1)} %collective-permute-done.3, bf16[18,128,512]{2,1,0:T(8,128)(2,1)S(1)} %constant_dynamic-update-slice_fusion, bf16[18,1,512]{2,1,0:T(2,128)(2,1)S(1)} %collective-permute-done.2, ...), kind=kLoop, calls=%fused_computation.10 | loop fusion | flops 32505856 | bytes 6868992 | tf_op jit(solution)/shard_map/convert_element_type | solution.py:93
  27.2 3.4 %collective-permute-start.4 = (bf16[16,128,512]{2,1,0:T(8,128)(2,1)}, bf16[16,128,512]{2,1,0:T(8,128)(2,1)}, u32[]{:S(2)}, u32[]{:S(2)}) collective-permute-start(bf16[16,128,512]{2,1,0:T(8,128)(2,1)} %fusion.5), channel_id=1, source_target_pairs={{0,1},{1,0},{2,3},{3,2},{4,5},{5,4},{6,7},{7,6},{8,9},{9,8},{10,11... | collective-permute-start | bytes 6291464 | tf_op jit(solution)/shard_map/ppermute | solution.py:109
  31.1 3.7 %collective-permute-done.4 = bf16[16,128,512]{2,1,0:T(8,128)(2,1)} collective-permute-done((bf16[16,128,512]{2,1,0:T(8,128)(2,1)}, bf16[16,128,512]{2,1,0:T(8,128)(2,1)}, u32[]{:S(2)}, u32[]{:S(2)}) %collective-permute-start.4) | collective-permute-done | bytes 2097184 | tf_op jit(solution)/shard_map/ppermute | solution.py:109
  34.7 2.4 %fusion.9 = f32[2,32,16,128]{3,1,2,0:T(8,128)S(1)} fusion(bf16[16,128,512]{2,1,0:T(8,128)(2,1)} %collective-permute-done.4, bf16[2,1024,64]{1,2,0:T(8,128)(2,1)} %param.11, s32[]{:T(128)S(6)} %select_n.27, s32[]{:T(128)S(6)} %select_n.29), kind=kOutput, calls=%fused_computation.20 | convolution fusion | flops 134217728 | bytes 2686984 | tf_op jit(solution)/shard_map/xyk,ckl->clxy/dot_general | solution.py:113
  37.1 2.4 %fusion.13 = f32[2,32,16,128]{3,1,2,0:T(8,128)S(1)} fusion(f32[2,32,16,128]{3,1,2,0:T(8,128)S(1)} %fusion.9, bf16[16,128,512]{2,1,0:T(8,128)(2,1)} %fusion.5, bf16[2,1024,64]{1,2,0:T(8,128)(2,1)} %param.11, s32[]{:T(128)S(6)} %select_n.23, s32[]{:T(128)S(6)} %select_n.29), kind=kOutput, calls=%fused_computation.25 | convolution fusion | flops 134348800 | bytes 3211272 | tf_op jit(solution)/shard_map/xyk,ckl->clxy/dot_general | solution.py:113
  40.1 3.2 %collective-permute-start.6 = (f32[129,3,128]{2,0,1:T(8,128)S(1)}, f32[129,3,128]{2,0,1:T(8,128)S(1)}, u32[]{:S(2)}, u32[]{:S(2)}) collective-permute-start(f32[129,3,128]{2,0,1:T(8,128)S(1)} %get-tuple-element.15), channel_id=1, source_target_pairs={{8,0},{16,8},{24,16},{0,24},{9,1},{17,9},{25,17},{1,25},{10,2},{18... | collective-permute-start | bytes 594440 | tf_op jit(solution)/shard_map/ppermute | solution.py:23
  43.3 3.0 %fusion.52 = f32[2048,512]{1,0:T(8,128)S(1)} fusion(bf16[2048,512]{1,0:T(8,128)(2,1)} %bitcast.5, bf16[1024,1024]{1,0:T(8,128)(2,1)S(1)} %copy-done, s32[]{:T(128)S(6)} %select_n.27, s32[]{:T(128)S(6)} %select_n.25), kind=kOutput, calls=%fused_computation.75 | convolution fusion | flops 1073741824 | bytes 6815752 | tf_op jit(solution)/shard_map/dot_general | solution.py:110
  46.3 5.0 %fusion.56 = f32[2048,512]{1,0:T(8,128)} fusion(f32[2048,512]{1,0:T(8,128)S(1)} %fusion.52, bf16[2048,512]{1,0:T(8,128)(2,1)} %bitcast.4, bf16[1024,1024]{1,0:T(8,128)(2,1)S(1)} %copy-done, s32[]{:T(128)S(6)} %select_n.23, s32[]{:T(128)S(6)} %select_n.25), kind=kOutput, calls=%fused_computation.79 | convolution fusion | flops 1074790400 | bytes 11010056 | tf_op jit(solution)/shard_map/dot_general | solution.py:110
  51.4 1.5 %collective-permute-done.5 = f32[129,3,128]{2,0,1:T(8,128)S(1)} collective-permute-done((f32[129,3,128]{2,0,1:T(8,128)S(1)}, f32[129,3,128]{2,0,1:T(8,128)S(1)}, u32[]{:S(2)}, u32[]{:S(2)}) %collective-permute-start.5) | collective-permute-done | bytes 198176 | tf_op jit(solution)/shard_map/ppermute | solution.py:20
  53.0 2.1 %fusion.87 = (f32[129,22,3]{2,0,1:T(8,128)}, f32[129,22,3]{2,0,1:T(8,128)}) fusion(f32[129,22,128]{2,0,1:T(8,128)S(1)} %pad_maximum_fusion.5), kind=kLoop, calls=%fused_computation.128 | loop fusion | bytes 136224 | tf_op jit(solution)/shard_map/slice | solution.py:21
  55.1 2.3 %copy.19 = f32[129,22,3]{0,1,2:T(8,128)S(1)} copy(f32[129,22,3]{2,0,1:T(8,128)} %get-tuple-element.13) | data formatting | bytes 68112 | tf_op jit(solution)/shard_map/slice | solution.py:23
  57.4 1.9 %collective-permute-start.8 = (f32[129,22,3]{0,1,2:T(8,128)S(1)}, f32[129,22,3]{0,1,2:T(8,128)S(1)}, u32[]{:S(2)}, u32[]{:S(2)}) collective-permute-start(f32[129,22,3]{0,1,2:T(8,128)S(1)} %copy.19), channel_id=1, source_target_pairs={{2,0},{4,2},{6,4},{3,1},{5,3},{7,5},{10,8},{12,10},{14,12},{11,9},... | collective-permute-start | bytes 102176 | tf_op jit(solution)/shard_map/ppermute | solution.py:23
  59.3 2.9 %copy.18 = f32[129,22,3]{0,1,2:T(8,128)} copy(f32[129,22,3]{2,0,1:T(8,128)} %get-tuple-element.12) | data formatting | bytes 68112 | tf_op jit(solution)/shard_map/slice | solution.py:21
  62.3 3.5 %collective-permute-start.7 = (f32[129,22,3]{0,1,2:T(8,128)}, f32[129,22,3]{0,1,2:T(8,128)}, u32[]{:S(2)}, u32[]{:S(2)}) collective-permute-start(f32[129,22,3]{0,1,2:T(8,128)} %copy.18), channel_id=1, source_target_pairs={{0,2},{2,4},{4,6},{1,3},{3,5},{5,7},{8,10},{10,12},{12,14},{9,11},... | collective-permute-start | bytes 102176 | tf_op jit(solution)/shard_map/ppermute | solution.py:20
  65.8 4.7 %multiply_convert_fusion = bf16[16,128,512]{2,1,0:T(8,128)(2,1)} fusion(f32[16,128,512]{2,1,0:T(8,128)} %bitcast.58, bf16[16,128,512]{2,1,0:T(8,128)(2,1)} %fusion.5, f32[16,128]{1,0:T(8,128)S(1)} %convert_element_type.42), kind=kLoop, calls=%fused_computation.14 | loop fusion | flops 4194304 | bytes 8396800 | tf_op jit(solution)/shard_map/convert_element_type | solution.py:120
  70.5 1.7 %copy.21 = f32[129,22,3]{2,0,1:T(8,128)} copy(f32[129,22,3]{0,1,2:T(8,128)S(1)} %collective-permute-done.8) | data formatting | bytes 68112 | tf_op jit(solution)/shard_map/ppermute | solution.py:23
  72.2 2.6 %copy.20 = f32[129,22,3]{2,0,1:T(8,128)} copy(f32[129,22,3]{0,1,2:T(8,128)} %collective-permute-done.7) | data formatting | bytes 68112 | tf_op jit(solution)/shard_map/ppermute | solution.py:20
  74.8 1.2 %pad_maximum_fusion.10 = f32[1,22,134]{2,0,1:T(1,128)S(1)} fusion(f32[129,22,3]{2,0,1:T(8,128)} %copy.21, f32[129,22,3]{2,0,1:T(8,128)} %copy.20, f32[129,3,128]{2,0,1:T(8,128)S(1)} %collective-permute-done.6, f32[129,3,128]{2,0,1:T(8,128)} %copy-done.6, f32[1,16,128]{2,0,1:T(1,128)S(1)} %bitcast.67, f32[64,16,128]{2,0,1:T(8,128)S(1)} %copy.17, ...), kind=kLoop, calls=%fused_computation.114 | loop fusion | flops 17688 | bytes 1532960 | tf_op jit(solution)/shard_map/slice | solution.py:133
  76.8 1.3 %pad_maximum_fusion = f32[129,22,134]{2,0,1:T(8,128)S(1)} fusion(f32[129,22,3]{2,0,1:T(8,128)S(1)} %copy-done.1, f32[129,3,128]{2,0,1:T(8,128)S(1)} %collective-permute-done.6, f32[1,16,128]{2,0,1:T(1,128)S(1)} %bitcast.68, f32[64,16,128]{2,0,1:T(8,128)S(1)} %copy.17, f32[64,16,128]{2,0,1:T(8,128)S(1)} %bitcast.62, f32[129,3,128]{2,0,1:T(8,128)S(1)} %copy-done.7, ...), kind=kLoop, calls=%fused_computation.15 | loop fusion | flops 2281752 | bytes 3042336 | tf_op jit(solution)/shard_map/concatenate | solution.py:24
  78.0 1.3 %fusion.21 = f32[32,20,132]{2,0,1:T(8,128)S(1)} fusion(f32[129,22,134]{2,0,1:T(8,128)S(1)} %pad_maximum_fusion, f32[20,132]{1,0:T(8,128)S(1)} %slice.302, f32[32]{0:T(128)S(1)} %copy-done.9, f32[132]{0:T(256)S(1)} %bitcast.74), kind=kLoop, calls=%fused_computation.32 | loop fusion | flops 1774080 | bytes 3390416 | tf_op jit(solution)/shard_map/mul | solution.py:68
  79.3 1.4 %fusion.31 = f32[32,20,132]{2,0,1:T(8,128)S(1)} fusion(f32[129,22,134]{2,0,1:T(8,128)S(1)} %pad_maximum_fusion, f32[20,132]{1,0:T(8,128)S(1)} %slice.302, f32[32]{0:T(128)S(1)} %copy-done.9, f32[132]{0:T(256)S(1)} %bitcast.75), kind=kLoop, calls=%fused_computation.45 | loop fusion | flops 1689600 | bytes 3390416 | tf_op jit(solution)/shard_map/mul | solution.py:68
  80.8 1.2 %fusion.39 = f32[32,18,130]{2,0,1:T(8,128)S(1)} fusion(f32[32,20,132]{2,0,1:T(8,128)S(1)} %fusion.21, f32[129,22,134]{2,0,1:T(8,128)S(1)} %pad_maximum_fusion, f32[32,20,132]{2,0,1:T(8,128)S(1)} %fusion.31, f32[18,130]{1,0:T(8,128)S(1)} %slice.316, f32[32]{0:T(128)S(1)} %copy-done.9, f32[130]{0:T(256)S(1)} %bitcast.72), kind=kLoop, calls=%fused_computation.56 | loop fusion | flops 1572480 | bytes 3005208 | tf_op jit(solution)/shard_map/mul | solution.py:68
  82.0 1.3 %fusion.49 = f32[32,18,130]{2,0,1:T(8,128)S(1)} fusion(f32[32,20,132]{2,0,1:T(8,128)S(1)} %fusion.31, f32[129,22,134]{2,0,1:T(8,128)S(1)} %pad_maximum_fusion, f32[32,20,132]{2,0,1:T(8,128)S(1)} %fusion.21, f32[18,130]{1,0:T(8,128)S(1)} %slice.316, f32[32]{0:T(128)S(1)} %copy-done.9, f32[130]{0:T(256)S(1)} %bitcast.73), kind=kLoop, calls=%fused_computation.69 | loop fusion | flops 1497600 | bytes 3005208 | tf_op jit(solution)/shard_map/mul | solution.py:68
  84.5 1.1 %copy.22 = f32[2,32,16,128]{3,2,1,0:T(8,128)} copy(f32[2,32,16,128]{3,1,0,2:T(8,128)S(1)} %bitcast.63) | data formatting | bytes 1048576
  (51 shorter events, 3.8 us)
Async XLA Ops:
  0.6 42.7 %copy-start = (bf16[1024,1024]{1,0:T(8,128)(2,1)S(1)}, bf16[1024,1024]{1,0:T(8,128)(2,1)}, u32[]{:S(2)}) copy-start(bf16[1024,1024]{1,0:T(8,128)(2,1)} %param.10) | copy-start | bytes 6291460
  1.8 6.4 %collective-permute-start = (bf16[1,128,512]{2,1,0:T(8,128)(2,1)S(1)}, bf16[1,128,512]{2,1,0:T(8,128)(2,1)S(1)}, u32[]{:S(2)}, u32[]{:S(2)}) collective-permute-start(bf16[1,128,512]{2,1,0:T(8,128)(2,1)S(1)} %get-tuple-element.11), channel_id=1, source_target_pairs={{0,8},{8,16},{16,24},{24,0},{1,9},{9,17},{17,25},{25,1},{2,10},{10... | collective-permute-start | bytes 393224 | tf_op jit(solution)/shard_map/ppermute | solution.py:20
  3.1 7.6 %collective-permute-start.1 = (bf16[1,128,512]{2,1,0:T(8,128)(2,1)S(1)}, bf16[1,128,512]{2,1,0:T(8,128)(2,1)S(1)}, u32[]{:S(2)}, u32[]{:S(2)}) collective-permute-start(bf16[1,128,512]{2,1,0:T(8,128)(2,1)S(1)} %get-tuple-element.10), channel_id=1, source_target_pairs={{8,0},{16,8},{24,16},{0,24},{9,1},{17,9},{25,17},{1,25},{10,2},{18... | collective-permute-start | bytes 393224 | tf_op jit(solution)/shard_map/ppermute | solution.py:23
  8.1 8.0 %copy-start.11 = (f32[2,512]{1,0:T(2,128)S(1)}, f32[2,512]{1,0:T(2,128)}, u32[]{:S(2)}) copy-start(f32[2,512]{1,0:T(2,128)} %param.9) | copy-start | bytes 12292
  8.2 8.0 %copy-start.10 = (s32[16,128]{1,0:T(8,128)S(1)}, s32[16,128]{1,0:T(8,128)}, u32[]{:S(2)}) copy-start(s32[16,128]{1,0:T(8,128)} %param.8) | copy-start | bytes 24580
  8.2 11.3 %copy-start.3 = (bf16[16,128,512]{2,1,0:T(8,128)(2,1)S(1)}, bf16[16,128,512]{2,1,0:T(8,128)(2,1)}, u32[]{:S(2)}) copy-start(bf16[16,128,512]{2,1,0:T(8,128)(2,1)} %param.7) | copy-start | bytes 6291460
  10.8 5.3 %collective-permute-start.3 = (bf16[18,1,512]{2,1,0:T(2,128)(2,1)S(1)}, bf16[18,1,512]{2,1,0:T(2,128)(2,1)S(1)}, u32[]{:S(2)}, u32[]{:S(2)}) collective-permute-start(bf16[18,1,512]{2,1,0:T(2,128)(2,1)S(1)} %get-tuple-element.9), channel_id=1, source_target_pairs={{2,0},{4,2},{6,4},{3,1},{5,3},{7,5},{10,8},{12,10},{14,12},{11,9},... | collective-permute-start | bytes 55304 | tf_op jit(solution)/shard_map/ppermute | solution.py:23
  13.9 5.6 %collective-permute-start.2 = (bf16[18,1,512]{2,1,0:T(2,128)(2,1)S(1)}, bf16[18,1,512]{2,1,0:T(2,128)(2,1)S(1)}, u32[]{:S(2)}, u32[]{:S(2)}) collective-permute-start(bf16[18,1,512]{2,1,0:T(2,128)(2,1)S(1)} %get-tuple-element.8), channel_id=1, source_target_pairs={{0,2},{2,4},{4,6},{1,3},{3,5},{5,7},{8,10},{10,12},{12,14},{9,11},... | collective-permute-start | bytes 55304 | tf_op jit(solution)/shard_map/ppermute | solution.py:20
  19.5 11.3 %copy-start.8 = (f32[2,32,16,128]{3,2,1,0:T(8,128)S(1)}, f32[2,32,16,128]{3,2,1,0:T(8,128)}, u32[]{:S(2)}) copy-start(f32[2,32,16,128]{3,2,1,0:T(8,128)} %param.12) | copy-start | bytes 1572868
  27.2 7.5 %collective-permute-start.4 = (bf16[16,128,512]{2,1,0:T(8,128)(2,1)}, bf16[16,128,512]{2,1,0:T(8,128)(2,1)}, u32[]{:S(2)}, u32[]{:S(2)}) collective-permute-start(bf16[16,128,512]{2,1,0:T(8,128)(2,1)} %fusion.5), channel_id=1, source_target_pairs={{0,1},{1,0},{2,3},{3,2},{4,5},{5,4},{6,7},{7,6},{8,9},{9,8},{10,11... | collective-permute-start | bytes 6291464 | tf_op jit(solution)/shard_map/ppermute | solution.py:109
  39.5 3.8 %copy-start.4 = (f32[2,32,16,128]{3,1,2,0:T(8,128)}, f32[2,32,16,128]{3,1,2,0:T(8,128)S(1)}, u32[]{:S(2)}) copy-start(f32[2,32,16,128]{3,1,2,0:T(8,128)S(1)} %fusion.13) | copy-start | bytes 1572868
  40.1 11.3 %collective-permute-start.6 = (f32[129,3,128]{2,0,1:T(8,128)S(1)}, f32[129,3,128]{2,0,1:T(8,128)S(1)}, u32[]{:S(2)}, u32[]{:S(2)}) collective-permute-start(f32[129,3,128]{2,0,1:T(8,128)S(1)} %get-tuple-element.15), channel_id=1, source_target_pairs={{8,0},{16,8},{24,16},{0,24},{9,1},{17,9},{25,17},{1,25},{10,2},{18... | collective-permute-start | bytes 594440 | tf_op jit(solution)/shard_map/ppermute | solution.py:23
  43.3 9.5 %collective-permute-start.5 = (f32[129,3,128]{2,0,1:T(8,128)S(1)}, f32[129,3,128]{2,0,1:T(8,128)S(1)}, u32[]{:S(2)}, u32[]{:S(2)}) collective-permute-start(f32[129,3,128]{2,0,1:T(8,128)S(1)} %get-tuple-element.14), channel_id=1, source_target_pairs={{0,8},{8,16},{16,24},{24,0},{1,9},{9,17},{17,25},{25,1},{2,10},{10... | collective-permute-start | bytes 594440 | tf_op jit(solution)/shard_map/ppermute | solution.py:20
  52.9 2.2 %copy-start.6 = (f32[129,3,128]{2,0,1:T(8,128)}, f32[129,3,128]{2,0,1:T(8,128)S(1)}, u32[]{:S(2)}) copy-start(f32[129,3,128]{2,0,1:T(8,128)S(1)} %collective-permute-done.5) | copy-start | bytes 594436
  57.4 13.1 %collective-permute-start.8 = (f32[129,22,3]{0,1,2:T(8,128)S(1)}, f32[129,22,3]{0,1,2:T(8,128)S(1)}, u32[]{:S(2)}, u32[]{:S(2)}) collective-permute-start(f32[129,22,3]{0,1,2:T(8,128)S(1)} %copy.19), channel_id=1, source_target_pairs={{2,0},{4,2},{6,4},{3,1},{5,3},{7,5},{10,8},{12,10},{14,12},{11,9},... | collective-permute-start | bytes 102176 | tf_op jit(solution)/shard_map/ppermute | solution.py:23
  62.3 10.0 %collective-permute-start.7 = (f32[129,22,3]{0,1,2:T(8,128)}, f32[129,22,3]{0,1,2:T(8,128)}, u32[]{:S(2)}, u32[]{:S(2)}) collective-permute-start(f32[129,22,3]{0,1,2:T(8,128)} %copy.18), channel_id=1, source_target_pairs={{0,2},{2,4},{4,6},{1,3},{3,5},{5,7},{8,10},{10,12},{12,14},{9,11},... | collective-permute-start | bytes 102176 | tf_op jit(solution)/shard_map/ppermute | solution.py:20
  74.8 1.5 %copy-start.1 = (f32[129,22,3]{2,0,1:T(8,128)S(1)}, f32[129,22,3]{2,0,1:T(8,128)}, u32[]{:S(2)}) copy-start(f32[129,22,3]{2,0,1:T(8,128)} %copy.21) | copy-start | bytes 102172
  74.8 2.0 %copy-start.2 = (f32[129,22,3]{2,0,1:T(8,128)S(1)}, f32[129,22,3]{2,0,1:T(8,128)}, u32[]{:S(2)}) copy-start(f32[129,22,3]{2,0,1:T(8,128)} %copy.20) | copy-start | bytes 102172
  74.8 2.0 %copy-start.7 = (f32[129,3,128]{2,0,1:T(8,128)S(1)}, f32[129,3,128]{2,0,1:T(8,128)}, u32[]{:S(2)}) copy-start(f32[129,3,128]{2,0,1:T(8,128)} %copy-done.6) | copy-start | bytes 594436
  76.8 1.3 %copy-start.9 = (f32[32]{0:T(128)S(1)}, f32[32]{0:T(128)}, u32[]{:S(2)}) copy-start(f32[32]{0:T(128)} %param.13) | copy-start | bytes 388
  82.0 1.4 %copy-start.5 = (f32[2,32,16,128]{3,1,2,0:T(8,128)S(1)}, f32[2,32,16,128]{3,1,2,0:T(8,128)}, u32[]{:S(2)}) copy-start(f32[2,32,16,128]{3,1,2,0:T(8,128)} %copy-done.4) | copy-start | bytes 1572868

commit v2 on v0

v2 whole, which is shorter than its diff:
```python
import functools

import jax
import jax.numpy as jnp
from jax import lax
from jax.experimental import pallas as pl
from jax.experimental.pallas import tpu as pltpu
from jax.sharding import PartitionSpec as P

SUBSTEPS = 3

time_step = 0.5
viscosity = 0.4

F32 = jnp.float32
BF16 = jnp.bfloat16
MIB = 1 << 20
EDGE = 3
PARTS = 5


def shifts(axis, periodic):
    count = lax.axis_size(axis)
    forward = [(i, i + 1) for i in range(count - 1)]
    if periodic:
        forward.append((count - 1, 0))
    return forward, [(target, source) for source, target in forward]


def diagonal(step_x, step_y):
    size_x, size_y = lax.axis_size("gx"), lax.axis_size("gy")
    return [
        (x * size_y + y, (x + step_x) % size_x * size_y + y + step_y)
        for x in range(size_x)
        for y in range(size_y)
        if 0 <= y + step_y < size_y
    ]


def lane_of(rows, width):
    return lax.broadcasted_iota(jnp.int32, (rows, width), 1)


def between(lane, low, high):
    return (lane >= low) & (lane < high)


def project_kernel(
    f_own, f_oth, wt_own, wt_oth, cur,
    s_main, s_aux, msg_e, msg_w, msg_n, msg_s, msg_ne, msg_nw, msg_se, msg_sw,
    proj,
):
    cells_x, fields, width = cur.shape
    chans = s_main.shape[1]
    stride = width // (cells_x + 2)
    half = width // 2
    contract = (((1,), (1,)), ((), ()))
    for pair in range(cells_x // 2):
        cells = pl.ds(pair * 2 * width, 2 * width)
        both = lax.dot_general(wt_own[...], f_own[cells, :], contract, preferred_element_type=F32)
        both += lax.dot_general(wt_oth[...], f_oth[cells, :], contract, preferred_element_type=F32)
        proj[2 * pair] = both[:, :width]
        proj[2 * pair + 1] = both[:, width:]

    lane = lane_of(chans, width)
    lane_f = lane_of(fields, width)

    def part(x, which):
        return proj[x, which * chans : (which + 1) * chans, :]

    pack_n = pack_s = jnp.zeros((chans, width), F32)
    cur_n = cur_s = jnp.zeros((fields, width), F32)
    for x in range(-1, cells_x + 1):
        start = stride * (x + 1)
        main = jnp.zeros((chans, width), F32)
        aux = jnp.zeros((chans, width), F32)
        if 0 <= x < cells_x:
            south = pltpu.roll(part(x, 3), 1, 1)
            north = pltpu.roll(part(x, 4), width - 1, 1)
            main = part(x, 0) + jnp.where(lane > 0, south, 0.0) + jnp.where(lane < width - 1, north, 0.0)
            aux = jnp.where(lane == 0, south, jnp.where(lane == width - 1, north, 0.0))
            s_aux[x] = aux
        if x >= 1:
            main += part(x - 1, 1)
        if x <= cells_x - 2:
            main += part(x + 1, 2)
        s_main[x + 1] = main
        window = between(lane, start, start + 4)
        ring_n = pltpu.roll(jnp.where(lane == 0, aux, main), (3 + start) % width, 1)
        ring_s = pltpu.roll(jnp.where(lane == width - 1, aux, main), (1 + start) % width, 1)
        pack_n = jnp.where(window, ring_n, pack_n)
        pack_s = jnp.where(window, ring_s, pack_s)
        if 0 <= x < cells_x:
            row = cur[x]
            cur_n = jnp.where(
                between(lane_f, start, start + 3), pltpu.roll(row, (3 + start) % width, 1), cur_n
            )
            cur_s = jnp.where(
                between(lane_f, start + 1, start + 4), pltpu.roll(row, (1 + start) % width, 1), cur_s
            )
    for msg, pack, cur_pack in ((msg_n, pack_n, cur_n), (msg_s, pack_s, cur_s)):
        msg[:chans] = pack.astype(BF16)
        msg[chans:] = cur_pack.astype(BF16)
    corners = (
        (msg_ne, pack_n, cur_n, cells_x - 1, cells_x - 2),
        (msg_nw, pack_n, cur_n, 0, 1),
        (msg_se, pack_s, cur_s, cells_x - 1, cells_x - 2),
        (msg_sw, pack_s, cur_s, 0, 1),
    )
    for msg, pack, cur_pack, first, first_cur in corners:
        kept = jnp.where(lane < EDGE * stride, pltpu.roll(pack, (-stride * first) % width, 1), 0.0)
        cur_kept = jnp.where(
            between(lane_f, half, half + EDGE * stride),
            pltpu.roll(cur_pack, (half - stride * first_cur) % width, 1),
            0.0,
        )
        msg[:chans] = (kept + cur_kept[:chans]).astype(BF16)
        msg[chans:] = cur_kept[chans:].astype(BF16)
    sides = ((msg_e, cells_x - 1, cells_x - 1, cells_x - EDGE), (msg_w, 0, 0, 0))
    for msg, first, aux_row, first_cur in sides:
        for i in range(EDGE):
            msg[i * chans : (i + 1) * chans] = s_main[first + i].astype(BF16)
            base = (EDGE + 1) * chans + i * fields
            msg[base : base + fields] = cur[first_cur + i].astype(BF16)
        msg[EDGE * chans : (EDGE + 1) * chans] = s_aux[aux_row].astype(BF16)


def momentum_kernel(
    s_main, s_aux, cur, from_w, from_e, from_s, from_n, from_sw, from_se, from_nw, from_ne, drag, cor,
    out,
    flow_a, flow_b, stokes, result, sem,
):
    cells_x, fields, width = cur.shape
    chans = s_main.shape[1]
    levels = chans // 2
    stride = width // (cells_x + 2)
    half = width // 2
    lane = lane_of(chans, width)
    lane_f = lane_of(fields, width)

    def southern(tile, start):
        return pltpu.roll(tile, (-start - 3) % width, 1)

    def northern(tile, start):
        return pltpu.roll(tile, (-start - 1) % width, 1)

    cur_base = (EDGE + 1) * chans
    cur_s, cur_n = from_s[chans:].astype(F32), from_n[chans:].astype(F32)
    for x in range(-SUBSTEPS, cells_x + SUBSTEPS):
        if x < 0:
            at = x + SUBSTEPS
            main = from_w[cur_base + at * fields : cur_base + (at + 1) * fields].astype(F32)
            low = southern(from_sw[...].astype(F32), half + stride * at)
            high = northern(from_nw[...].astype(F32), half + stride * at)
        elif x < cells_x:
            main = cur[x]
            low = southern(cur_s, stride * (x + 1))
            high = northern(cur_n, stride * (x + 1))
        else:
            at = x - cells_x
            main = from_e[cur_base + at * fields : cur_base + (at + 1) * fields].astype(F32)
            low = southern(from_se[...].astype(F32), half + stride * at)
            high = northern(from_ne[...].astype(F32), half + stride * at)
        flow_a[x + SUBSTEPS, :, :width] = main
        flow_a[x + SUBSTEPS, :, width:] = jnp.where(
            lane_f >= width - 3, low, jnp.where(lane_f < 3, high, 0.0)
        )

    pack_s, pack_n = from_s[:chans].astype(F32), from_n[:chans].astype(F32)
    margin = SUBSTEPS - 1
    for x in range(-margin, cells_x + margin):
        main = aux = low = high = jnp.zeros((chans, width), F32)
        if -1 <= x <= cells_x:
            main += s_main[x + 1]
            low += southern(pack_s, stride * (x + 1))
            high += northern(pack_n, stride * (x + 1))
        if 0 <= x < cells_x:
            aux += s_aux[x]
        for message, message_s, message_n, first, spill in (
            (from_w, from_sw, from_nw, -2, -1),
            (from_e, from_se, from_ne, cells_x - 1, cells_x),
        ):
            at = x - first
            if 0 <= at < EDGE:
                main += message[at * chans : (at + 1) * chans].astype(F32)
                low += southern(message_s[:chans].astype(F32), stride * at)
                high += northern(message_n[:chans].astype(F32), stride * at)
            if x == spill:
                aux += message[EDGE * chans : (EDGE + 1) * chans].astype(F32)
        main += jnp.where(lane == 0, low, 0.0) + jnp.where(lane == width - 1, high, 0.0)
        aux += jnp.where(lane >= width - 3, low, jnp.where(lane < 3, high, 0.0))
        sea = flow_a[x + SUBSTEPS, chans : chans + 1, :]
        stokes[x + margin, :, :width] = main * sea[:, :width]
        stokes[x + margin, :, width:] = aux * sea[:, width:]

    half_cor = time_step * cor[...]
    keep = 1.0 - 4.0 * time_step * viscosity - time_step * drag[...]
    ring = 2 * width
    source, target = flow_a, flow_b
    for step in range(SUBSTEPS):
        margin = SUBSTEPS - 1 - step
        last = step == SUBSTEPS - 1
        for x in range(-margin, cells_x + margin):
            at = x + SUBSTEPS
            u, v = source[at, :levels], source[at, levels:chans]
            u_w, v_w = source[at - 1, :levels], source[at - 1, levels:chans]
            u_e, v_e = source[at + 1, :levels], source[at + 1, levels:chans]
            u_s, v_s = pltpu.roll(u, 1, 1), pltpu.roll(v, 1, 1)
            u_n, v_n = pltpu.roll(u, ring - 1, 1), pltpu.roll(v, ring - 1, 1)
            drift = stokes[x + SUBSTEPS - 1]
            spin = half_cor + 0.5 * time_step * ((v_e - v_w) - (u_n - u_s))
            sea = flow_a[at, chans : chans + 1, :]
            u_new = keep * u + spin * (v + drift[levels:])
            v_new = keep * v - spin * (u + drift[:levels])
            u_new = sea * (u_new + time_step * viscosity * ((u_e + u_w) + (u_n + u_s)))
            v_new = sea * (v_new + time_step * viscosity * ((v_e + v_w) + (v_n + v_s)))
            if last:
                result[x, :levels] = u_new[:, :width]
                result[x, levels:] = v_new[:, :width]
                for c in range(2):
                    pltpu.make_async_copy(
                        result.at[x, pl.ds(c * levels, levels), :], out.at[c, :, x, :], sem.at[c, x]
                    ).start()
            else:
                target[at, :levels] = u_new
                target[at, levels:chans] = v_new
        source, target = target, source
    for x in range(cells_x):
        for c in range(2):
            pltpu.make_async_copy(
                result.at[x, pl.ds(c * levels, levels), :], out.at[c, :, x, :], sem.at[c, x]
            ).wait()


def advect(centre, west, east, south, north, coef, sea, adv, row, col):
    width, bins = centre.shape
    chunk = 128
    at_y = lax.broadcasted_iota(jnp.int32, (width, chunk), 0)
    for j in range(bins // chunk):
        cols = slice(j * chunk, (j + 1) * chunk)
        mid = centre[:, cols].astype(F32)
        low = jnp.where(at_y == 0, south[:, cols].astype(F32), pltpu.roll(mid, 1, 0))
        high = jnp.where(at_y == width - 1, north[:, cols].astype(F32), pltpu.roll(mid, width - 1, 0))
        beside = jnp.where(coef[3:4, cols] > 0, west[:, cols].astype(F32), east[:, cols].astype(F32))
        along = jnp.where(coef[4:5, cols] > 0, low, high)
        value = coef[0:1, cols] * mid + coef[1:2, cols] * beside + coef[2:3, cols] * along
        adv[row : row + width, col + j * chunk : col + (j + 1) * chunk] = (value * sea).astype(BF16)


def sea_column(mask, x, width):
    return jnp.transpose(jnp.broadcast_to(mask[pl.ds(x, 1), :], (128, width)))


def finish(adv, inter_own, inter_oth, seas, out_slot):
    bins = inter_own.shape[1]
    width = seas[0].shape[0]
    gain = jnp.dot(adv[:, :bins], inter_own[...], preferred_element_type=F32)
    gain += jnp.dot(adv[:, bins:], inter_oth[...], preferred_element_type=F32)
    for i, sea in enumerate(seas):
        rows = slice(i * width, (i + 1) * width)
        for j in range(bins // 128):
            cols = slice(j * 128, (j + 1) * 128)
            total = adv[rows, cols].astype(F32) + gain[rows, cols]
            out_slot[i, :, cols] = (total * sea).astype(BF16)


def interior_kernel(
    f_own, f_oth, south_own, south_oth, north_own, north_oth, mask, coef_own, coef_oth, inter_own, inter_oth,
    out,
    adv, slots, out_sem,
):
    cells_x, width, bins = f_own.shape
    pairs = cells_x // 2 - 1

    def copy_out(pair):
        slot = lax.rem(pair, 2)
        return pltpu.make_async_copy(
            slots.at[slot], out.at[pl.ds(1 + 2 * pair, 2)], out_sem.at[slot]
        )

    def body(pair, carry):
        seas = []
        for i in range(2):
            x = 1 + 2 * pair + i
            sea = sea_column(mask, x, width)
            seas.append(sea)
            for f, south, north, coef, col in (
                (f_own, south_own, north_own, coef_own, 0),
                (f_oth, south_oth, north_oth, coef_oth, bins),
            ):
                advect(
                    f.at[x], f.at[x - 1], f.at[x + 1], south.at[x], north.at[x],
                    coef, sea, adv, i * width, col,
                )

        @pl.when(pair >= 2)
        def _():
            copy_out(pair - 2).wait()

        finish(adv, inter_own, inter_oth, seas, slots.at[lax.rem(pair, 2)])
        copy_out(pair).start()
        return carry

    lax.fori_loop(0, pairs, body, 0)
    for pair in range(max(pairs - 2, 0), pairs):
        copy_out(pair).wait()


def edge_kernel(
    f_own, f_oth, west_own, west_oth, east_own, east_oth, south_own, south_oth, north_own, north_oth,
    mask, coef_own, coef_oth, inter_own, inter_oth, wave,
    out,
    rows_own, rows_oth, adv, slots, in_sem, out_sem,
):
    del wave
    cells_x, width, bins = f_own.shape
    picked = ((0, 0), (cells_x - 2, 2))
    copies = [
        pltpu.make_async_copy(f.at[pl.ds(first, 2)], rows.at[pl.ds(at, 2)], in_sem.at[n, i])
        for n, (f, rows) in enumerate(((f_own, rows_own), (f_oth, rows_oth)))
        for i, (first, at) in enumerate(picked)
    ]
    for copy in copies:
        copy.start()
    for copy in copies:
        copy.wait()
    seas = []
    for i, x in enumerate((0, cells_x - 1)):
        sea = sea_column(mask, x, width)
        seas.append(sea)
        for rows, west, east, south, north, coef, col in (
            (rows_own, west_own, east_own, south_own, north_own, coef_own, 0),
            (rows_oth, west_oth, east_oth, south_oth, north_oth, coef_oth, bins),
        ):
            if i == 0:
                centre, west_row, east_row = rows.at[0], west.at[0], rows.at[1]
            else:
                centre, west_row, east_row = rows.at[3], rows.at[2], east.at[0]
            advect(
                centre, west_row, east_row, south.at[x], north.at[x], coef, sea, adv, i * width, col
            )
    finish(adv, inter_own, inter_oth, seas, slots)
    writes = [
        pltpu.make_async_copy(slots.at[i], out.at[x], out_sem.at[i])
        for i, x in enumerate((0, cells_x - 1))
    ]
    for copy in writes:
        copy.start()
    for copy in writes:
        copy.wait()


def lat_coriolis(cells_y):
    ny_total = lax.axis_size("gy") * cells_y
    lane = jnp.arange(2 * cells_y)
    lane = jnp.where(lane >= cells_y + cells_y // 2, lane - 2 * cells_y, lane)
    lat_index = lax.axis_index("gy") * cells_y + lane
    return jnp.sin(jnp.pi * ((lat_index.astype(F32) + 0.5) / ny_total - 0.5))[None, :]


def coefficients(courant):
    cour_x, cour_y = courant[0], courant[1]
    rows = [
        1.0 - jnp.abs(cour_x) - jnp.abs(cour_y),
        jnp.abs(cour_x),
        jnp.abs(cour_y),
        cour_x,
        cour_y,
    ]
    return jnp.stack(rows + [jnp.zeros_like(cour_x)] * 3)


def projections(proj_rows, courant):
    cour_x, cour_y = courant[0], courant[1]
    weights = jnp.stack(
        [
            1.0 - jnp.abs(cour_x) - jnp.abs(cour_y),
            jnp.maximum(cour_x, 0.0),
            -jnp.minimum(cour_x, 0.0),
            jnp.maximum(cour_y, 0.0),
            -jnp.minimum(cour_y, 0.0),
        ]
    )
    scaled = weights[:, None, :] * proj_rows.astype(F32)[None]
    return scaled.reshape(-1, proj_rows.shape[1]).astype(BF16)


VMEM = pl.BlockSpec(memory_space=pltpu.VMEM)
ANY = pl.BlockSpec(memory_space=pl.ANY)


def params(limit):
    return pltpu.CompilerParams(vmem_limit_bytes=limit * MIB)


def local(spectrum, sea_mask, courant, interaction, stokes_proj, currents, level_drag):
    cells_x, cells_y, bins = spectrum.shape
    levels = currents.shape[1]
    chans = 2 * levels
    fields = chans + 16
    core = lax.axis_index("comp")
    swap = [(0, 1), (1, 0)]
    east, west = shifts("gx", True)
    north, south = shifts("gy", False)

    f_oth = lax.ppermute(spectrum, "comp", swap)
    courant_oth = lax.ppermute(courant, "comp", swap)
    south_own = lax.ppermute(spectrum[:, -1:], "gy", north)
    north_own = lax.ppermute(spectrum[:, :1], "gy", south)
    west_own = lax.ppermute(spectrum[-1:], "gx", east)
    east_own = lax.ppermute(spectrum[:1], "gx", west)
    south_oth = lax.ppermute(south_own, "comp", swap)
    north_oth = lax.ppermute(north_own, "comp", swap)
    west_oth = lax.ppermute(west_own, "comp", swap)
    east_oth = lax.ppermute(east_own, "comp", swap)

    sea = sea_mask.astype(F32)
    coef_own, coef_oth = coefficients(courant), coefficients(courant_oth)
    own_at, oth_at = core * bins, (1 - core) * bins
    inter_own = lax.dynamic_slice(interaction, (own_at, own_at), (bins, bins))
    inter_oth = lax.dynamic_slice(interaction, (oth_at, own_at), (bins, bins))
    proj_t = lax.dynamic_slice_in_dim(stokes_proj, core * levels, levels, 2)
    proj_t = jnp.transpose(proj_t, (0, 2, 1)).reshape(chans, -1)
    wt_own = projections(lax.dynamic_slice_in_dim(proj_t, own_at, bins, 1), courant)
    wt_oth = projections(lax.dynamic_slice_in_dim(proj_t, oth_at, bins, 1), courant_oth)
    cur = jnp.concatenate(
        [
            jnp.transpose(currents, (2, 0, 1, 3)).reshape(cells_x, chans, cells_y),
            jnp.broadcast_to(sea[:, None, :], (cells_x, 16, cells_y)),
        ],
        1,
    )

    side_rows = (EDGE + 1) * chans + EDGE * fields
    message = lambda rows: jax.ShapeDtypeStruct((rows, cells_y), BF16)
    s_main, s_aux, to_e, to_w, to_n, to_s, to_ne, to_nw, to_se, to_sw = pl.pallas_call(
        project_kernel,
        out_shape=(
            jax.ShapeDtypeStruct((cells_x + 2, chans, cells_y), F32),
            jax.ShapeDtypeStruct((cells_x, chans, cells_y), F32),
            message(side_rows),
            message(side_rows),
            message(chans + fields),
            message(chans + fields),
            *[message(fields)] * 4,
        ),
        in_specs=[VMEM] * 5,
        out_specs=(VMEM,) * 10,
        scratch_shapes=[pltpu.VMEM((cells_x, PARTS * chans, cells_y), F32)],
        compiler_params=params(20),
        cost_estimate=pl.CostEstimate(flops=3 * 10**9, bytes_accessed=8 * MIB, transcendentals=0),
        name="project",
    )(
        spectrum.reshape(-1, bins), f_oth.reshape(-1, bins), wt_own, wt_oth, cur
    )
    from_w = lax.ppermute(to_e, "gx", east)
    from_e = lax.ppermute(to_w, "gx", west)
    from_s = lax.ppermute(to_n, "gy", north)
    from_n = lax.ppermute(to_s, "gy", south)
    from_sw = lax.ppermute(to_ne, ("gx", "gy"), diagonal(1, 1))
    from_se = lax.ppermute(to_nw, ("gx", "gy"), diagonal(-1, 1))
    from_nw = lax.ppermute(to_se, ("gx", "gy"), diagonal(1, -1))
    from_ne = lax.ppermute(to_sw, ("gx", "gy"), diagonal(-1, -1))

    wave_type = jax.ShapeDtypeStruct(spectrum.shape, BF16)
    wave = pl.pallas_call(
        interior_kernel,
        out_shape=wave_type,
        in_specs=[VMEM] * 11,
        out_specs=ANY,
        scratch_shapes=[
            pltpu.VMEM((2 * cells_y, 2 * bins), BF16),
            pltpu.VMEM((2, 2, cells_y, bins), BF16),
            pltpu.SemaphoreType.DMA((2,)),
        ],
        compiler_params=params(20),
        cost_estimate=pl.CostEstimate(flops=4 * 10**9, bytes_accessed=10 * MIB, transcendentals=0),
        name="interior",
    )(
        spectrum, f_oth, south_own, south_oth, north_own, north_oth,
        sea, coef_own, coef_oth, inter_own, inter_oth,
    )
    out_type = jax.ShapeDtypeStruct(currents.shape, F32)
    currents_out = pl.pallas_call(
        momentum_kernel,
        out_shape=out_type,
        in_specs=[VMEM] * 13,
        out_specs=ANY,
        scratch_shapes=[
            pltpu.VMEM((cells_x + 2 * SUBSTEPS, fields, 2 * cells_y), F32),
            pltpu.VMEM((cells_x + 2 * SUBSTEPS, chans, 2 * cells_y), F32),
            pltpu.VMEM((cells_x + 2 * SUBSTEPS - 2, chans, 2 * cells_y), F32),
            pltpu.VMEM((cells_x, chans, cells_y), F32),
            pltpu.SemaphoreType.DMA((2, cells_x)),
        ],
        compiler_params=params(20),
        cost_estimate=pl.CostEstimate(flops=10**8, bytes_accessed=4 * MIB, transcendentals=0),
        name="momentum",
    )(
        s_main, s_aux, cur, from_w, from_e, from_s, from_n, from_sw, from_se, from_nw, from_ne,
        level_drag[:, None], lat_coriolis(cells_y),
    )
    wave_out = pl.pallas_call(
        edge_kernel,
        out_shape=wave_type,
        in_specs=[ANY] * 2 + [VMEM] * 13 + [ANY],
        out_specs=ANY,
        input_output_aliases={15: 0},
        scratch_shapes=[
            pltpu.VMEM((4, cells_y, bins), BF16),
            pltpu.VMEM((4, cells_y, bins), BF16),
            pltpu.VMEM((2 * cells_y, 2 * bins), BF16),
            pltpu.VMEM((2, cells_y, bins), BF16),
            pltpu.SemaphoreType.DMA((2, 2)),
            pltpu.SemaphoreType.DMA((2,)),
        ],
        compiler_params=params(20),
        cost_estimate=pl.CostEstimate(flops=10**9, bytes_accessed=3 * MIB, transcendentals=0),
        name="edge",
    )(
        spectrum, f_oth, west_own, west_oth, east_own, east_oth, south_own, south_oth, north_own, north_oth,
        sea, coef_own, coef_oth, inter_own, inter_oth, wave,
    )
    return (wave_out, currents_out)


def solution(mesh):
    in_specs = (
        P("gx", "gy", "comp"),
        P("gx", "gy"),
        P(None, "comp"),
        P(),
        P(),
        P(None, "comp", "gx", "gy"),
        P("comp"),
    )
    out_specs = (P("gx", "gy", "comp"), P(None, "comp", "gx", "gy"))
    return jax.shard_map(local, mesh=mesh, in_specs=in_specs, out_specs=out_specs, check_vma=False)
```

time: 114 us -> 82.8 us (0.73)
  the two profiles are of different devices: /device:TPU:0 before, /device:TPU:6 now
where the time goes in v2:
time: 82.8 us; the launch traced here: 81.9 us
  starting transfers between devices  40 us (48%)
  Pallas kernels  20.6 us (25%)
  local copies, waits for them, and re-layouts  14.8 us (18%)
  other arithmetic  5.48 us (7%)
  between operations  0.96 us (1%)
    ppermute x1, starting transfers between devices, local(): from_ne = lax.ppermute(to_sw, ('gx', 'gy'), diagonal(-1, -1))  10.5 us
    pallas_call x1, Pallas kernels, local(): pl.pallas_call(interior_kernel, out_shape=wave_type, in_specs=[VMEM] * 11...  9.91 us
    ppermute x1, starting transfers between devices, local(): from_nw = lax.ppermute(to_se, ('gx', 'gy'), diagonal(1, -1))  5.45 us
    ppermute x1, starting transfers between devices, local(): north_own = lax.ppermute(spectrum[:, :1], 'gy', south)  5.14 us
    ppermute x1, starting transfers between devices, local(): from_n = lax.ppermute(to_s, 'gy', south)  4.91 us
    ppermute x1, starting transfers between devices, local(): from_e = lax.ppermute(to_w, 'gx', west)  3.8 us
    pallas_call x1, Pallas kernels, local(): pl.pallas_call(edge_kernel, out_shape=wave_type, in_specs=[ANY] * 2 + [VM...  3.69 us
    pallas_call x1, Pallas kernels, local(): pl.pallas_call(project_kernel, out_shape=(jax.ShapeDtypeStruct((cells_x +...  3.6 us
  transfers between devices with their start and end apart: 18, of which 0 were waited for; matrix products, arithmetic and copies ran while one was open for 21% of the time, Pallas kernels for 21%

profile of v2, /device:TPU:6, one launch (start us, length us, event | category | flops | bytes accessed | tf_op | source)
XLA Modules:
  0.0 81.9 jit_solution(16023453306398772121)
XLA Ops:
  0.7 1.7 %fusion.9 = (bf16[1,128,512]{2,1,0:T(8,128)(2,1)}, bf16[1,128,512]{2,1,0:T(8,128)(2,1)}) fusion(bf16[16,128,512]{2,1,0:T(8,128)(2,1)} %f_own.3), kind=kLoop, calls=%fused_computation.30 | loop fusion | bytes 524288 | tf_op jit(solution)/shard_map/slice | solution.py:411
  2.4 1.6 %collective-permute-start.1 = (bf16[1,128,512]{2,1,0:T(8,128)(2,1)}, bf16[1,128,512]{2,1,0:T(8,128)(2,1)}, u32[]{:S(2)}, u32[]{:S(2)}) collective-permute-start(bf16[1,128,512]{2,1,0:T(8,128)(2,1)} %get-tuple-element.27), channel_id=1, source_target_pairs={{0,8},{8,16},{16,24},{24,0},{1,9},{9,17},{17,25},{25,1},{2,10},{10... | collective-permute-start | bytes 393224 | tf_op jit(solution)/shard_map/ppermute | solution.py:410
  4.0 2.2 %collective-permute-start.3 = (bf16[1,128,512]{2,1,0:T(8,128)(2,1)}, bf16[1,128,512]{2,1,0:T(8,128)(2,1)}, u32[]{:S(2)}, u32[]{:S(2)}) collective-permute-start(bf16[1,128,512]{2,1,0:T(8,128)(2,1)} %get-tuple-element.26), channel_id=1, source_target_pairs={{8,0},{16,8},{24,16},{0,24},{9,1},{17,9},{25,17},{1,25},{10,2},{18... | collective-permute-start | bytes 393224 | tf_op jit(solution)/shard_map/ppermute | solution.py:411
  6.2 1.6 %fusion.8 = (bf16[16,1,512]{2,1,0:T(2,128)(2,1)}, bf16[16,1,512]{2,1,0:T(2,128)(2,1)}) fusion(bf16[16,128,512]{2,1,0:T(8,128)(2,1)} %f_own.3), kind=kLoop, calls=%fused_computation.29 | loop fusion | bytes 65536 | tf_op jit(solution)/shard_map/slice | solution.py:409
  7.9 1.3 %collective-permute-start.5 = (bf16[16,1,512]{2,1,0:T(2,128)(2,1)}, bf16[16,1,512]{2,1,0:T(2,128)(2,1)}, u32[]{:S(2)}, u32[]{:S(2)}) collective-permute-start(bf16[16,1,512]{2,1,0:T(2,128)(2,1)} %get-tuple-element.25), channel_id=1, source_target_pairs={{0,2},{2,4},{4,6},{1,3},{3,5},{5,7},{8,10},{10,12},{12,14},{9,11},... | collective-permute-start | bytes 49160 | tf_op jit(solution)/shard_map/ppermute | solution.py:408
  9.3 0.7 convert_element_type.29.mask
  10.0 1.2 %copy.10 = f32[16,2,32,128]{3,2,1,0:T(8,128)S(1)} copy(f32[16,2,32,128]{3,0,2,1:T(8,128)} %bitcast.15) | data formatting | bytes 1048576 | tf_op jit(solution)/shard_map/transpose | solution.py:428
  11.3 0.7 dynamic-slice_convert_fusion
  12.1 0.8 copy-done.8
  12.9 0.9 %fusion.7 = (bf16[512,512]{1,0:T(8,128)(2,1)S(1)}, bf16[512,512]{1,0:T(8,128)(2,1)}) fusion(bf16[1024,1024]{1,0:T(8,128)(2,1)S(1)} %copy-done.8, s32[]{:T(128)S(6)} %select_n.25, s32[]{:T(128)S(6)} %select_n.24), kind=kLoop, calls=%fused_computation.28 | loop fusion | bytes 2097160 | tf_op jit(solution)/shard_map/dynamic_slice | solution.py:421
  13.8 0.6 minimum_negate_fusion.2
  14.5 0.7 copy.11.drag
  15.7 1.3 %stack.8.coef_own = f32[8,512]{1,0:T(8,128)} concatenate(f32[1,512]{1,0:T(1,128)} %get-tuple-element.38, f32[1,512]{1,0:T(1,128)} %get-tuple-element.43, f32[1,512]{1,0:T(1,128)} %get-tuple-element.42, f32[2,512]{1,0:T(2,128)} %param.9, f32[1,512]{1,0:T(1,128)} %broadcast.89, f32[2,512]{1,0:T(2,128)S(1)} %broadcast.90), dimensions={0} | concatenate | bytes 32768 | tf_op jit(solution)/shard_map/stack | solution.py:370
  17.1 1.3 %stack.10 = f32[5,512]{1,0:T(8,128)} concatenate(f32[1,512]{1,0:T(1,128)} %get-tuple-element.38, f32[1,512]{1,0:T(1,128)} %get-tuple-element.39, f32[1,512]{1,0:T(1,128)} %get-tuple-element.40, f32[1,512]{1,0:T(1,128)} %get-tuple-element.41, f32[1,512]{1,0:T(1,128)} %get-tuple-element.37), dimensions={0} | concatenate | bytes 20480 | tf_op jit(solution)/shard_map/stack | solution.py:375
  18.4 5.1 %collective-permute-start.7 = (bf16[16,1,512]{2,1,0:T(2,128)(2,1)}, bf16[16,1,512]{2,1,0:T(2,128)(2,1)}, u32[]{:S(2)}, u32[]{:S(2)}) collective-permute-start(bf16[16,1,512]{2,1,0:T(2,128)(2,1)} %get-tuple-element.24), channel_id=1, source_target_pairs={{2,0},{4,2},{6,4},{3,1},{5,3},{7,5},{10,8},{12,10},{14,12},{11,9},... | collective-permute-start | bytes 49160 | tf_op jit(solution)/shard_map/ppermute | solution.py:409
  23.5 1.4 %minimum_negate_fusion = (f32[1,512]{1,0:T(1,128)}, f32[1,512]{1,0:T(1,128)}, f32[1,512]{1,0:T(1,128)}, f32[1,512]{1,0:T(1,128)}, f32[1,512]{1,0:T(1,128)}, /*index=5*/f32[1,512]{1,0:T(1,128)}, f32[1,512]{1,0:T(1,128)}) fusion(f32[2,512]{1,0:T(2,128)} %collective-permute-done.9), kind=kLoop, calls=%fused_computation.6 | loop fusion | flops 5120 | bytes 18432 | tf_op jit(solution)/shard_map/neg | solution.py:381
  24.9 1.3 %stack.11 = f32[5,512]{1,0:T(8,128)} concatenate(f32[1,512]{1,0:T(1,128)} %get-tuple-element.31, f32[1,512]{1,0:T(1,128)} %get-tuple-element.32, f32[1,512]{1,0:T(1,128)} %get-tuple-element.33, f32[1,512]{1,0:T(1,128)} %get-tuple-element.34, f32[1,512]{1,0:T(1,128)} %get-tuple-element.30), dimensions={0} | concatenate | bytes 20480 | tf_op jit(solution)/shard_map/stack | solution.py:375
  26.2 1.9 %multiply_convert_fusion = (bf16[5,64,512]{2,1,0:T(8,128)(2,1)}, bf16[5,64,512]{2,1,0:T(8,128)(2,1)}) fusion(f32[64,512]{1,0:T(8,128)} %get-tuple-element.28, f32[5,512]{1,0:T(8,128)} %stack.11, f32[64,512]{1,0:T(8,128)} %get-tuple-element.29, f32[5,512]{1,0:T(8,128)} %stack.10), kind=kLoop, calls=%fused_computation.1 | loop fusion | flops 655360 | bytes 937984 | tf_op jit(solution)/shard_map/convert_element_type | solution.py:385
  28.1 1.3 %stack.9.coef_oth = f32[8,512]{1,0:T(8,128)} concatenate(f32[1,512]{1,0:T(1,128)} %get-tuple-element.31, f32[1,512]{1,0:T(1,128)} %get-tuple-element.36, f32[1,512]{1,0:T(1,128)} %get-tuple-element.35, f32[2,512]{1,0:T(2,128)} %collective-permute-done.9, f32[1,512]{1,0:T(1,128)} %broadcast.89, f32[2,512]{1,0:T(2,128)S(1)} %broadcast.90), dimensions={0} | concatenate | bytes 32768 | tf_op jit(solution)/shard_map/stack | solution.py:370
  30.5 1.0 %copy-done.3 = bf16[5,64,512]{2,1,0:T(8,128)(2,1)S(1)} copy-done((bf16[5,64,512]{2,1,0:T(8,128)(2,1)S(1)}, bf16[5,64,512]{2,1,0:T(8,128)(2,1)}, u32[]{:S(2)}) %copy-start.3) | copy-done | bytes 327704
  31.5 1.0 %copy-done.4 = bf16[5,64,512]{2,1,0:T(8,128)(2,1)S(1)} copy-done((bf16[5,64,512]{2,1,0:T(8,128)(2,1)S(1)}, bf16[5,64,512]{2,1,0:T(8,128)(2,1)}, u32[]{:S(2)}) %copy-start.4) | copy-done | bytes 327704
  32.5 3.6 %project.1 = (f32[18,64,128]{2,1,0:T(8,128)S(1)}, f32[16,64,128]{2,1,0:T(8,128)S(1)}, bf16[496,128]{1,0:T(8,128)(2,1)S(1)}, bf16[496,128]{1,0:T(8,128)(2,1)S(1)}...) custom-call(bf16[2048,512]{1,0:T(8,128)(2,1)S(1)} %bitcast.10, ...), custom_call_target="tpu_custom_call" | custom-call | flops 3000000000 | bytes 8388608 | tf_op jit(solution)/shard_map/project/pallas_call | solution.py:436
  36.2 3.8 %collective-permute-start.11 = (bf16[496,128]{1,0:T(8,128)(2,1)S(1)}, bf16[496,128]{1,0:T(8,128)(2,1)S(1)}, u32[]{:S(2)}, u32[]{:S(2)}) collective-permute-start(bf16[496,128]{1,0:T(8,128)(2,1)S(1)} %get-tuple-element.15), channel_id=1, source_target_pairs={{8,0},{16,8},{24,16},{0,24},{9,1},{17,9},{25,17},{1,25},{10,2},{18... | collective-permute-start | bytes 380936 | tf_op jit(solution)/shard_map/ppermute | solution.py:457
  40.0 1.3 %collective-permute-start.14 = (bf16[80,128]{1,0:T(8,128)(2,1)S(1)}, bf16[80,128]{1,0:T(8,128)(2,1)S(1)}, u32[]{:S(2)}, u32[]{:S(2)}) collective-permute-start(bf16[80,128]{1,0:T(8,128)(2,1)S(1)} %get-tuple-element.18), channel_id=1, source_target_pairs={{0,10},{2,12},{4,14},{8,18},{10,20},{12,22},{16,26},{18,28},{20,30... | collective-permute-start | bytes 61448 | tf_op jit(solution)/shard_map/ppermute | solution.py:460
  41.3 1.3 %collective-permute-start.15 = (bf16[80,128]{1,0:T(8,128)(2,1)S(1)}, bf16[80,128]{1,0:T(8,128)(2,1)S(1)}, u32[]{:S(2)}, u32[]{:S(2)}) collective-permute-start(bf16[80,128]{1,0:T(8,128)(2,1)S(1)} %get-tuple-element.19), channel_id=1, source_target_pairs={{0,26},{2,28},{4,30},{8,2},{10,4},{12,6},{16,10},{18,12},{20,14},{... | collective-permute-start | bytes 61448 | tf_op jit(solution)/shard_map/ppermute | solution.py:461
  42.6 5.4 %collective-permute-start.16 = (bf16[80,128]{1,0:T(8,128)(2,1)S(1)}, bf16[80,128]{1,0:T(8,128)(2,1)S(1)}, u32[]{:S(2)}, u32[]{:S(2)}) collective-permute-start(bf16[80,128]{1,0:T(8,128)(2,1)S(1)} %get-tuple-element.20), channel_id=1, source_target_pairs={{2,8},{4,10},{6,12},{10,16},{12,18},{14,20},{18,24},{20,26},{22,28... | collective-permute-start | bytes 61448 | tf_op jit(solution)/shard_map/ppermute | solution.py:462
  48.1 9.9 %interior.1.wave = bf16[16,128,512]{2,1,0:T(8,128)(2,1)} custom-call(bf16[16,128,512]{2,1,0:T(8,128)(2,1)S(1)} %copy-done.1, bf16[16,128,512]{2,1,0:T(8,128)(2,1)} %collective-permute-done.f_oth, bf16[16,1,512]{2,1,0:T(2,128)(2,1)} %collective-permute-done.5.south_own, bf16[16,1,512]{2,1,0:T(2,128)(2,1)S(1)} %collective-permute-done.6.south_oth, ...), custom_call_target="tpu_custom_call" | custom-call | flops 4000000000 | bytes 10485760 | tf_op jit(solution)/shard_map/interior/pallas_call | solution.py:466
  58.0 1.3 %collective-permute-start.12 = (bf16[144,128]{1,0:T(8,128)(2,1)S(1)}, bf16[144,128]{1,0:T(8,128)(2,1)S(1)}, u32[]{:S(2)}, u32[]{:S(2)}) collective-permute-start(bf16[144,128]{1,0:T(8,128)(2,1)S(1)} %get-tuple-element.16), channel_id=1, source_target_pairs={{0,2},{2,4},{4,6},{1,3},{3,5},{5,7},{8,10},{10,12},{12,14},{9,11},... | collective-permute-start | bytes 110600 | tf_op jit(solution)/shard_map/ppermute | solution.py:458
  59.3 4.9 %collective-permute-start.13 = (bf16[144,128]{1,0:T(8,128)(2,1)S(1)}, bf16[144,128]{1,0:T(8,128)(2,1)S(1)}, u32[]{:S(2)}, u32[]{:S(2)}) collective-permute-start(bf16[144,128]{1,0:T(8,128)(2,1)S(1)} %get-tuple-element.17), channel_id=1, source_target_pairs={{2,0},{4,2},{6,4},{3,1},{5,3},{7,5},{10,8},{12,10},{14,12},{11,9},... | collective-permute-start | bytes 110600 | tf_op jit(solution)/shard_map/ppermute | solution.py:459
  64.2 10.5 %collective-permute-start.17 = (bf16[80,128]{1,0:T(8,128)(2,1)S(1)}, bf16[80,128]{1,0:T(8,128)(2,1)S(1)}, u32[]{:S(2)}, u32[]{:S(2)}) collective-permute-start(bf16[80,128]{1,0:T(8,128)(2,1)S(1)} %get-tuple-element.21), channel_id=1, source_target_pairs={{2,24},{4,26},{6,28},{10,0},{12,2},{14,4},{18,8},{20,10},{22,12},{... | collective-permute-start | bytes 61448 | tf_op jit(solution)/shard_map/ppermute | solution.py:463
  74.7 3.7 %edge.1 = bf16[16,128,512]{2,1,0:T(8,128)(2,1)} custom-call(bf16[16,128,512]{2,1,0:T(8,128)(2,1)S(1)} %copy-done.1, bf16[16,128,512]{2,1,0:T(8,128)(2,1)} %collective-permute-done.f_oth, bf16[1,128,512]{2,1,0:T(8,128)(2,1)} %collective-permute-done.1.west_own, ...), custom_call_target="tpu_custom_call", output_to_operand_aliasing={{}: (15, {})} | custom-call | flops 1000000000 | bytes 3145728 | tf_op jit(solution)/shard_map/edge/pallas_call | solution.py:503
  78.5 3.4 %momentum.1 = f32[2,32,16,128]{3,2,1,0:T(8,128)} custom-call(f32[18,64,128]{2,1,0:T(8,128)S(1)} %get-tuple-element.12.s_main, f32[16,64,128]{2,1,0:T(8,128)S(1)} %get-tuple-element.13.s_aux, f32[16,80,128]{2,1,0:T(8,128)S(1)} %pad_maximum_fusion.cur, bf16[496,128]{1,0:T(8,128)(2,1)S(1)} %collective-permute-done.10.from_w, ...), custom_call_target="tpu_custom_call" | custom-call | flops 100000000 | bytes 4194304 | tf_op jit(solution)/shard_map/momentum/pallas_call | solution.py:484
  (50 shorter events, 2.0 us)
Async XLA Ops:
  0.6 10.6 %copy-start = (bf16[2,1024,64]{1,2,0:T(8,128)(2,1)S(1)}, bf16[2,1024,64]{1,2,0:T(8,128)(2,1)}, u32[]{:S(2)}) copy-start(bf16[2,1024,64]{1,2,0:T(8,128)(2,1)} %param.11) | copy-start | bytes 786436
  0.6 29.9 %collective-permute-start = (bf16[16,128,512]{2,1,0:T(8,128)(2,1)}, bf16[16,128,512]{2,1,0:T(8,128)(2,1)}, u32[]{:S(2)}, u32[]{:S(2)}) collective-permute-start(bf16[16,128,512]{2,1,0:T(8,128)(2,1)} %f_own.3), channel_id=1, source_target_pairs={{0,1},{1,0},{2,3},{3,2},{4,5},{5,4},{6,7},{7,6},{8,9},{9,8},{10,11... | collective-permute-start | bytes 6291464 | tf_op jit(solution)/shard_map/ppermute | solution.py:406
  2.4 27.6 %collective-permute-start.1 = (bf16[1,128,512]{2,1,0:T(8,128)(2,1)}, bf16[1,128,512]{2,1,0:T(8,128)(2,1)}, u32[]{:S(2)}, u32[]{:S(2)}) collective-permute-start(bf16[1,128,512]{2,1,0:T(8,128)(2,1)} %get-tuple-element.27), channel_id=1, source_target_pairs={{0,8},{8,16},{16,24},{24,0},{1,9},{9,17},{17,25},{25,1},{2,10},{10... | collective-permute-start | bytes 393224 | tf_op jit(solution)/shard_map/ppermute | solution.py:410
  4.0 26.2 %collective-permute-start.3 = (bf16[1,128,512]{2,1,0:T(8,128)(2,1)}, bf16[1,128,512]{2,1,0:T(8,128)(2,1)}, u32[]{:S(2)}, u32[]{:S(2)}) collective-permute-start(bf16[1,128,512]{2,1,0:T(8,128)(2,1)} %get-tuple-element.26), channel_id=1, source_target_pairs={{8,0},{16,8},{24,16},{0,24},{9,1},{17,9},{25,17},{1,25},{10,2},{18... | collective-permute-start | bytes 393224 | tf_op jit(solution)/shard_map/ppermute | solution.py:411
  7.9 21.6 %collective-permute-start.5 = (bf16[16,1,512]{2,1,0:T(2,128)(2,1)}, bf16[16,1,512]{2,1,0:T(2,128)(2,1)}, u32[]{:S(2)}, u32[]{:S(2)}) collective-permute-start(bf16[16,1,512]{2,1,0:T(2,128)(2,1)} %get-tuple-element.25), channel_id=1, source_target_pairs={{0,2},{2,4},{4,6},{1,3},{3,5},{5,7},{8,10},{10,12},{12,14},{9,11},... | collective-permute-start | bytes 49160 | tf_op jit(solution)/shard_map/ppermute | solution.py:408
  9.2 9.2 %collective-permute-start.9 = (f32[2,512]{1,0:T(2,128)}, f32[2,512]{1,0:T(2,128)}, u32[]{:S(2)}, u32[]{:S(2)}) collective-permute-start(f32[2,512]{1,0:T(2,128)} %param.9), channel_id=1, source_target_pairs={{0,1},{1,0},{2,3},{3,2},{4,5},{5,4},{6,7},{7,6},{8,9},{9,8},{10,11... | collective-permute-start | bytes 12296 | tf_op jit(solution)/shard_map/ppermute | solution.py:407
  11.2 1.7 %copy-start.8 = (bf16[1024,1024]{1,0:T(8,128)(2,1)S(1)}, bf16[1024,1024]{1,0:T(8,128)(2,1)}, u32[]{:S(2)}) copy-start(bf16[1024,1024]{1,0:T(8,128)(2,1)} %param.10) | copy-start | bytes 6291460
  11.2 2.6 %copy-start.9 = (f32[2,512]{1,0:T(2,128)S(1)}, f32[2,512]{1,0:T(2,128)}, u32[]{:S(2)}) copy-start(f32[2,512]{1,0:T(2,128)} %param.9) | copy-start | bytes 12292
  11.2 3.3 %copy-start.10 = (f32[32]{0:T(128)S(1)}, f32[32]{0:T(128)}, u32[]{:S(2)}) copy-start(f32[32]{0:T(128)} %param.13) | copy-start | bytes 388
  12.0 18.5 %copy-start.1 = (bf16[16,128,512]{2,1,0:T(8,128)(2,1)S(1)}, bf16[16,128,512]{2,1,0:T(8,128)(2,1)}, u32[]{:S(2)}) copy-start(bf16[16,128,512]{2,1,0:T(8,128)(2,1)} %f_own.3) | copy-start | bytes 6291460
  18.4 11.3 %collective-permute-start.7 = (bf16[16,1,512]{2,1,0:T(2,128)(2,1)}, bf16[16,1,512]{2,1,0:T(2,128)(2,1)}, u32[]{:S(2)}, u32[]{:S(2)}) collective-permute-start(bf16[16,1,512]{2,1,0:T(2,128)(2,1)} %get-tuple-element.24), channel_id=1, source_target_pairs={{2,0},{4,2},{6,4},{3,1},{5,3},{7,5},{10,8},{12,10},{14,12},{11,9},... | collective-permute-start | bytes 49160 | tf_op jit(solution)/shard_map/ppermute | solution.py:409
  29.5 6.7 %collective-permute-start.6 = (bf16[16,1,512]{2,1,0:T(2,128)(2,1)}, bf16[16,1,512]{2,1,0:T(2,128)(2,1)S(1)}, u32[]{:S(2)}, u32[]{:S(2)}) collective-permute-start(bf16[16,1,512]{2,1,0:T(2,128)(2,1)} %collective-permute-done.5.south_own), channel_id=1, source_target_pairs={{0,1},{1,0},{2,3},{3,2},{4,5},{5,4},{6,7},{7,6},{8,9},{9,8},{10,11... | collective-permute-start | bytes 49160 | tf_op jit(solution)/shard_map/ppermute | solution.py:412
  29.7 10.3 %collective-permute-start.8 = (bf16[16,1,512]{2,1,0:T(2,128)(2,1)}, bf16[16,1,512]{2,1,0:T(2,128)(2,1)S(1)}, u32[]{:S(2)}, u32[]{:S(2)}) collective-permute-start(bf16[16,1,512]{2,1,0:T(2,128)(2,1)} %collective-permute-done.7.north_own), channel_id=1, source_target_pairs={{0,1},{1,0},{2,3},{3,2},{4,5},{5,4},{6,7},{7,6},{8,9},{9,8},{10,11... | collective-permute-start | bytes 49160 | tf_op jit(solution)/shard_map/ppermute | solution.py:413
  30.0 11.3 %collective-permute-start.2 = (bf16[1,128,512]{2,1,0:T(8,128)(2,1)}, bf16[1,128,512]{2,1,0:T(8,128)(2,1)S(1)}, u32[]{:S(2)}, u32[]{:S(2)}) collective-permute-start(bf16[1,128,512]{2,1,0:T(8,128)(2,1)} %collective-permute-done.1.west_own), channel_id=1, source_target_pairs={{0,1},{1,0},{2,3},{3,2},{4,5},{5,4},{6,7},{7,6},{8,9},{9,8},{10,11... | collective-permute-start | bytes 393224 | tf_op jit(solution)/shard_map/ppermute | solution.py:414
  30.2 12.4 %collective-permute-start.4 = (bf16[1,128,512]{2,1,0:T(8,128)(2,1)}, bf16[1,128,512]{2,1,0:T(8,128)(2,1)S(1)}, u32[]{:S(2)}, u32[]{:S(2)}) collective-permute-start(bf16[1,128,512]{2,1,0:T(8,128)(2,1)} %collective-permute-done.3.east_own), channel_id=1, source_target_pairs={{0,1},{1,0},{2,3},{3,2},{4,5},{5,4},{6,7},{7,6},{8,9},{9,8},{10,11... | collective-permute-start | bytes 393224 | tf_op jit(solution)/shard_map/ppermute | solution.py:415
  30.5 1.0 %copy-start.3 = (bf16[5,64,512]{2,1,0:T(8,128)(2,1)S(1)}, bf16[5,64,512]{2,1,0:T(8,128)(2,1)}, u32[]{:S(2)}) copy-start(bf16[5,64,512]{2,1,0:T(8,128)(2,1)} %get-tuple-element.44) | copy-start | bytes 983044
  31.5 1.0 %copy-start.4 = (bf16[5,64,512]{2,1,0:T(8,128)(2,1)S(1)}, bf16[5,64,512]{2,1,0:T(8,128)(2,1)}, u32[]{:S(2)}) copy-start(bf16[5,64,512]{2,1,0:T(8,128)(2,1)} %get-tuple-element.45) | copy-start | bytes 983044
  32.5 15.6 %copy-start.2 = (bf16[512,512]{1,0:T(8,128)(2,1)S(1)}, bf16[512,512]{1,0:T(8,128)(2,1)}, u32[]{:S(2)}) copy-start(bf16[512,512]{1,0:T(8,128)(2,1)} %get-tuple-element.23.inter_own) | copy-start | bytes 1572868
  32.5 15.6 %copy-start.6 = (f32[8,512]{1,0:T(8,128)S(1)}, f32[8,512]{1,0:T(8,128)}, u32[]{:S(2)}) copy-start(f32[8,512]{1,0:T(8,128)} %stack.8.coef_own) | copy-start | bytes 49156
  32.5 15.6 %copy-start.7 = (f32[8,512]{1,0:T(8,128)S(1)}, f32[8,512]{1,0:T(8,128)}, u32[]{:S(2)}) copy-start(f32[8,512]{1,0:T(8,128)} %stack.9.coef_oth) | copy-start | bytes 49156
  36.1 42.4 %collective-permute-start.10 = (bf16[496,128]{1,0:T(8,128)(2,1)S(1)}, bf16[496,128]{1,0:T(8,128)(2,1)S(1)}, u32[]{:S(2)}, u32[]{:S(2)}) collective-permute-start(bf16[496,128]{1,0:T(8,128)(2,1)S(1)} %get-tuple-element.14), channel_id=1, source_target_pairs={{0,8},{8,16},{16,24},{24,0},{1,9},{9,17},{17,25},{25,1},{2,10},{10... | collective-permute-start | bytes 380936 | tf_op jit(solution)/shard_map/ppermute | solution.py:456
  36.2 42.3 %collective-permute-start.11 = (bf16[496,128]{1,0:T(8,128)(2,1)S(1)}, bf16[496,128]{1,0:T(8,128)(2,1)S(1)}, u32[]{:S(2)}, u32[]{:S(2)}) collective-permute-start(bf16[496,128]{1,0:T(8,128)(2,1)S(1)} %get-tuple-element.15), channel_id=1, source_target_pairs={{8,0},{16,8},{24,16},{0,24},{9,1},{17,9},{25,17},{1,25},{10,2},{18... | collective-permute-start | bytes 380936 | tf_op jit(solution)/shard_map/ppermute | solution.py:457
  40.0 18.0 %collective-permute-start.14 = (bf16[80,128]{1,0:T(8,128)(2,1)S(1)}, bf16[80,128]{1,0:T(8,128)(2,1)S(1)}, u32[]{:S(2)}, u32[]{:S(2)}) collective-permute-start(bf16[80,128]{1,0:T(8,128)(2,1)S(1)} %get-tuple-element.18), channel_id=1, source_target_pairs={{0,10},{2,12},{4,14},{8,18},{10,20},{12,22},{16,26},{18,28},{20,30... | collective-permute-start | bytes 61448 | tf_op jit(solution)/shard_map/ppermute | solution.py:460
  41.3 18.0 %collective-permute-start.15 = (bf16[80,128]{1,0:T(8,128)(2,1)S(1)}, bf16[80,128]{1,0:T(8,128)(2,1)S(1)}, u32[]{:S(2)}, u32[]{:S(2)}) collective-permute-start(bf16[80,128]{1,0:T(8,128)(2,1)S(1)} %get-tuple-element.19), channel_id=1, source_target_pairs={{0,26},{2,28},{4,30},{8,2},{10,4},{12,6},{16,10},{18,12},{20,14},{... | collective-permute-start | bytes 61448 | tf_op jit(solution)/shard_map/ppermute | solution.py:461
  42.6 21.6 %collective-permute-start.16 = (bf16[80,128]{1,0:T(8,128)(2,1)S(1)}, bf16[80,128]{1,0:T(8,128)(2,1)S(1)}, u32[]{:S(2)}, u32[]{:S(2)}) collective-permute-start(bf16[80,128]{1,0:T(8,128)(2,1)S(1)} %get-tuple-element.20), channel_id=1, source_target_pairs={{2,8},{4,10},{6,12},{10,16},{12,18},{14,20},{18,24},{20,26},{22,28... | collective-permute-start | bytes 61448 | tf_op jit(solution)/shard_map/ppermute | solution.py:462
  58.0 20.4 %collective-permute-start.12 = (bf16[144,128]{1,0:T(8,128)(2,1)S(1)}, bf16[144,128]{1,0:T(8,128)(2,1)S(1)}, u32[]{:S(2)}, u32[]{:S(2)}) collective-permute-start(bf16[144,128]{1,0:T(8,128)(2,1)S(1)} %get-tuple-element.16), channel_id=1, source_target_pairs={{0,2},{2,4},{4,6},{1,3},{3,5},{5,7},{8,10},{10,12},{12,14},{9,11},... | collective-permute-start | bytes 110600 | tf_op jit(solution)/shard_map/ppermute | solution.py:458
  59.3 19.1 %collective-permute-start.13 = (bf16[144,128]{1,0:T(8,128)(2,1)S(1)}, bf16[144,128]{1,0:T(8,128)(2,1)S(1)}, u32[]{:S(2)}, u32[]{:S(2)}) collective-permute-start(bf16[144,128]{1,0:T(8,128)(2,1)S(1)} %get-tuple-element.17), channel_id=1, source_target_pairs={{2,0},{4,2},{6,4},{3,1},{5,3},{7,5},{10,8},{12,10},{14,12},{11,9},... | collective-permute-start | bytes 110600 | tf_op jit(solution)/shard_map/ppermute | solution.py:459
  64.2 14.3 %copy-start.5 = (f32[32,1]{1,0:T(8,128)S(1)}, f32[32,1]{1,0:T(8,128)}, u32[]{:S(2)}) copy-start(f32[32,1]{1,0:T(8,128)} %copy.11.drag) | copy-start | bytes 388
  64.2 14.2 %collective-permute-start.17 = (bf16[80,128]{1,0:T(8,128)(2,1)S(1)}, bf16[80,128]{1,0:T(8,128)(2,1)S(1)}, u32[]{:S(2)}, u32[]{:S(2)}) collective-permute-start(bf16[80,128]{1,0:T(8,128)(2,1)S(1)} %get-tuple-element.21), channel_id=1, source_target_pairs={{2,24},{4,26},{6,28},{10,0},{12,2},{14,4},{18,8},{20,10},{22,12},{... | collective-permute-start | bytes 61448 | tf_op jit(solution)/shard_map/ppermute | solution.py:463

commit v3 on v0

v3 whole, which is shorter than its diff:
```python
import functools

import jax
import jax.numpy as jnp
from jax import lax
from jax.experimental import pallas as pl
from jax.experimental.pallas import tpu as pltpu
from jax.sharding import PartitionSpec as P

SUBSTEPS = 3

time_step = 0.5
viscosity = 0.4

F32 = jnp.float32
BF16 = jnp.bfloat16
MIB = 1 << 20
EDGE = 3
MASK_ROWS = 16
SLOT = 8
CHUNK = 128
PARTS = 5


def ring(axis):
    count = lax.axis_size(axis)
    forward = [(i, (i + 1) % count) for i in range(count)]
    return forward, [(target, source) for source, target in forward]


def pairing(axis, first):
    swaps = [(i, i + 1) for i in range(first, lax.axis_size(axis) - 1, 2)]
    return swaps + [(target, source) for source, target in swaps]


def lane_of(rows, width):
    return lax.broadcasted_iota(jnp.int32, (rows, width), 1)


def between(lane, low, high):
    return (lane >= low) & (lane < high)


def chunks_of(bins):
    return [slice(j * CHUNK, (j + 1) * CHUNK) for j in range(bins // CHUNK)]


def load_currents(currents, rows, cur, sem):
    levels = currents.shape[1]
    return [
        pltpu.make_async_copy(
            currents.at[c, :, x, :], cur.at[i, pl.ds(c * levels, levels), :], sem.at[i, c]
        )
        for i, x in enumerate(rows)
        for c in range(2)
    ]


def sea_row(mask, x, rows):
    return jnp.broadcast_to(mask[x : x + 1, :].astype(F32), (rows, mask.shape[1]))


def outgoing_kernel(spectrum, currents, mask, msg_e, msg_w, cur, sem, row_sem):
    cells_x, width, bins = spectrum.shape
    chans = cur.shape[1]
    fields = chans + MASK_ROWS
    rows = list(range(EDGE)) + list(range(cells_x - EDGE, cells_x))
    copies = load_currents(currents, rows, cur, sem)
    for side, (msg, x) in enumerate(((msg_e, cells_x - 1), (msg_w, 0))):
        for j, cols in enumerate(chunks_of(bins)):
            copies.append(
                pltpu.make_async_copy(
                    spectrum.at[x, :, cols], msg.at[pl.ds(j * width, width), :], row_sem.at[side, j]
                )
            )
    for copy in copies:
        copy.start()
    for copy in copies:
        copy.wait()
    base = bins // CHUNK * width
    for i, x in enumerate(rows):
        msg = msg_w if i < EDGE else msg_e
        at = base + i % EDGE * fields
        msg[at : at + chans] = cur[i].astype(BF16)
        msg[at + chans : at + fields] = sea_row(mask, x, MASK_ROWS).astype(BF16)


def stokes_weights(proj, courant, core, owner, weights):
    levels = proj.shape[1] // 2
    bins = courant.shape[1]
    bins_at = pl.ds(pl.multiple_of(owner * bins, bins), bins)
    cour_x, cour_y = courant[0:1, :], courant[1:2, :]
    terms = (
        1.0 - jnp.abs(cour_x) - jnp.abs(cour_y),
        jnp.maximum(cour_x, 0.0),
        -jnp.minimum(cour_x, 0.0),
        jnp.maximum(cour_y, 0.0),
        -jnp.minimum(cour_y, 0.0),
    )
    for c in range(2):
        mine = proj[c, pl.ds(pl.multiple_of(core * levels, levels), levels), bins_at].astype(F32)
        for k, term in enumerate(terms):
            row = (2 * k + c) * levels
            weights[row : row + levels] = (mine * term).astype(BF16)


def project_kernel(
    f_own, f_oth, courant_own, courant_oth, stokes_proj, currents, mask,
    s_main, s_aux, s_edge, msg_a, msg_b,
    proj, wt_own, wt_oth, cur, sem,
):
    cells_x, width, bins = f_own.shape
    chans = s_main.shape[1]
    fields = chans + MASK_ROWS
    stride = width // (cells_x + 2)
    core = lax.axis_index("comp")
    copies = load_currents(currents, range(cells_x), cur, sem)
    for copy in copies:
        copy.start()
    stokes_weights(stokes_proj, courant_own, core, core, wt_own)
    stokes_weights(stokes_proj, courant_oth, core, 1 - core, wt_oth)
    contract = (((1,), (1,)), ((), ()))
    for pair in range(cells_x // 2):
        both = 0.0
        for wt, f in ((wt_own, f_own), (wt_oth, f_oth)):
            cells = f[2 * pair : 2 * pair + 2].reshape(2 * width, bins)
            both += lax.dot_general(wt[...], cells, contract, preferred_element_type=F32)
        proj[2 * pair] = both[:, :width]
        proj[2 * pair + 1] = both[:, width:]
    for copy in copies:
        copy.wait()

    lane = lane_of(chans, width)
    lane_f = lane_of(fields, width)

    def part(x, which):
        return proj[x, which * chans : (which + 1) * chans, :]

    pack_n = pack_s = jnp.zeros((chans, width), F32)
    cur_n = cur_s = jnp.zeros((fields, width), F32)
    for x in range(-1, cells_x + 1):
        start = stride * (x + 1)
        main = jnp.zeros((chans, width), F32)
        aux = jnp.zeros((chans, width), F32)
        if 0 <= x < cells_x:
            south = pltpu.roll(part(x, 3), 1, 1)
            north = pltpu.roll(part(x, 4), width - 1, 1)
            main = part(x, 0) + jnp.where(lane > 0, south, 0.0) + jnp.where(lane < width - 1, north, 0.0)
            aux = jnp.where(lane == 0, south, jnp.where(lane == width - 1, north, 0.0))
            s_aux[x] = aux
        if x >= 1:
            main += part(x - 1, 1)
        if x <= cells_x - 2:
            main += part(x + 1, 2)
        s_main[x + 1] = main
        if x < EDGE - 1 or x > cells_x - EDGE:
            at = x + 1 if x < EDGE - 1 else x - (cells_x - 2) + EDGE
            s_edge[at, :, :width] = main
            s_edge[at, :, width:] = aux
        window = between(lane, start, start + 4)
        ring_n = pltpu.roll(jnp.where(lane == 0, aux, main), (3 + start) % width, 1)
        ring_s = pltpu.roll(jnp.where(lane == width - 1, aux, main), (1 + start) % width, 1)
        pack_n = jnp.where(window, ring_n, pack_n)
        pack_s = jnp.where(window, ring_s, pack_s)
        if 0 <= x < cells_x:
            row = jnp.concatenate([cur[x], sea_row(mask, x, MASK_ROWS)], 0)
            cur_n = jnp.where(
                between(lane_f, start, start + 3), pltpu.roll(row, (3 + start) % width, 1), cur_n
            )
            cur_s = jnp.where(
                between(lane_f, start + 1, start + 4), pltpu.roll(row, (1 + start) % width, 1), cur_s
            )
    even = is_even("gy")
    for msg, north_first in ((msg_a, even), (msg_b, ~even)):
        msg[:chans] = jnp.where(north_first, pack_n, pack_s).astype(BF16)
        msg[chans : chans + fields] = jnp.where(north_first, cur_n, cur_s).astype(BF16)
    base = chans + fields
    for f in (f_own, f_oth):
        for cols in chunks_of(bins):
            high = [f[x, width - 16 :, cols].astype(F32)[15:] for x in range(cells_x)]
            low = [f[x, :16, cols].astype(F32)[:1] for x in range(cells_x)]
            high, low = jnp.concatenate(high, 0), jnp.concatenate(low, 0)
            msg_a[base : base + cells_x] = jnp.where(even, high, low).astype(BF16)
            msg_b[base : base + cells_x] = jnp.where(even, low, high).astype(BF16)
            base += cells_x


def is_even(axis):
    return lax.rem(lax.axis_index(axis), 2) == 0


def from_sides(from_a, from_b, rows):
    even = is_even("gy")
    a, b = from_a[rows].astype(F32), from_b[rows].astype(F32)
    return jnp.where(even, b, a), jnp.where(even, a, b)


def southern(tile, start, width):
    return pltpu.roll(tile, (-start - 3) % width, 1)


def northern(tile, start, width):
    return pltpu.roll(tile, (-start - 1) % width, 1)


def halo_lanes(lane, low, high, width):
    return jnp.where(lane >= width - 3, low, jnp.where(lane < 3, high, 0.0))


def stokes_row(main, aux, pack_s, pack_n, start, lane, width):
    low = southern(pack_s, start, width)
    high = northern(pack_n, start, width)
    main = main + jnp.where(lane == 0, low, 0.0) + jnp.where(lane == width - 1, high, 0.0)
    return main, aux + halo_lanes(lane, low, high, width)


def relay_kernel(cells_x, s_edge, from_a, from_b, side_w, side_e, msg_e, msg_w, spectra):
    rows = spectra.shape[0] // 2
    spectra[:rows] = side_w[:rows]
    spectra[rows:] = side_e[:rows]
    chans, width = s_edge.shape[1], s_edge.shape[2] // 2
    fields = chans + MASK_ROWS
    stride = width // (cells_x + 2)
    half = width // 2
    lane = lane_of(chans, width)
    lane_f = lane_of(fields, width)
    pack_s, pack_n = from_sides(from_a, from_b, slice(0, chans))
    cur_s, cur_n = from_sides(from_a, from_b, slice(chans, chans + fields))
    for msg, first, first_cur, first_edge in (
        (msg_e, cells_x - 2, cells_x - EDGE, EDGE),
        (msg_w, -1, 0, 0),
    ):
        tile = jnp.zeros((chans, width), F32)
        cur_tile = jnp.zeros((fields, width), F32)
        for i in range(EDGE):
            edge = s_edge[first_edge + i]
            start = stride * (first + i + 1)
            main, aux = stokes_row(
                edge[:, :width], edge[:, width:], pack_s, pack_n, start, lane, width
            )
            msg[i * chans : (i + 1) * chans] = main.astype(BF16)
            at = SLOT * i
            tile = jnp.where(between(lane, at, at + 6), pltpu.roll(aux, at + 3, 1), tile)
            x = first_cur + i
            ring = halo_lanes(
                lane_f,
                southern(cur_s, stride * (x + 1), width),
                northern(cur_n, stride * (x + 1), width),
                width,
            )
            at += half
            cur_tile = jnp.where(between(lane_f, at, at + 6), pltpu.roll(ring, at + 3, 1), cur_tile)
        base = EDGE * chans
        msg[base : base + chans] = (tile + cur_tile[:chans]).astype(BF16)
        msg[base + chans : base + fields] = cur_tile[chans:].astype(BF16)


def momentum_kernel(
    s_main, s_aux, currents, mask, side_w, side_e, from_a, from_b, from_w, from_e, token, drag, cor,
    out,
    cur, flow_a, flow_b, stokes, result, in_sem, sem,
):
    del token
    cells_x, chans, width = s_aux.shape
    fields = chans + MASK_ROWS
    levels = chans // 2
    stride = width // (cells_x + 2)
    half = width // 2
    lane = lane_of(chans, width)
    lane_f = lane_of(fields, width)
    copies = load_currents(currents, range(cells_x), cur, in_sem)
    for copy in copies:
        copy.start()

    side_base = side_w.shape[0] - EDGE * fields
    corner_w, corner_e = from_w[EDGE * chans :].astype(F32), from_e[EDGE * chans :].astype(F32)
    pack_s, pack_n = from_sides(from_a, from_b, slice(0, chans))
    cur_s, cur_n = from_sides(from_a, from_b, slice(chans, chans + fields))

    def corner(tile, at, lanes):
        ring = pltpu.roll(tile, (-at - 3) % width, 1)
        return halo_lanes(lanes, ring, ring, width)

    for x in range(-SUBSTEPS, cells_x + SUBSTEPS):
        if 0 <= x < cells_x:
            flow_a[x + SUBSTEPS, chans:, :width] = sea_row(mask, x, MASK_ROWS)
            aux = halo_lanes(
                lane_f,
                southern(cur_s, stride * (x + 1), width),
                northern(cur_n, stride * (x + 1), width),
                width,
            )
        else:
            side, tile, i = (side_w, corner_w, x + SUBSTEPS) if x < 0 else (side_e, corner_e, x - cells_x)
            at = side_base + i * fields
            flow_a[x + SUBSTEPS, :, :width] = side[at : at + fields].astype(F32)
            aux = corner(tile, half + SLOT * i, lane_f)
        flow_a[x + SUBSTEPS, :, width:] = aux

    margin = SUBSTEPS - 1
    for x in range(-margin, cells_x + margin):
        main = aux = 0.0
        if -1 <= x <= cells_x:
            own_aux = s_aux[x] if 0 <= x < cells_x else 0.0
            main, aux = stokes_row(
                s_main[x + 1], own_aux, pack_s, pack_n, stride * (x + 1), lane, width
            )
        for message, tile, first in ((from_w, corner_w, -2), (from_e, corner_e, cells_x - 1)):
            i = x - first
            if 0 <= i < EDGE:
                main += message[i * chans : (i + 1) * chans].astype(F32)
                aux += corner(tile[:chans], SLOT * i, lane)
        sea = flow_a[x + SUBSTEPS, chans : chans + 1, :]
        stokes[x + margin, :, :width] = main * sea[:, :width]
        stokes[x + margin, :, width:] = aux * sea[:, width:]

    for copy in copies:
        copy.wait()
    for x in range(cells_x):
        flow_a[x + SUBSTEPS, :chans, :width] = cur[x]
    at_level = lax.broadcasted_iota(jnp.int32, (levels, 1), 0)
    drag_col = jnp.zeros((levels, 1), F32)
    for level in range(levels):
        drag_col = jnp.where(at_level == level, drag[level], drag_col)
    half_cor = time_step * cor[...]
    keep = 1.0 - 4.0 * time_step * viscosity - time_step * drag_col
    ring = 2 * width
    source, target = flow_a, flow_b
    for step in range(SUBSTEPS):
        margin = SUBSTEPS - 1 - step
        last = step == SUBSTEPS - 1
        for x in range(-margin, cells_x + margin):
            at = x + SUBSTEPS
            u, v = source[at, :levels], source[at, levels:chans]
            u_w, v_w = source[at - 1, :levels], source[at - 1, levels:chans]
            u_e, v_e = source[at + 1, :levels], source[at + 1, levels:chans]
            u_s, v_s = pltpu.roll(u, 1, 1), pltpu.roll(v, 1, 1)
            u_n, v_n = pltpu.roll(u, ring - 1, 1), pltpu.roll(v, ring - 1, 1)
            drift = stokes[x + SUBSTEPS - 1]
            if last:
                u, v, u_w, v_w, u_e, v_e, u_s, v_s, u_n, v_n, drift = (
                    field[:, :width] for field in (u, v, u_w, v_w, u_e, v_e, u_s, v_s, u_n, v_n, drift)
                )
            lanes = u.shape[1]
            spin = half_cor[:, :lanes] + 0.5 * time_step * ((v_e - v_w) - (u_n - u_s))
            sea = flow_a[at, chans : chans + 1, :lanes]
            u_new = keep * u + spin * (v + drift[levels:])
            v_new = keep * v - spin * (u + drift[:levels])
            u_new = sea * (u_new + time_step * viscosity * ((u_e + u_w) + (u_n + u_s)))
            v_new = sea * (v_new + time_step * viscosity * ((v_e + v_w) + (v_n + v_s)))
            if last:
                result[x, :levels] = u_new
                result[x, levels:] = v_new
                for c in range(2):
                    pltpu.make_async_copy(
                        result.at[x, pl.ds(c * levels, levels), :], out.at[c, :, x, :], sem.at[c, x]
                    ).start()
            else:
                target[at, :levels] = u_new
                target[at, levels:chans] = v_new
        source, target = target, source
    for x in range(cells_x):
        for c in range(2):
            pltpu.make_async_copy(
                result.at[x, pl.ds(c * levels, levels), :], out.at[c, :, x, :], sem.at[c, x]
            ).wait()


def wave_kernel(
    f_own, f_oth, courant_own, courant_oth, mask, interaction,
    sides_own, sides_oth, from_a, from_b,
    out, token,
    adv, shifted, slots, out_sem,
):
    cells_x, width, bins = f_own.shape
    pairs = cells_x // 2
    core = lax.axis_index("comp")
    own_at, oth_at = pl.multiple_of(core * bins, bins), pl.multiple_of((1 - core) * bins, bins)
    base = from_a.shape[0] - 2 * bins // CHUNK * cells_x
    halves = []
    for rows, sides, courant in (
        (f_own, sides_own, courant_own),
        (f_oth, sides_oth, courant_oth),
    ):
        for j, cols in enumerate(chunks_of(bins)):
            cour_x, cour_y = courant[0:1, cols], courant[1:2, cols]
            size_x, size_y = jnp.abs(cour_x), jnp.abs(cour_y)
            halves.append(
                (
                    rows, sides, j, cols,
                    *from_sides(from_a, from_b, slice(base, base + cells_x)),
                    1.0 - size_x - size_y, size_x, size_y, cour_x > 0.0, cour_y > 0.0,
                )
            )
            base += cells_x

    token[...] = jnp.zeros_like(token)

    def sea_column(x):
        return jnp.transpose(sea_row(mask, x, CHUNK))

    def advect(pair):
        for i in range(2):
            x = 2 * pair + i
            sea = sea_column(x)
            for n, (rows, sides, j, cols, south, north, c_mid, c_x, c_y, up_x, up_y) in enumerate(halves):
                west = slice(j * width, (j + 1) * width)
                east = slice(bins // CHUNK * width + j * width, bins // CHUNK * width + (j + 1) * width)
                mid = rows[x, :, cols].astype(F32)
                west_cell = rows[x - 1, :, cols] if x else sides[west]
                east_cell = rows[x + 1, :, cols] if x < cells_x - 1 else sides[east]
                shifted[n, 8 : 8 + width] = mid
                shifted[n, 7:8] = south[x : x + 1]
                shifted[n, 8 + width : 9 + width] = north[x : x + 1]
                beside = jnp.where(up_x, west_cell.astype(F32), east_cell.astype(F32))
                along = jnp.where(up_y, shifted[n, 7 : 7 + width], shifted[n, 9 : 9 + width])
                value = c_mid * mid + c_x * beside + c_y * along
                adv[pair % 2, i * width : (i + 1) * width, n * CHUNK : (n + 1) * CHUNK] = (
                    value * sea
                ).astype(BF16)

    def copy_out(pair):
        return pltpu.make_async_copy(
            slots.at[pair % 2], out.at[pl.ds(2 * pair, 2)], out_sem.at[pair % 2]
        )

    def finish(pair):
        at = pair % 2
        gain = 0.0
        for half, owner_at in ((adv[at, :, :bins], own_at), (adv[at, :, bins:], oth_at)):
            block = interaction[pl.ds(owner_at, bins), pl.ds(own_at, bins)]
            gain += jnp.dot(half, block, preferred_element_type=F32)
        if pair >= 2:
            copy_out(pair - 2).wait()
        for i in range(2):
            sea = sea_column(2 * pair + i)
            rows = slice(i * width, (i + 1) * width)
            for cols in chunks_of(bins):
                total = adv[at, rows, cols].astype(F32) + gain[rows, cols]
                slots[at, i, :, cols] = (total * sea).astype(BF16)
        copy_out(pair).start()

    advect(0)
    for pair in range(1, pairs):
        advect(pair)
        finish(pair - 1)
    finish(pairs - 1)
    for pair in range(max(pairs - 2, 0), pairs):
        copy_out(pair).wait()


def lat_coriolis(cells_y):
    ny_total = lax.axis_size("gy") * cells_y
    lane = jnp.arange(2 * cells_y)
    lane = jnp.where(lane >= cells_y + cells_y // 2, lane - 2 * cells_y, lane)
    lat_index = lax.axis_index("gy") * cells_y + lane
    return jnp.sin(jnp.pi * ((lat_index.astype(F32) + 0.5) / ny_total - 0.5))[None, :]


VMEM = pl.BlockSpec(memory_space=pltpu.VMEM)
SMEM = pl.BlockSpec(memory_space=pltpu.SMEM)
HBM = pl.BlockSpec(memory_space=pltpu.HBM)
DMA = pltpu.SemaphoreType.DMA


def call(kernel, name, out_shape, in_specs, out_specs, scratch, flops, traffic, limit):
    return pl.pallas_call(
        kernel,
        out_shape=out_shape,
        in_specs=in_specs,
        out_specs=out_specs,
        scratch_shapes=scratch,
        compiler_params=pltpu.CompilerParams(vmem_limit_bytes=limit * MIB),
        cost_estimate=pl.CostEstimate(flops=flops, bytes_accessed=traffic, transcendentals=0),
        name=name,
    )


def local(spectrum, sea_mask, courant, interaction, stokes_proj, currents, level_drag):
    cells_x, cells_y, bins = spectrum.shape
    levels = currents.shape[1]
    chans = 2 * levels
    fields = chans + MASK_ROWS
    swap = [(0, 1), (1, 0)]
    east, west = ring("gx")

    def message(rows):
        return jax.ShapeDtypeStruct((rows, cells_y), BF16)

    f_oth = lax.ppermute(spectrum, "comp", swap)
    courant_oth = lax.ppermute(courant, "comp", swap)
    side_rows = bins // CHUNK * cells_y + EDGE * fields
    to_e, to_w = call(
        outgoing_kernel,
        "outgoing",
        (message(side_rows),) * 2,
        [HBM, HBM, VMEM],
        (VMEM,) * 2,
        [
            pltpu.VMEM((2 * EDGE, chans, cells_y), F32),
            DMA((2 * EDGE, 2)),
            DMA((2, bins // CHUNK)),
        ],
        10**6,
        MIB,
        52,
    )(spectrum, currents, sea_mask)
    west_own = lax.ppermute(to_e, "gx", east)
    east_own = lax.ppermute(to_w, "gx", west)

    edge_rows = chans + fields + 2 * bins // CHUNK * cells_x
    s_main, s_aux, s_edge, to_a, to_b = call(
        project_kernel,
        "project",
        (
            jax.ShapeDtypeStruct((cells_x + 2, chans, cells_y), F32),
            jax.ShapeDtypeStruct((cells_x, chans, cells_y), F32),
            jax.ShapeDtypeStruct((2 * EDGE, chans, 2 * cells_y), F32),
            message(edge_rows),
            message(edge_rows),
        ),
        [VMEM] * 5 + [HBM, VMEM],
        (VMEM,) * 5,
        [
            pltpu.VMEM((cells_x, PARTS * chans, cells_y), F32),
            pltpu.VMEM((PARTS * chans, bins), BF16),
            pltpu.VMEM((PARTS * chans, bins), BF16),
            pltpu.VMEM((cells_x, chans, cells_y), F32),
            DMA((cells_x, 2)),
        ],
        3 * 10**9,
        8 * MIB,
        10,
    )(
        spectrum, f_oth, courant, courant_oth, jnp.transpose(stokes_proj, (0, 2, 1)), currents, sea_mask
    )
    from_a = lax.ppermute(to_a, "gy", pairing("gy", 0))
    from_b = lax.ppermute(to_b, "gy", pairing("gy", 1))

    to_e, to_w, sides_own = call(
        functools.partial(relay_kernel, cells_x),
        "relay",
        (message(EDGE * chans + fields),) * 2 + (message(2 * bins // CHUNK * cells_y),),
        [VMEM] * 5,
        (VMEM,) * 3,
        [],
        10**6,
        MIB,
        4,
    )(s_edge, from_a, from_b, west_own, east_own)
    sides_oth = lax.ppermute(sides_own, "comp", swap)
    from_w = lax.ppermute(to_e, "gx", east)
    from_e = lax.ppermute(to_w, "gx", west)

    wave_out, token = call(
        wave_kernel,
        "wave",
        (jax.ShapeDtypeStruct(spectrum.shape, BF16), jax.ShapeDtypeStruct((8, CHUNK), F32)),
        [VMEM] * 10,
        (HBM, VMEM),
        [
            pltpu.VMEM((2, 2 * cells_y, 2 * bins), BF16),
            pltpu.VMEM((2 * bins // CHUNK, cells_y + 16, CHUNK), F32),
            pltpu.VMEM((2, 2, cells_y, bins), BF16),
            DMA((2,)),
        ],
        4 * 10**9,
        10 * MIB,
        8,
    )(
        spectrum, f_oth, courant, courant_oth, sea_mask, interaction,
        sides_own, sides_oth, from_a, from_b,
    )
    currents_out = call(
        momentum_kernel,
        "momentum",
        jax.ShapeDtypeStruct(currents.shape, F32),
        [VMEM] * 2 + [HBM] + [VMEM] * 8 + [SMEM, VMEM],
        HBM,
        [
            pltpu.VMEM((cells_x, chans, cells_y), F32),
            pltpu.VMEM((cells_x + 2 * SUBSTEPS, fields, 2 * cells_y), F32),
            pltpu.VMEM((cells_x + 2 * SUBSTEPS, chans, 2 * cells_y), F32),
            pltpu.VMEM((cells_x + 2 * SUBSTEPS - 2, chans, 2 * cells_y), F32),
            pltpu.VMEM((cells_x, chans, cells_y), F32),
            DMA((cells_x, 2)),
            DMA((2, cells_x)),
        ],
        10**8,
        4 * MIB,
        10,
    )(
        s_main, s_aux, currents, sea_mask, west_own, east_own, from_a, from_b, from_w, from_e, token,
        level_drag, lat_coriolis(cells_y),
    )
    return (wave_out, currents_out)


def solution(mesh):
    in_specs = (
        P("gx", "gy", "comp"),
        P("gx", "gy"),
        P(None, "comp"),
        P(),
        P(),
        P(None, "comp", "gx", "gy"),
        P("comp"),
    )
    out_specs = (P("gx", "gy", "comp"), P(None, "comp", "gx", "gy"))
    return jax.shard_map(local, mesh=mesh, in_specs=in_specs, out_specs=out_specs, check_vma=False)
```

time: 114 us -> 45.5 us (0.40)
  the two profiles are of different devices: /device:TPU:0 before, /device:TPU:5 now
where the time goes in v3:
time: 45.5 us; the launch traced here: 45.2 us
  Pallas kernels  20 us (44%)
  starting transfers between devices  13.2 us (29%)
  local copies, waits for them, and re-layouts  7.04 us (15%)
  waiting for transfers between devices  3.83 us (8%)
  between operations  1.01 us (2%)
    pallas_call x1, Pallas kernels, local(): call(wave_kernel, 'wave', (jax.ShapeDtypeStruct(spectrum.shape, BF16), ja...  9.12 us
    unnamed x32, local copies, waits for them, and re-layouts  7.04 us
    pallas_call x1, Pallas kernels, local(): call(momentum_kernel, 'momentum', jax.ShapeDtypeStruct(currents.shape, F3...  5.04 us
    pallas_call x1, Pallas kernels, local(): call(project_kernel, 'project', (jax.ShapeDtypeStruct((cells_x + 2, chans...  4.04 us
    ppermute x1, waiting for transfers between devices, local(): from_b = lax.ppermute(to_b, 'gy', pairing('gy', 1))  3.69 us
    ppermute x1, starting transfers between devices, local(): from_e = lax.ppermute(to_w, 'gx', west)  3.22 us
    ppermute x1, starting transfers between devices, local(): sides_oth = lax.ppermute(sides_own, 'comp', swap)  2.35 us
    ppermute x1, starting transfers between devices, local(): from_b = lax.ppermute(to_b, 'gy', pairing('gy', 1))  2.1 us
  transfers between devices with their start and end apart: 9, of which 2 were waited for; matrix products, arithmetic and copies ran while one was open for 0% of the time, Pallas kernels for 32%

profile of v3, /device:TPU:5, one launch (start us, length us, event | category | flops | bytes accessed | tf_op | source)
XLA Modules:
  0.0 45.2 jit_solution(208647091259629734)
XLA Ops:
  0.6 0.7 %collective-permute-start = (bf16[16,128,512]{2,1,0:T(8,128)(2,1)}, bf16[16,128,512]{2,1,0:T(8,128)(2,1)S(1)}, u32[]{:S(2)}, u32[]{:S(2)}) collective-permute-start(bf16[16,128,512]{2,1,0:T(8,128)(2,1)} %f_own.3), channel_id=1, source_target_pairs={{0,1},{1,0},{2,3},{3,2},{4,5},{5,4},{6,7},{7,6},{8,9},{9,8},{10,11... | collective-permute-start | bytes 6291464 | tf_op jit(solution)/shard_map/ppermute | solution.py:490
  1.4 0.1 collective-permute-start.1
  1.5 1.0 %copy-done.1 = f32[2,32,16,128]{3,2,1,0:T(8,128)S(1)} copy-done((f32[2,32,16,128]{3,2,1,0:T(8,128)S(1)}, f32[2,32,16,128]{3,2,1,0:T(8,128)}, u32[]{:S(2)}) %copy-start.1) | copy-done | bytes 524312
  2.5 0.7 %copy-done.5 = s32[16,128]{1,0:T(8,128)S(1)} copy-done((s32[16,128]{1,0:T(8,128)S(1)}, s32[16,128]{1,0:T(8,128)}, u32[]{:S(2)}) %copy-start.5) | copy-done | bytes 8216
  3.2 1.2 %outgoing.1 = (bf16[752,128]{1,0:T(8,128)(2,1)S(1)}, bf16[752,128]{1,0:T(8,128)(2,1)S(1)}) custom-call(bf16[16,128,512]{2,1,0:T(8,128)(2,1)} %f_own.3, f32[2,32,16,128]{3,2,1,0:T(8,128)S(1)} %copy-done.1, s32[16,128]{1,0:T(8,128)S(1)} %copy-done.5), custom_call_target="tpu_custom_call" | custom-call | flops 1000000 | bytes 1048576 | tf_op jit(solution)/shard_map/outgoing/pallas_call | solution.py:493
  4.4 1.3 %collective-permute-start.4 = (bf16[752,128]{1,0:T(8,128)(2,1)S(1)}, bf16[752,128]{1,0:T(8,128)(2,1)S(1)}, u32[]{:S(2)}, u32[]{:S(2)}) collective-permute-start(bf16[752,128]{1,0:T(8,128)(2,1)S(1)} %get-tuple-element.17), channel_id=1, source_target_pairs={{0,8},{8,16},{16,24},{24,0},{1,9},{9,17},{17,25},{25,1},{2,10},{10... | collective-permute-start | bytes 577544 | tf_op jit(solution)/shard_map/ppermute | solution.py:508
  5.8 2.1 %collective-permute-start.5 = (bf16[752,128]{1,0:T(8,128)(2,1)S(1)}, bf16[752,128]{1,0:T(8,128)(2,1)S(1)}, u32[]{:S(2)}, u32[]{:S(2)}) collective-permute-start(bf16[752,128]{1,0:T(8,128)(2,1)S(1)} %get-tuple-element.18), channel_id=1, source_target_pairs={{8,0},{16,8},{24,16},{0,24},{9,1},{17,9},{25,17},{1,25},{10,2},{18... | collective-permute-start | bytes 577544 | tf_op jit(solution)/shard_map/ppermute | solution.py:509
  7.9 0.0 collective-permute-done.1.courant_oth
  7.9 0.0 copy-start.9
  7.9 0.0 copy-start.6
  7.9 4.0 %project.1 = (f32[18,64,128]{2,1,0:T(8,128)S(1)}, f32[16,64,128]{2,1,0:T(8,128)S(1)}, f32[6,64,256]{2,1,0:T(8,128)S(1)}, bf16[272,128]{1,0:T(8,128)(2,1)S(1)}, bf16[272,128]{1,0:T(8,128)(2,1)S(1)}) custom-call(bf16[16,128,512]{2,1,0:T(8,128)(2,1)S(1)} %copy-done, bf16[16,128,512]{2,1,0:T(8,128)(2,1)S(1)} %collective-permute-done.f_oth, ...), custom_call_target="tpu_custom_call" | custom-call | flops 3000000000 | bytes 8388608 | tf_op jit(solution)/shard_map/project/pallas_call | solution.py:512
  12.0 0.0 copy-start.3
  12.0 0.8 %copy-done.3 = f32[16,64,128]{2,1,0:T(8,128)} copy-done((f32[16,64,128]{2,1,0:T(8,128)}, f32[16,64,128]{2,1,0:T(8,128)S(1)}, u32[]{:S(2)}) %copy-start.3) | copy-done | bytes 524312
  12.8 1.2 %collective-permute-start.2 = (bf16[272,128]{1,0:T(8,128)(2,1)S(1)}, bf16[272,128]{1,0:T(8,128)(2,1)S(1)}, u32[]{:S(2)}, u32[]{:S(2)}) collective-permute-start(bf16[272,128]{1,0:T(8,128)(2,1)S(1)} %get-tuple-element.15), channel_id=1, source_target_pairs={{0,2},{4,6},{2,0},{6,4},{1,3},{5,7},{3,1},{7,5},{8,10},{12,14},{10... | collective-permute-start | bytes 208904 | tf_op jit(solution)/shard_map/ppermute | solution.py:537
  14.0 2.1 %collective-permute-start.3 = (bf16[272,128]{1,0:T(8,128)(2,1)S(1)}, bf16[272,128]{1,0:T(8,128)(2,1)S(1)}, u32[]{:S(2)}, u32[]{:S(2)}) collective-permute-start(bf16[272,128]{1,0:T(8,128)(2,1)S(1)} %get-tuple-element.16), channel_id=1, source_target_pairs={{2,4},{4,2},{3,5},{5,3},{10,12},{12,10},{11,13},{13,11},{18,20},{2... | collective-permute-start | bytes 208904 | tf_op jit(solution)/shard_map/ppermute | solution.py:538
  16.1 0.0 collective-permute-done.4.side_w
  16.1 0.1 collective-permute-done.2.from_a
  16.2 3.7 %collective-permute-done.3.from_b = bf16[272,128]{1,0:T(8,128)(2,1)S(1)} collective-permute-done((bf16[272,128]{1,0:T(8,128)(2,1)S(1)}, bf16[272,128]{1,0:T(8,128)(2,1)S(1)}, u32[]{:S(2)}, u32[]{:S(2)}) %collective-permute-start.3) | collective-permute-done | bytes 69664 | tf_op jit(solution)/shard_map/ppermute | solution.py:538
  19.9 0.6 %relay.1 = (bf16[272,128]{1,0:T(8,128)(2,1)S(1)}, bf16[272,128]{1,0:T(8,128)(2,1)S(1)}, bf16[1024,128]{1,0:T(8,128)(2,1)S(1)}) custom-call(f32[6,64,256]{2,1,0:T(8,128)S(1)} %get-tuple-element.14.s_edge, bf16[272,128]{1,0:T(8,128)(2,1)S(1)} %collective-permute-done.2.from_a, bf16[272,128]{1,0:T(8,128)(2,1)S(1)} %collective-permute-done.3.from_b, ...), custom_call_target="tpu_custom_call" | custom-call | flops 1000000 | bytes 1048576 | tf_op jit(solution)/shard_map/relay/pallas_call | solution.py:540
  20.6 0.6 %copy-done.12 = bf16[272,128]{1,0:T(8,128)(2,1)} copy-done((bf16[272,128]{1,0:T(8,128)(2,1)}, bf16[272,128]{1,0:T(8,128)(2,1)S(1)}, u32[]{:S(2)}) %copy-start.12) | copy-done | bytes 69656
  21.2 2.3 %collective-permute-start.6 = (bf16[1024,128]{1,0:T(8,128)(2,1)S(1)}, bf16[1024,128]{1,0:T(8,128)(2,1)}, u32[]{:S(2)}, u32[]{:S(2)}) collective-permute-start(bf16[1024,128]{1,0:T(8,128)(2,1)S(1)} %get-tuple-element.19.sides_own), channel_id=1, source_target_pairs={{0,1},{1,0},{2,3},{3,2},{4,5},{5,4},{6,7},{7,6},{8,9},{9,8},{10,11... | collective-permute-start | bytes 786440 | tf_op jit(solution)/shard_map/ppermute | solution.py:551
  23.5 0.1 fusion.6.cor
  23.6 0.1 collective-permute-start.7
  23.7 0.0 copy-start.2
  23.7 0.0 copy-start.4
  23.7 0.0 copy-start.7
  23.7 3.2 %collective-permute-start.8 = (bf16[272,128]{1,0:T(8,128)(2,1)S(1)}, bf16[272,128]{1,0:T(8,128)(2,1)S(1)}, u32[]{:S(2)}, u32[]{:S(2)}) collective-permute-start(bf16[272,128]{1,0:T(8,128)(2,1)S(1)} %get-tuple-element.24), channel_id=1, source_target_pairs={{8,0},{16,8},{24,16},{0,24},{9,1},{17,9},{25,17},{1,25},{10,2},{18... | collective-permute-start | bytes 208904 | tf_op jit(solution)/shard_map/ppermute | solution.py:553
  26.9 1.6 %copy-done.8 = bf16[1024,1024]{1,0:T(8,128)(2,1)S(1)} copy-done((bf16[1024,1024]{1,0:T(8,128)(2,1)S(1)}, bf16[1024,1024]{1,0:T(8,128)(2,1)}, u32[]{:S(2)}) %copy-start.8) | copy-done | bytes 2097176
  28.5 1.6 %copy-done.10 = bf16[16,128,512]{2,1,0:T(8,128)(2,1)S(1)} copy-done((bf16[16,128,512]{2,1,0:T(8,128)(2,1)S(1)}, bf16[16,128,512]{2,1,0:T(8,128)(2,1)}, u32[]{:S(2)}) %copy-start.10) | copy-done | bytes 2097176
  30.1 0.7 %copy-done.15 = f32[2,512]{1,0:T(2,128)S(1)} copy-done((f32[2,512]{1,0:T(2,128)S(1)}, f32[2,512]{1,0:T(2,128)}, u32[]{:S(2)}) %copy-start.15) | copy-done | bytes 4120
  30.8 9.1 %wave.1 = (bf16[16,128,512]{2,1,0:T(8,128)(2,1)}, f32[8,128]{1,0:T(8,128)S(1)}) custom-call(bf16[16,128,512]{2,1,0:T(8,128)(2,1)S(1)} %copy-done, bf16[16,128,512]{2,1,0:T(8,128)(2,1)S(1)} %copy-done.10, f32[2,512]{1,0:T(2,128)S(1)} %copy-done.13, f32[2,512]{1,0:T(2,128)S(1)} %copy-done.15, s32[16,128]{1,0:T(8,128)S(1)} %copy-done.6, ...), custom_call_target="tpu_custom_call" | custom-call | flops 4000000000 | bytes 10485760 | tf_op jit(solution)/shard_map/wave/pallas_call | solution.py:555
  40.0 5.0 %momentum.1 = f32[2,32,16,128]{3,2,1,0:T(8,128)} custom-call(f32[18,64,128]{2,1,0:T(8,128)S(1)} %get-tuple-element.21.s_main, f32[16,64,128]{2,1,0:T(8,128)S(1)} %copy-done.4, f32[2,32,16,128]{3,2,1,0:T(8,128)S(1)} %copy-done.2, s32[16,128]{1,0:T(8,128)S(1)} %copy-done.6, bf16[752,128]{1,0:T(8,128)(2,1)S(1)} %collective-permute-done.4.side_w, ...), custom_call_target="tpu_custom_call" | custom-call | flops 100000000 | bytes 4194304 | tf_op jit(solution)/shard_map/momentum/pallas_call | solution.py:574
  (24 shorter events, 0.0 us)
Async XLA Ops:
  0.6 7.3 %copy-start = (bf16[16,128,512]{2,1,0:T(8,128)(2,1)S(1)}, bf16[16,128,512]{2,1,0:T(8,128)(2,1)}, u32[]{:S(2)}) copy-start(bf16[16,128,512]{2,1,0:T(8,128)(2,1)} %f_own.3) | copy-start | bytes 6291460
  0.6 7.2 %collective-permute-start = (bf16[16,128,512]{2,1,0:T(8,128)(2,1)}, bf16[16,128,512]{2,1,0:T(8,128)(2,1)S(1)}, u32[]{:S(2)}, u32[]{:S(2)}) collective-permute-start(bf16[16,128,512]{2,1,0:T(8,128)(2,1)} %f_own.3), channel_id=1, source_target_pairs={{0,1},{1,0},{2,3},{3,2},{4,5},{5,4},{6,7},{7,6},{8,9},{9,8},{10,11... | collective-permute-start | bytes 6291464 | tf_op jit(solution)/shard_map/ppermute | solution.py:490
  1.4 6.5 %collective-permute-start.1 = (f32[2,512]{1,0:T(2,128)}, f32[2,512]{1,0:T(2,128)S(1)}, u32[]{:S(2)}, u32[]{:S(2)}) collective-permute-start(f32[2,512]{1,0:T(2,128)} %courant_own.3), channel_id=1, source_target_pairs={{0,1},{1,0},{2,3},{3,2},{4,5},{5,4},{6,7},{7,6},{8,9},{9,8},{10,11... | collective-permute-start | bytes 12296 | tf_op jit(solution)/shard_map/ppermute | solution.py:491
  1.5 1.0 %copy-start.1 = (f32[2,32,16,128]{3,2,1,0:T(8,128)S(1)}, f32[2,32,16,128]{3,2,1,0:T(8,128)}, u32[]{:S(2)}) copy-start(f32[2,32,16,128]{3,2,1,0:T(8,128)} %currents.5) | copy-start | bytes 1572868
  2.5 0.7 %copy-start.5 = (s32[16,128]{1,0:T(8,128)S(1)}, s32[16,128]{1,0:T(8,128)}, u32[]{:S(2)}) copy-start(s32[16,128]{1,0:T(8,128)} %mask.7) | copy-start | bytes 24580
  3.2 4.7 %copy-start.11 = (bf16[2,1024,64]{1,2,0:T(8,128)(2,1)S(1)}, bf16[2,1024,64]{1,2,0:T(8,128)(2,1)}, u32[]{:S(2)}) copy-start(bf16[2,1024,64]{1,2,0:T(8,128)(2,1)} %param.11) | copy-start | bytes 786436
  3.2 4.7 %copy-start.13 = (f32[2,512]{1,0:T(2,128)S(1)}, f32[2,512]{1,0:T(2,128)}, u32[]{:S(2)}) copy-start(f32[2,512]{1,0:T(2,128)} %courant_own.3) | copy-start | bytes 12292
  4.4 11.7 %collective-permute-start.4 = (bf16[752,128]{1,0:T(8,128)(2,1)S(1)}, bf16[752,128]{1,0:T(8,128)(2,1)S(1)}, u32[]{:S(2)}, u32[]{:S(2)}) collective-permute-start(bf16[752,128]{1,0:T(8,128)(2,1)S(1)} %get-tuple-element.17), channel_id=1, source_target_pairs={{0,8},{8,16},{16,24},{24,0},{1,9},{9,17},{17,25},{25,1},{2,10},{10... | collective-permute-start | bytes 577544 | tf_op jit(solution)/shard_map/ppermute | solution.py:508
  5.8 10.3 %collective-permute-start.5 = (bf16[752,128]{1,0:T(8,128)(2,1)S(1)}, bf16[752,128]{1,0:T(8,128)(2,1)S(1)}, u32[]{:S(2)}, u32[]{:S(2)}) collective-permute-start(bf16[752,128]{1,0:T(8,128)(2,1)S(1)} %get-tuple-element.18), channel_id=1, source_target_pairs={{8,0},{16,8},{24,16},{0,24},{9,1},{17,9},{25,17},{1,25},{10,2},{18... | collective-permute-start | bytes 577544 | tf_op jit(solution)/shard_map/ppermute | solution.py:509
  7.9 4.1 %copy-start.14 = (f32[2,512]{1,0:T(2,128)}, f32[2,512]{1,0:T(2,128)S(1)}, u32[]{:S(2)}) copy-start(f32[2,512]{1,0:T(2,128)S(1)} %collective-permute-done.1.courant_oth) | copy-start | bytes 12292
  7.9 4.1 %copy-start.9 = (bf16[16,128,512]{2,1,0:T(8,128)(2,1)}, bf16[16,128,512]{2,1,0:T(8,128)(2,1)S(1)}, u32[]{:S(2)}) copy-start(bf16[16,128,512]{2,1,0:T(8,128)(2,1)S(1)} %collective-permute-done.f_oth) | copy-start | bytes 6291460
  7.9 19.0 %copy-start.6 = (s32[16,128]{1,0:T(8,128)S(1)}, s32[16,128]{1,0:T(8,128)}, u32[]{:S(2)}) copy-start(s32[16,128]{1,0:T(8,128)} %mask.7) | copy-start | bytes 24580
  12.0 0.8 %copy-start.3 = (f32[16,64,128]{2,1,0:T(8,128)}, f32[16,64,128]{2,1,0:T(8,128)S(1)}, u32[]{:S(2)}) copy-start(f32[16,64,128]{2,1,0:T(8,128)S(1)} %get-tuple-element.22.s_aux) | copy-start | bytes 1572868
  12.8 3.5 %collective-permute-start.2 = (bf16[272,128]{1,0:T(8,128)(2,1)S(1)}, bf16[272,128]{1,0:T(8,128)(2,1)S(1)}, u32[]{:S(2)}, u32[]{:S(2)}) collective-permute-start(bf16[272,128]{1,0:T(8,128)(2,1)S(1)} %get-tuple-element.15), channel_id=1, source_target_pairs={{0,2},{4,6},{2,0},{6,4},{1,3},{5,7},{3,1},{7,5},{8,10},{12,14},{10... | collective-permute-start | bytes 208904 | tf_op jit(solution)/shard_map/ppermute | solution.py:537
  14.0 5.9 %collective-permute-start.3 = (bf16[272,128]{1,0:T(8,128)(2,1)S(1)}, bf16[272,128]{1,0:T(8,128)(2,1)S(1)}, u32[]{:S(2)}, u32[]{:S(2)}) collective-permute-start(bf16[272,128]{1,0:T(8,128)(2,1)S(1)} %get-tuple-element.16), channel_id=1, source_target_pairs={{2,4},{4,2},{3,5},{5,3},{10,12},{12,10},{11,13},{13,11},{18,20},{2... | collective-permute-start | bytes 208904 | tf_op jit(solution)/shard_map/ppermute | solution.py:538
  20.6 0.6 %copy-start.12 = (bf16[272,128]{1,0:T(8,128)(2,1)}, bf16[272,128]{1,0:T(8,128)(2,1)S(1)}, u32[]{:S(2)}) copy-start(bf16[272,128]{1,0:T(8,128)(2,1)S(1)} %get-tuple-element.23) | copy-start | bytes 208900
  21.2 5.7 %collective-permute-start.6 = (bf16[1024,128]{1,0:T(8,128)(2,1)S(1)}, bf16[1024,128]{1,0:T(8,128)(2,1)}, u32[]{:S(2)}, u32[]{:S(2)}) collective-permute-start(bf16[1024,128]{1,0:T(8,128)(2,1)S(1)} %get-tuple-element.19.sides_own), channel_id=1, source_target_pairs={{0,1},{1,0},{2,3},{3,2},{4,5},{5,4},{6,7},{7,6},{8,9},{9,8},{10,11... | collective-permute-start | bytes 786440 | tf_op jit(solution)/shard_map/ppermute | solution.py:551
  23.6 16.3 %collective-permute-start.7 = (bf16[272,128]{1,0:T(8,128)(2,1)}, bf16[272,128]{1,0:T(8,128)(2,1)S(1)}, u32[]{:S(2)}, u32[]{:S(2)}) collective-permute-start(bf16[272,128]{1,0:T(8,128)(2,1)} %copy-done.12), channel_id=1, source_target_pairs={{0,8},{8,16},{16,24},{24,0},{1,9},{9,17},{17,25},{25,1},{2,10},{10... | collective-permute-start | bytes 208904 | tf_op jit(solution)/shard_map/ppermute | solution.py:552
  23.7 16.3 %copy-start.2 = (f32[2,32,16,128]{3,2,1,0:T(8,128)S(1)}, f32[2,32,16,128]{3,2,1,0:T(8,128)}, u32[]{:S(2)}) copy-start(f32[2,32,16,128]{3,2,1,0:T(8,128)} %currents.5) | copy-start | bytes 1572868
  23.7 16.3 %copy-start.4 = (f32[16,64,128]{2,1,0:T(8,128)S(1)}, f32[16,64,128]{2,1,0:T(8,128)}, u32[]{:S(2)}) copy-start(f32[16,64,128]{2,1,0:T(8,128)} %copy-done.3) | copy-start | bytes 1572868
  23.7 16.3 %copy-start.7 = (f32[32]{0:T(128)S(1)}, f32[32]{0:T(128)}, u32[]{:S(2)}) copy-start(f32[32]{0:T(128)} %drag.1) | copy-start | bytes 388
  23.7 16.2 %collective-permute-start.8 = (bf16[272,128]{1,0:T(8,128)(2,1)S(1)}, bf16[272,128]{1,0:T(8,128)(2,1)S(1)}, u32[]{:S(2)}, u32[]{:S(2)}) collective-permute-start(bf16[272,128]{1,0:T(8,128)(2,1)S(1)} %get-tuple-element.24), channel_id=1, source_target_pairs={{8,0},{16,8},{24,16},{0,24},{9,1},{17,9},{25,17},{1,25},{10,2},{18... | collective-permute-start | bytes 208904 | tf_op jit(solution)/shard_map/ppermute | solution.py:553
  26.9 1.6 %copy-start.8 = (bf16[1024,1024]{1,0:T(8,128)(2,1)S(1)}, bf16[1024,1024]{1,0:T(8,128)(2,1)}, u32[]{:S(2)}) copy-start(bf16[1024,1024]{1,0:T(8,128)(2,1)} %interaction.1) | copy-start | bytes 6291460
  28.5 1.6 %copy-start.10 = (bf16[16,128,512]{2,1,0:T(8,128)(2,1)S(1)}, bf16[16,128,512]{2,1,0:T(8,128)(2,1)}, u32[]{:S(2)}) copy-start(bf16[16,128,512]{2,1,0:T(8,128)(2,1)} %copy-done.9) | copy-start | bytes 6291460
  30.1 0.7 %copy-start.15 = (f32[2,512]{1,0:T(2,128)S(1)}, f32[2,512]{1,0:T(2,128)}, u32[]{:S(2)}) copy-start(f32[2,512]{1,0:T(2,128)} %copy-done.14) | copy-start | bytes 12292

commit v4 on v3

--- a/solution.py
+++ b/solution.py
@@ -60,12 +60,20 @@
     return jnp.broadcast_to(mask[x : x + 1, :].astype(F32), (rows, mask.shape[1]))
 
 
-def outgoing_kernel(spectrum, currents, mask, msg_e, msg_w, cur, sem, row_sem):
+def outgoing_kernel(
+    spectrum, currents, mask_in, proj_in,
+    msg_e, msg_w, proj,
+    cur, mask, sem, row_sem,
+):
     cells_x, width, bins = spectrum.shape
-    chans = cur.shape[1]
+    levels = cur.shape[1]
+    chans = 2 * levels
     fields = chans + MASK_ROWS
-    rows = list(range(EDGE)) + list(range(cells_x - EDGE, cells_x))
-    copies = load_currents(currents, rows, cur, sem)
+    copies = [
+        pltpu.make_async_copy(currents, cur, sem.at[0]),
+        pltpu.make_async_copy(mask_in, mask, sem.at[1]),
+    ]
+    proj_copy = pltpu.make_async_copy(proj_in, proj, sem.at[2])
     for side, (msg, x) in enumerate(((msg_e, cells_x - 1), (msg_w, 0))):
         for j, cols in enumerate(chunks_of(bins)):
             copies.append(
@@ -73,16 +81,20 @@
                     spectrum.at[x, :, cols], msg.at[pl.ds(j * width, width), :], row_sem.at[side, j]
                 )
             )
-    for copy in copies:
+    for copy in (*copies, proj_copy):
         copy.start()
-    for copy in copies:
+    copies[0].wait()
+    copies[1].wait()
+    base = bins // CHUNK * width
+    for msg, first in ((msg_e, cells_x - EDGE), (msg_w, 0)):
+        for i in range(EDGE):
+            x = first + i
+            at = base + i * fields
+            for c in range(2):
+                msg[at + c * levels : at + (c + 1) * levels] = cur[c, :, x, :].astype(BF16)
+            msg[at + chans : at + fields] = sea_row(mask, x, MASK_ROWS).astype(BF16)
+    for copy in (*copies[2:], proj_copy):
         copy.wait()
-    base = bins // CHUNK * width
-    for i, x in enumerate(rows):
-        msg = msg_w if i < EDGE else msg_e
-        at = base + i % EDGE * fields
-        msg[at : at + chans] = cur[i].astype(BF16)
-        msg[at + chans : at + fields] = sea_row(mask, x, MASK_ROWS).astype(BF16)
 
 
 def stokes_weights(proj, courant, core, owner, weights):
@@ -112,7 +124,6 @@
     cells_x, width, bins = f_own.shape
     chans = s_main.shape[1]
     fields = chans + MASK_ROWS
-    stride = width // (cells_x + 2)
     core = lax.axis_index("comp")
     copies = load_currents(currents, range(cells_x), cur, sem)
     for copy in copies:
@@ -139,7 +150,7 @@
     pack_n = pack_s = jnp.zeros((chans, width), F32)
     cur_n = cur_s = jnp.zeros((fields, width), F32)
     for x in range(-1, cells_x + 1):
-        start = stride * (x + 1)
+        start = stokes_lane(x)
         main = jnp.zeros((chans, width), F32)
         aux = jnp.zeros((chans, width), F32)
         if 0 <= x < cells_x:
@@ -164,25 +175,22 @@
         pack_s = jnp.where(window, ring_s, pack_s)
         if 0 <= x < cells_x:
             row = jnp.concatenate([cur[x], sea_row(mask, x, MASK_ROWS)], 0)
-            cur_n = jnp.where(
-                between(lane_f, start, start + 3), pltpu.roll(row, (3 + start) % width, 1), cur_n
-            )
-            cur_s = jnp.where(
-                between(lane_f, start + 1, start + 4), pltpu.roll(row, (1 + start) % width, 1), cur_s
-            )
+            start = current_lane(x, cells_x)
+            window = between(lane_f, start, start + 3)
+            cur_n = jnp.where(window, pltpu.roll(row, (3 + start) % width, 1), cur_n)
+            cur_s = jnp.where(window, pltpu.roll(row, start, 1), cur_s)
     even = is_even("gy")
     for msg, north_first in ((msg_a, even), (msg_b, ~even)):
-        msg[:chans] = jnp.where(north_first, pack_n, pack_s).astype(BF16)
-        msg[chans : chans + fields] = jnp.where(north_first, cur_n, cur_s).astype(BF16)
-    base = chans + fields
-    for f in (f_own, f_oth):
-        for cols in chunks_of(bins):
-            high = [f[x, width - 16 :, cols].astype(F32)[15:] for x in range(cells_x)]
-            low = [f[x, :16, cols].astype(F32)[:1] for x in range(cells_x)]
-            high, low = jnp.concatenate(high, 0), jnp.concatenate(low, 0)
-            msg_a[base : base + cells_x] = jnp.where(even, high, low).astype(BF16)
-            msg_b[base : base + cells_x] = jnp.where(even, low, high).astype(BF16)
-            base += cells_x
+        pack, cur_pack = jnp.where(north_first, pack_n, pack_s), jnp.where(north_first, cur_n, cur_s)
+        msg[:chans] = (pack + cur_pack[:chans]).astype(BF16)
+        msg[chans:fields] = cur_pack[chans:].astype(BF16)
+    for j, cols in enumerate(chunks_of(bins)):
+        high = [f_own[x, width - 16 :, cols].astype(F32)[15:] for x in range(cells_x)]
+        low = [f_own[x, :16, cols].astype(F32)[:1] for x in range(cells_x)]
+        high, low = jnp.concatenate(high, 0), jnp.concatenate(low, 0)
+        base = fields + j * cells_x
+        msg_a[base : base + cells_x] = jnp.where(even, high, low).astype(BF16)
+        msg_b[base : base + cells_x] = jnp.where(even, low, high).astype(BF16)
 
 
 def is_even(axis):
@@ -193,6 +201,20 @@
     even = is_even("gy")
     a, b = from_a[rows].astype(F32), from_b[rows].astype(F32)
     return jnp.where(even, b, a), jnp.where(even, a, b)
+
+
+def stokes_lane(x):
+    return 4 * (x + 1)
+
+
+def current_lane(x, cells_x):
+    return 4 * (cells_x + 2) + 3 * x
+
+
+def current_halo(tile_s, tile_n, x, cells_x, lane, width):
+    start = current_lane(x, cells_x)
+    low = pltpu.roll(tile_s, (-start - 3) % width, 1)
+    return halo_lanes(lane, low, pltpu.roll(tile_n, (-start) % width, 1), width)
 
 
 def southern(tile, start, width):
@@ -215,17 +237,17 @@
 
 
 def relay_kernel(cells_x, s_edge, from_a, from_b, side_w, side_e, msg_e, msg_w, spectra):
-    rows = spectra.shape[0] // 2
-    spectra[:rows] = side_w[:rows]
-    spectra[rows:] = side_e[:rows]
     chans, width = s_edge.shape[1], s_edge.shape[2] // 2
     fields = chans + MASK_ROWS
-    stride = width // (cells_x + 2)
+    rows, edges = side_w.shape[0] - EDGE * fields, from_a.shape[0] - fields
+    spectra[:rows] = side_w[:rows]
+    spectra[rows : 2 * rows] = side_e[:rows]
+    spectra[2 * rows : 2 * rows + edges] = from_a[fields:]
+    spectra[2 * rows + edges :] = from_b[fields:]
     half = width // 2
     lane = lane_of(chans, width)
     lane_f = lane_of(fields, width)
-    pack_s, pack_n = from_sides(from_a, from_b, slice(0, chans))
-    cur_s, cur_n = from_sides(from_a, from_b, slice(chans, chans + fields))
+    tile_s, tile_n = from_sides(from_a, from_b, slice(0, fields))
     for msg, first, first_cur, first_edge in (
         (msg_e, cells_x - 2, cells_x - EDGE, EDGE),
         (msg_w, -1, 0, 0),
@@ -234,20 +256,14 @@
         cur_tile = jnp.zeros((fields, width), F32)
         for i in range(EDGE):
             edge = s_edge[first_edge + i]
-            start = stride * (first + i + 1)
+            start = stokes_lane(first + i)
             main, aux = stokes_row(
-                edge[:, :width], edge[:, width:], pack_s, pack_n, start, lane, width
+                edge[:, :width], edge[:, width:], tile_s[:chans], tile_n[:chans], start, lane, width
             )
             msg[i * chans : (i + 1) * chans] = main.astype(BF16)
             at = SLOT * i
             tile = jnp.where(between(lane, at, at + 6), pltpu.roll(aux, at + 3, 1), tile)
-            x = first_cur + i
-            ring = halo_lanes(
-                lane_f,
-                southern(cur_s, stride * (x + 1), width),
-                northern(cur_n, stride * (x + 1), width),
-                width,
-            )
+            ring = current_halo(tile_s, tile_n, first_cur + i, cells_x, lane_f, width)
             at += half
             cur_tile = jnp.where(between(lane_f, at, at + 6), pltpu.roll(ring, at + 3, 1), cur_tile)
         base = EDGE * chans
@@ -255,41 +271,44 @@
         msg[base + chans : base + fields] = cur_tile[chans:].astype(BF16)
 
 
+def lat_coriolis(cells_y):
+    ny_total = lax.axis_size("gy") * cells_y
+    lane = lane_of(1, 2 * cells_y)
+    lane = jnp.where(lane >= cells_y + cells_y // 2, lane - 2 * cells_y, lane)
+    lat_index = lax.axis_index("gy") * cells_y + lane
+    return jnp.sin(jnp.pi * ((lat_index.astype(F32) + 0.5) / ny_total - 0.5))
+
+
 def momentum_kernel(
-    s_main, s_aux, currents, mask, side_w, side_e, from_a, from_b, from_w, from_e, token, drag, cor,
+    s_main, s_aux, currents, mask_in, side_w, side_e, from_a, from_b, from_w, from_e, token, drag,
     out,
-    cur, flow_a, flow_b, stokes, result, in_sem, sem,
+    cur, mask, flow_a, flow_b, stokes, result, mask_sem, in_sem, sem,
 ):
     del token
     cells_x, chans, width = s_aux.shape
     fields = chans + MASK_ROWS
     levels = chans // 2
-    stride = width // (cells_x + 2)
     half = width // 2
     lane = lane_of(chans, width)
     lane_f = lane_of(fields, width)
     copies = load_currents(currents, range(cells_x), cur, in_sem)
-    for copy in copies:
+    mask_copy = pltpu.make_async_copy(mask_in, mask, mask_sem)
+    for copy in (mask_copy, *copies):
         copy.start()
 
     side_base = side_w.shape[0] - EDGE * fields
     corner_w, corner_e = from_w[EDGE * chans :].astype(F32), from_e[EDGE * chans :].astype(F32)
-    pack_s, pack_n = from_sides(from_a, from_b, slice(0, chans))
-    cur_s, cur_n = from_sides(from_a, from_b, slice(chans, chans + fields))
+    tile_s, tile_n = from_sides(from_a, from_b, slice(0, fields))
 
     def corner(tile, at, lanes):
         ring = pltpu.roll(tile, (-at - 3) % width, 1)
         return halo_lanes(lanes, ring, ring, width)
 
+    mask_copy.wait()
     for x in range(-SUBSTEPS, cells_x + SUBSTEPS):
         if 0 <= x < cells_x:
             flow_a[x + SUBSTEPS, chans:, :width] = sea_row(mask, x, MASK_ROWS)
-            aux = halo_lanes(
-                lane_f,
-                southern(cur_s, stride * (x + 1), width),
-                northern(cur_n, stride * (x + 1), width),
-                width,
-            )
+            aux = current_halo(tile_s, tile_n, x, cells_x, lane_f, width)
         else:
             side, tile, i = (side_w, corner_w, x + SUBSTEPS) if x < 0 else (side_e, corner_e, x - cells_x)
             at = side_base + i * fields
@@ -303,7 +322,7 @@
         if -1 <= x <= cells_x:
             own_aux = s_aux[x] if 0 <= x < cells_x else 0.0
             main, aux = stokes_row(
-                s_main[x + 1], own_aux, pack_s, pack_n, stride * (x + 1), lane, width
+                s_main[x + 1], own_aux, tile_s[:chans], tile_n[:chans], stokes_lane(x), lane, width
             )
         for message, tile, first in ((from_w, corner_w, -2), (from_e, corner_e, cells_x - 1)):
             i = x - first
@@ -322,7 +341,7 @@
     drag_col = jnp.zeros((levels, 1), F32)
     for level in range(levels):
         drag_col = jnp.where(at_level == level, drag[level], drag_col)
-    half_cor = time_step * cor[...]
+    half_cor = time_step * lat_coriolis(width)
     keep = 1.0 - 4.0 * time_step * viscosity - time_step * drag_col
     ring = 2 * width
     source, target = flow_a, flow_b
@@ -367,100 +386,123 @@
 
 
 def wave_kernel(
-    f_own, f_oth, courant_own, courant_oth, mask, interaction,
-    sides_own, sides_oth, from_a, from_b,
+    rows_own, rows_oth, courant_own, courant_oth, mask, interaction,
+    sides_own, sides_oth,
     out, token,
-    adv, shifted, slots, out_sem,
+    inter, adv_a, adv_b, shifted, slots, inter_sem, out_sem,
 ):
-    cells_x, width, bins = f_own.shape
+    cells_x, width, bins = rows_own.shape
     pairs = cells_x // 2
     core = lax.axis_index("comp")
     own_at, oth_at = pl.multiple_of(core * bins, bins), pl.multiple_of((1 - core) * bins, bins)
-    base = from_a.shape[0] - 2 * bins // CHUNK * cells_x
+    inter_copies = [
+        pltpu.make_async_copy(
+            interaction.at[pl.ds(at, bins), pl.ds(own_at, bins)],
+            inter.at[pl.ds(n * bins, bins)],
+            inter_sem.at[n],
+        )
+        for n, at in enumerate((own_at, oth_at))
+    ]
+    for copy in inter_copies:
+        copy.start()
+
+    even = is_even("gy")
     halves = []
     for rows, sides, courant in (
-        (f_own, sides_own, courant_own),
-        (f_oth, sides_oth, courant_oth),
+        (rows_own, sides_own, courant_own),
+        (rows_oth, sides_oth, courant_oth),
     ):
         for j, cols in enumerate(chunks_of(bins)):
             cour_x, cour_y = courant[0:1, cols], courant[1:2, cols]
             size_x, size_y = jnp.abs(cour_x), jnp.abs(cour_y)
+            base = bins // CHUNK * 2 * width + j * cells_x
+            edge_a = sides[base : base + cells_x].astype(F32)
+            base += bins // CHUNK * cells_x
+            edge_b = sides[base : base + cells_x].astype(F32)
             halves.append(
                 (
-                    rows, sides, j, cols,
-                    *from_sides(from_a, from_b, slice(base, base + cells_x)),
+                    rows, sides, j, cols, jnp.where(even, edge_b, edge_a), jnp.where(even, edge_a, edge_b),
                     1.0 - size_x - size_y, size_x, size_y, cour_x > 0.0, cour_y > 0.0,
                 )
             )
-            base += cells_x
 
     token[...] = jnp.zeros_like(token)
 
     def sea_column(x):
         return jnp.transpose(sea_row(mask, x, CHUNK))
 
-    def advect(pair):
+    adv = (adv_a, adv_b)
+
+    def advect(pair, n):
+        rows, sides, j, cols, south, north, c_mid, c_x, c_y, up_x, up_y = halves[n]
+        first = 2 * pair
+        cells = []
+        for x in range(first - 1, first + 3):
+            if x < 0:
+                cells.append(sides[j * width : (j + 1) * width].astype(F32))
+            elif x == cells_x:
+                base = bins // CHUNK * width
+                cells.append(sides[base + j * width : base + (j + 1) * width].astype(F32))
+            else:
+                cells.append(rows[x, :, cols].astype(F32))
         for i in range(2):
-            x = 2 * pair + i
-            sea = sea_column(x)
-            for n, (rows, sides, j, cols, south, north, c_mid, c_x, c_y, up_x, up_y) in enumerate(halves):
-                west = slice(j * width, (j + 1) * width)
-                east = slice(bins // CHUNK * width + j * width, bins // CHUNK * width + (j + 1) * width)
-                mid = rows[x, :, cols].astype(F32)
-                west_cell = rows[x - 1, :, cols] if x else sides[west]
-                east_cell = rows[x + 1, :, cols] if x < cells_x - 1 else sides[east]
-                shifted[n, 8 : 8 + width] = mid
-                shifted[n, 7:8] = south[x : x + 1]
-                shifted[n, 8 + width : 9 + width] = north[x : x + 1]
-                beside = jnp.where(up_x, west_cell.astype(F32), east_cell.astype(F32))
-                along = jnp.where(up_y, shifted[n, 7 : 7 + width], shifted[n, 9 : 9 + width])
-                value = c_mid * mid + c_x * beside + c_y * along
-                adv[pair % 2, i * width : (i + 1) * width, n * CHUNK : (n + 1) * CHUNK] = (
-                    value * sea
-                ).astype(BF16)
+            x = first + i
+            mid = cells[i + 1]
+            moved = shifted.at[2 * n + i]
+            moved[8 : 8 + width] = mid
+            moved[7:8] = south[x : x + 1]
+            moved[8 + width : 9 + width] = north[x : x + 1]
+            low, high = moved[7 : 7 + width], moved[9 : 9 + width]
+            beside = jnp.where(up_x, cells[i], cells[i + 2])
+            value = c_mid * mid + c_x * beside + c_y * jnp.where(up_y, low, high)
+            adv[pair % 2][i * width : (i + 1) * width, n * CHUNK : (n + 1) * CHUNK] = value.astype(BF16)
 
     def copy_out(pair):
         return pltpu.make_async_copy(
-            slots.at[pair % 2], out.at[pl.ds(2 * pair, 2)], out_sem.at[pair % 2]
+            slots.at[pl.ds(2 * pair, 2)], out.at[pl.ds(2 * pair, 2)], out_sem.at[pair]
         )
 
-    def finish(pair):
-        at = pair % 2
-        gain = 0.0
-        for half, owner_at in ((adv[at, :, :bins], own_at), (adv[at, :, bins:], oth_at)):
-            block = interaction[pl.ds(owner_at, bins), pl.ds(own_at, bins)]
-            gain += jnp.dot(half, block, preferred_element_type=F32)
-        if pair >= 2:
-            copy_out(pair - 2).wait()
-        for i in range(2):
-            sea = sea_column(2 * pair + i)
-            rows = slice(i * width, (i + 1) * width)
-            for cols in chunks_of(bins):
-                total = adv[at, rows, cols].astype(F32) + gain[rows, cols]
-                slots[at, i, :, cols] = (total * sea).astype(BF16)
-        copy_out(pair).start()
-
-    advect(0)
-    for pair in range(1, pairs):
-        advect(pair)
-        finish(pair - 1)
-    finish(pairs - 1)
-    for pair in range(max(pairs - 2, 0), pairs):
+    def finish(pair, seas, piece):
+        done = adv[pair % 2]
+        i, block = piece // blocks, piece % blocks
+        rows = slice(i * width, (i + 1) * width)
+        cols = slice(block * bins // blocks, (block + 1) * bins // blocks)
+        gain = jnp.dot(done[rows, :], inter[:, cols], preferred_element_type=F32)
+        for c in chunks_of(bins // blocks):
+            own = slice(cols.start + c.start, cols.start + c.stop)
+            total = done[rows, own].astype(F32) + gain[:, c]
+            slots[2 * pair + i, :, own] = (total * seas[i]).astype(BF16)
+
+    def both_seas(pair):
+        return [sea_column(2 * pair + i) for i in range(2)]
+
+    blocks = 2
+    pieces = 2 * blocks
+    parts = len(halves)
+    for n in range(parts):
+        advect(0, n)
+    for copy in inter_copies:
+        copy.wait()
+    for pair in range(1, pairs + 1):
+        seas = both_seas(pair - 1)
+        for piece in range(pieces):
+            if pair < pairs:
+                for n in range(piece * parts // pieces, (piece + 1) * parts // pieces):
+                    advect(pair, n)
+            finish(pair - 1, seas, piece)
+        copy_out(pair - 1).start()
+    for pair in range(pairs):
         copy_out(pair).wait()
-
-
-def lat_coriolis(cells_y):
-    ny_total = lax.axis_size("gy") * cells_y
-    lane = jnp.arange(2 * cells_y)
-    lane = jnp.where(lane >= cells_y + cells_y // 2, lane - 2 * cells_y, lane)
-    lat_index = lax.axis_index("gy") * cells_y + lane
-    return jnp.sin(jnp.pi * ((lat_index.astype(F32) + 0.5) / ny_total - 0.5))[None, :]
 
 
 VMEM = pl.BlockSpec(memory_space=pltpu.VMEM)
 SMEM = pl.BlockSpec(memory_space=pltpu.SMEM)
 HBM = pl.BlockSpec(memory_space=pltpu.HBM)
 DMA = pltpu.SemaphoreType.DMA
+
+
+def in_hbm(array):
+    return pltpu.with_memory_space_constraint(array, pltpu.HBM)
 
 
 def call(kernel, name, out_shape, in_specs, out_specs, scratch, flops, traffic, limit):
@@ -489,26 +531,28 @@
 
     f_oth = lax.ppermute(spectrum, "comp", swap)
     courant_oth = lax.ppermute(courant, "comp", swap)
+    stokes_proj = jnp.transpose(stokes_proj, (0, 2, 1))
     side_rows = bins // CHUNK * cells_y + EDGE * fields
-    to_e, to_w = call(
+    to_e, to_w, stokes_proj = call(
         outgoing_kernel,
         "outgoing",
-        (message(side_rows),) * 2,
-        [HBM, HBM, VMEM],
-        (VMEM,) * 2,
+        (message(side_rows),) * 2 + (jax.ShapeDtypeStruct(stokes_proj.shape, BF16),),
+        [HBM] * 4,
+        (VMEM,) * 3,
         [
-            pltpu.VMEM((2 * EDGE, chans, cells_y), F32),
-            DMA((2 * EDGE, 2)),
+            pltpu.VMEM(currents.shape, F32),
+            pltpu.VMEM(sea_mask.shape, jnp.int32),
+            DMA((3,)),
             DMA((2, bins // CHUNK)),
         ],
         10**6,
         MIB,
-        52,
-    )(spectrum, currents, sea_mask)
+        4,
+    )(in_hbm(spectrum), in_hbm(currents), in_hbm(sea_mask), in_hbm(stokes_proj))
     west_own = lax.ppermute(to_e, "gx", east)
     east_own = lax.ppermute(to_w, "gx", west)
 
-    edge_rows = chans + fields + 2 * bins // CHUNK * cells_x
+    edge_rows = fields + bins // CHUNK * cells_x
     s_main, s_aux, s_edge, to_a, to_b = call(
         project_kernel,
         "project",
@@ -519,7 +563,7 @@
             message(edge_rows),
             message(edge_rows),
         ),
-        [VMEM] * 5 + [HBM, VMEM],
+        [VMEM] * 7,
         (VMEM,) * 5,
         [
             pltpu.VMEM((cells_x, PARTS * chans, cells_y), F32),
@@ -530,9 +574,9 @@
         ],
         3 * 10**9,
         8 * MIB,
-        10,
+        8,
     )(
-        spectrum, f_oth, courant, courant_oth, jnp.transpose(stokes_proj, (0, 2, 1)), currents, sea_mask
+        spectrum, f_oth, courant, courant_oth, stokes_proj, currents, sea_mask
     )
     from_a = lax.ppermute(to_a, "gy", pairing("gy", 0))
     from_b = lax.ppermute(to_b, "gy", pairing("gy", 1))
@@ -540,7 +584,8 @@
     to_e, to_w, sides_own = call(
         functools.partial(relay_kernel, cells_x),
         "relay",
-        (message(EDGE * chans + fields),) * 2 + (message(2 * bins // CHUNK * cells_y),),
+        (message(EDGE * chans + fields),) * 2
+        + (message(2 * bins // CHUNK * (cells_y + cells_x)),),
         [VMEM] * 5,
         (VMEM,) * 3,
         [],
@@ -556,33 +601,38 @@
         wave_kernel,
         "wave",
         (jax.ShapeDtypeStruct(spectrum.shape, BF16), jax.ShapeDtypeStruct((8, CHUNK), F32)),
-        [VMEM] * 10,
+        [VMEM] * 5 + [HBM] + [VMEM] * 2,
         (HBM, VMEM),
         [
-            pltpu.VMEM((2, 2 * cells_y, 2 * bins), BF16),
-            pltpu.VMEM((2 * bins // CHUNK, cells_y + 16, CHUNK), F32),
-            pltpu.VMEM((2, 2, cells_y, bins), BF16),
+            pltpu.VMEM((2 * bins, bins), BF16),
+            pltpu.VMEM((2 * cells_y, 2 * bins), BF16),
+            pltpu.VMEM((2 * cells_y, 2 * bins), BF16),
+            pltpu.VMEM((4 * bins // CHUNK, cells_y + 16, CHUNK), F32),
+            pltpu.VMEM(spectrum.shape, BF16),
             DMA((2,)),
+            DMA((cells_x // 2,)),
         ],
         4 * 10**9,
         10 * MIB,
-        8,
+        20,
     )(
-        spectrum, f_oth, courant, courant_oth, sea_mask, interaction,
-        sides_own, sides_oth, from_a, from_b,
+        spectrum, f_oth, courant, courant_oth, sea_mask, in_hbm(interaction),
+        sides_own, sides_oth,
     )
     currents_out = call(
         momentum_kernel,
         "momentum",
         jax.ShapeDtypeStruct(currents.shape, F32),
-        [VMEM] * 2 + [HBM] + [VMEM] * 8 + [SMEM, VMEM],
+        [VMEM] * 2 + [HBM] * 2 + [VMEM] * 7 + [SMEM],
         HBM,
         [
             pltpu.VMEM((cells_x, chans, cells_y), F32),
+            pltpu.VMEM(sea_mask.shape, jnp.int32),
             pltpu.VMEM((cells_x + 2 * SUBSTEPS, fields, 2 * cells_y), F32),
             pltpu.VMEM((cells_x + 2 * SUBSTEPS, chans, 2 * cells_y), F32),
             pltpu.VMEM((cells_x + 2 * SUBSTEPS - 2, chans, 2 * cells_y), F32),
             pltpu.VMEM((cells_x, chans, cells_y), F32),
+            DMA,
             DMA((cells_x, 2)),
             DMA((2, cells_x)),
         ],
@@ -590,8 +640,8 @@
         4 * MIB,
         10,
     )(
-        s_main, s_aux, currents, sea_mask, west_own, east_own, from_a, from_b, from_w, from_e, token,
-        level_drag, lat_coriolis(cells_y),
+        s_main, s_aux, in_hbm(currents), in_hbm(sea_mask), west_own, east_own, from_a, from_b, from_w, from_e, token,
+        level_drag,
     )
     return (wave_out, currents_out)
 

time: 45.5 us -> 37.1 us (0.82)
  local copies, waits for them, and re-layouts: 7.04 us -> 0.02 us
  Pallas kernels: 20 us -> 19 us
    unnamed x32 -> x10, local copies, waits for them, and re-layouts: 7.04 us -> 0.02 us
    pallas_call x1, Pallas kernels: 9.12 us -> 6.96 us  [local(): call(wave_kernel, 'wave', (jax.ShapeDtypeStruct(spectrum.shape, BF16), ja...]
    ppermute x1, waiting for transfers between devices: 3.69 us -> 2.99 us  [local(): from_b = lax.ppermute(to_b, 'gy', pairing('gy', 1))]
    pallas_call x1, Pallas kernels: 5.04 us -> 5.67 us  [local(): call(momentum_kernel, 'momentum', jax.ShapeDtypeStruct(currents.shape, F3...]
    ppermute x1, waiting for transfers between devices: 0.01 us -> 0.48 us  [local(): east_own = lax.ppermute(to_w, 'gx', west)]
  transfers between devices with their start and end apart: 9 -> 9, of which waited for: 2 -> 2; matrix products, arithmetic and copies ran while one was open for 0% -> 0% of each run, Pallas kernels for 32% -> 34%
where the time goes in v4:
time: 37.1 us; the launch traced here: 36.8 us
  Pallas kernels  19 us (51%)
  starting transfers between devices  13.4 us (36%)
  waiting for transfers between devices  3.49 us (9%)
  between operations  0.93 us (3%)
    pallas_call x1, Pallas kernels, local(): call(wave_kernel, 'wave', (jax.ShapeDtypeStruct(spectrum.shape, BF16), ja...  6.96 us
    pallas_call x1, Pallas kernels, local(): call(momentum_kernel, 'momentum', jax.ShapeDtypeStruct(currents.shape, F3...  5.67 us
    pallas_call x1, Pallas kernels, local(): call(project_kernel, 'project', (jax.ShapeDtypeStruct((cells_x + 2, chans...  4.23 us
    ppermute x1, starting transfers between devices, local(): from_e = lax.ppermute(to_w, 'gx', west)  3.26 us
    ppermute x1, waiting for transfers between devices, local(): from_b = lax.ppermute(to_b, 'gy', pairing('gy', 1))  2.99 us
    ppermute x1, starting transfers between devices, local(): sides_oth = lax.ppermute(sides_own, 'comp', swap)  2.55 us
    ppermute x1, starting transfers between devices, local(): from_b = lax.ppermute(to_b, 'gy', pairing('gy', 1))  2.09 us
    ppermute x1, starting transfers between devices, local(): east_own = lax.ppermute(to_w, 'gx', west)  2.09 us
  transfers between devices with their start and end apart: 9, of which 2 were waited for; matrix products, arithmetic and copies ran while one was open for 0% of the time, Pallas kernels for 34%

profile of v4, /device:TPU:5, one launch (start us, length us, event | category | flops | bytes accessed | tf_op | source)
XLA Modules:
  0.0 36.8 jit_solution(1105562401360822849)
XLA Ops:
  0.6 0.0 copy-start
  0.6 0.0 copy-start.4
  0.6 0.0 copy-start.2
  0.7 0.0 copy-start.1
  0.7 0.7 %collective-permute-start = (bf16[16,128,512]{2,1,0:T(8,128)(2,1)}, bf16[16,128,512]{2,1,0:T(8,128)(2,1)S(1)}, u32[]{:S(2)}, u32[]{:S(2)}) collective-permute-start(bf16[16,128,512]{2,1,0:T(8,128)(2,1)} %rows_own.1), channel_id=1, source_target_pairs={{0,1},{1,0},{2,3},{3,2},{4,5},{5,4},{6,7},{7,6},{8,9},{9,8},{10,11... | collective-permute-start | bytes 6291464 | tf_op jit(solution)/shard_map/ppermute | solution.py:532
  1.4 0.1 collective-permute-start.1
  1.5 1.5 %outgoing.1 = (bf16[752,128]{1,0:T(8,128)(2,1)S(1)}, bf16[752,128]{1,0:T(8,128)(2,1)S(1)}, bf16[2,64,1024]{2,1,0:T(8,128)(2,1)S(1)}) custom-call(bf16[16,128,512]{2,1,0:T(8,128)(2,1)} %rows_own.1, f32[2,32,16,128]{3,2,1,0:T(8,128)} %currents.5, s32[16,128]{1,0:T(8,128)} %mask_in.3, bf16[2,64,1024]{2,1,0:T(8,128)(2,1)} %bitcast.1), custom_call_target="tpu_custom_call" | custom-call | flops 1000000 | bytes 1048576 | tf_op jit(solution)/shard_map/outgoing/pallas_call | solution.py:536
  3.0 1.3 %collective-permute-start.4 = (bf16[752,128]{1,0:T(8,128)(2,1)S(1)}, bf16[752,128]{1,0:T(8,128)(2,1)S(1)}, u32[]{:S(2)}, u32[]{:S(2)}) collective-permute-start(bf16[752,128]{1,0:T(8,128)(2,1)S(1)} %get-tuple-element.19), channel_id=1, source_target_pairs={{0,8},{8,16},{16,24},{24,0},{1,9},{9,17},{17,25},{25,1},{2,10},{10... | collective-permute-start | bytes 577544 | tf_op jit(solution)/shard_map/ppermute | solution.py:552
  4.3 2.1 %collective-permute-start.5 = (bf16[752,128]{1,0:T(8,128)(2,1)S(1)}, bf16[752,128]{1,0:T(8,128)(2,1)S(1)}, u32[]{:S(2)}, u32[]{:S(2)}) collective-permute-start(bf16[752,128]{1,0:T(8,128)(2,1)S(1)} %get-tuple-element.20), channel_id=1, source_target_pairs={{8,0},{16,8},{24,16},{0,24},{9,1},{17,9},{25,17},{1,25},{10,2},{18... | collective-permute-start | bytes 577544 | tf_op jit(solution)/shard_map/ppermute | solution.py:553
  6.4 0.0 collective-permute-done.1.courant_oth
  6.4 0.0 collective-permute-done.f_oth.rows_oth
  6.4 0.0 copy-done
  6.4 0.0 copy-done.4
  6.4 0.0 copy-done.2
  6.4 0.0 copy-done.1
  6.4 4.2 %project.1 = (f32[18,64,128]{2,1,0:T(8,128)S(1)}, f32[16,64,128]{2,1,0:T(8,128)S(1)}, f32[6,64,256]{2,1,0:T(8,128)S(1)}, bf16[144,128]{1,0:T(8,128)(2,1)S(1)}, bf16[144,128]{1,0:T(8,128)(2,1)S(1)}) custom-call(bf16[16,128,512]{2,1,0:T(8,128)(2,1)S(1)} %copy-done, bf16[16,128,512]{2,1,0:T(8,128)(2,1)S(1)} %collective-permute-done.f_oth.rows_oth, ...), custom_call_target="tpu_custom_call" | custom-call | flops 3000000000 | bytes 8388608 | tf_op jit(solution)/shard_map/project/pallas_call | solution.py:556
  10.7 1.3 %collective-permute-start.2 = (bf16[144,128]{1,0:T(8,128)(2,1)S(1)}, bf16[144,128]{1,0:T(8,128)(2,1)S(1)}, u32[]{:S(2)}, u32[]{:S(2)}) collective-permute-start(bf16[144,128]{1,0:T(8,128)(2,1)S(1)} %get-tuple-element.17), channel_id=1, source_target_pairs={{0,2},{4,6},{2,0},{6,4},{1,3},{5,7},{3,1},{7,5},{8,10},{12,14},{10... | collective-permute-start | bytes 110600 | tf_op jit(solution)/shard_map/ppermute | solution.py:581
  12.0 2.1 %collective-permute-start.3 = (bf16[144,128]{1,0:T(8,128)(2,1)S(1)}, bf16[144,128]{1,0:T(8,128)(2,1)S(1)}, u32[]{:S(2)}, u32[]{:S(2)}) collective-permute-start(bf16[144,128]{1,0:T(8,128)(2,1)S(1)} %get-tuple-element.18), channel_id=1, source_target_pairs={{2,4},{4,2},{3,5},{5,3},{10,12},{12,10},{11,13},{13,11},{18,20},{2... | collective-permute-start | bytes 110600 | tf_op jit(solution)/shard_map/ppermute | solution.py:582
  14.1 0.0 collective-permute-done.4.side_w
  14.1 0.5 %collective-permute-done.5.side_e = bf16[752,128]{1,0:T(8,128)(2,1)S(1)} collective-permute-done((bf16[752,128]{1,0:T(8,128)(2,1)S(1)}, bf16[752,128]{1,0:T(8,128)(2,1)S(1)}, u32[]{:S(2)}, u32[]{:S(2)}) %collective-permute-start.5) | collective-permute-done | bytes 192544 | tf_op jit(solution)/shard_map/ppermute | solution.py:553
  14.6 0.0 collective-permute-done.2.from_a
  14.6 3.0 %collective-permute-done.3.from_b = bf16[144,128]{1,0:T(8,128)(2,1)S(1)} collective-permute-done((bf16[144,128]{1,0:T(8,128)(2,1)S(1)}, bf16[144,128]{1,0:T(8,128)(2,1)S(1)}, u32[]{:S(2)}, u32[]{:S(2)}) %collective-permute-start.3) | collective-permute-done | bytes 36896 | tf_op jit(solution)/shard_map/ppermute | solution.py:582
  17.5 0.6 %relay.1 = (bf16[272,128]{1,0:T(8,128)(2,1)S(1)}, bf16[272,128]{1,0:T(8,128)(2,1)S(1)}, bf16[1152,128]{1,0:T(8,128)(2,1)S(1)}) custom-call(f32[6,64,256]{2,1,0:T(8,128)S(1)} %get-tuple-element.16.s_edge, bf16[144,128]{1,0:T(8,128)(2,1)S(1)} %collective-permute-done.2.from_a, bf16[144,128]{1,0:T(8,128)(2,1)S(1)} %collective-permute-done.3.from_b, ...), custom_call_target="tpu_custom_call" | custom-call | flops 1000000 | bytes 1048576 | tf_op jit(solution)/shard_map/relay/pallas_call | solution.py:584
  18.2 2.5 %collective-permute-start.6 = (bf16[1152,128]{1,0:T(8,128)(2,1)S(1)}, bf16[1152,128]{1,0:T(8,128)(2,1)S(1)}, u32[]{:S(2)}, u32[]{:S(2)}) collective-permute-start(bf16[1152,128]{1,0:T(8,128)(2,1)S(1)} %get-tuple-element.21.sides_own), channel_id=1, source_target_pairs={{0,1},{1,0},{2,3},{3,2},{4,5},{5,4},{6,7},{7,6},{8,9},{9,8},{10,11... | collective-permute-start | bytes 884744 | tf_op jit(solution)/shard_map/ppermute | solution.py:596
  20.7 0.0 collective-permute-start.7
  20.8 3.3 %collective-permute-start.8 = (bf16[272,128]{1,0:T(8,128)(2,1)S(1)}, bf16[272,128]{1,0:T(8,128)(2,1)S(1)}, u32[]{:S(2)}, u32[]{:S(2)}) collective-permute-start(bf16[272,128]{1,0:T(8,128)(2,1)S(1)} %get-tuple-element.26), channel_id=1, source_target_pairs={{8,0},{16,8},{24,16},{0,24},{9,1},{17,9},{25,17},{1,25},{10,2},{18... | collective-permute-start | bytes 208904 | tf_op jit(solution)/shard_map/ppermute | solution.py:598
  24.0 0.0 collective-permute-done.6.sides_oth
  24.0 7.0 %wave.1 = (bf16[16,128,512]{2,1,0:T(8,128)(2,1)}, f32[8,128]{1,0:T(8,128)S(1)}) custom-call(bf16[16,128,512]{2,1,0:T(8,128)(2,1)S(1)} %copy-done, bf16[16,128,512]{2,1,0:T(8,128)(2,1)S(1)} %collective-permute-done.f_oth.rows_oth, f32[2,512]{1,0:T(2,128)S(1)} %copy-done.4, f32[2,512]{1,0:T(2,128)S(1)} %collective-permute-done.1.courant_oth, ...), custom_call_target="tpu_custom_call" | custom-call | flops 4000000000 | bytes 10485760 | tf_op jit(solution)/shard_map/wave/pallas_call | solution.py:600
  31.0 0.0 collective-permute-done.7.from_w
  31.0 0.0 collective-permute-done.8.from_e
  31.0 0.0 copy-done.3
  31.0 5.7 %momentum.1 = f32[2,32,16,128]{3,2,1,0:T(8,128)} custom-call(f32[18,64,128]{2,1,0:T(8,128)S(1)} %get-tuple-element.23.s_main, f32[16,64,128]{2,1,0:T(8,128)S(1)} %get-tuple-element.24.s_aux, f32[2,32,16,128]{3,2,1,0:T(8,128)} %currents.5, s32[16,128]{1,0:T(8,128)} %mask_in.3, bf16[752,128]{1,0:T(8,128)(2,1)S(1)} %collective-permute-done.4.side_w, ...), custom_call_target="tpu_custom_call" | custom-call | flops 100000000 | bytes 4194304 | tf_op jit(solution)/shard_map/momentum/pallas_call | solution.py:622
  (1 shorter events, 0.0 us)
Async XLA Ops:
  0.6 5.8 %copy-start = (bf16[16,128,512]{2,1,0:T(8,128)(2,1)S(1)}, bf16[16,128,512]{2,1,0:T(8,128)(2,1)}, u32[]{:S(2)}) copy-start(bf16[16,128,512]{2,1,0:T(8,128)(2,1)} %rows_own.1) | copy-start | bytes 6291460
  0.6 5.8 %copy-start.4 = (f32[2,512]{1,0:T(2,128)S(1)}, f32[2,512]{1,0:T(2,128)}, u32[]{:S(2)}) copy-start(f32[2,512]{1,0:T(2,128)} %courant_own.3) | copy-start | bytes 12292
  0.6 5.8 %copy-start.2 = (s32[16,128]{1,0:T(8,128)S(1)}, s32[16,128]{1,0:T(8,128)}, u32[]{:S(2)}) copy-start(s32[16,128]{1,0:T(8,128)} %mask_in.3) | copy-start | bytes 24580
  0.7 5.8 %copy-start.1 = (f32[2,32,16,128]{3,2,1,0:T(8,128)S(1)}, f32[2,32,16,128]{3,2,1,0:T(8,128)}, u32[]{:S(2)}) copy-start(f32[2,32,16,128]{3,2,1,0:T(8,128)} %currents.5) | copy-start | bytes 1572868
  0.7 5.7 %collective-permute-start = (bf16[16,128,512]{2,1,0:T(8,128)(2,1)}, bf16[16,128,512]{2,1,0:T(8,128)(2,1)S(1)}, u32[]{:S(2)}, u32[]{:S(2)}) collective-permute-start(bf16[16,128,512]{2,1,0:T(8,128)(2,1)} %rows_own.1), channel_id=1, source_target_pairs={{0,1},{1,0},{2,3},{3,2},{4,5},{5,4},{6,7},{7,6},{8,9},{9,8},{10,11... | collective-permute-start | bytes 6291464 | tf_op jit(solution)/shard_map/ppermute | solution.py:532
  1.4 5.0 %collective-permute-start.1 = (f32[2,512]{1,0:T(2,128)}, f32[2,512]{1,0:T(2,128)S(1)}, u32[]{:S(2)}, u32[]{:S(2)}) collective-permute-start(f32[2,512]{1,0:T(2,128)} %courant_own.3), channel_id=1, source_target_pairs={{0,1},{1,0},{2,3},{3,2},{4,5},{5,4},{6,7},{7,6},{8,9},{9,8},{10,11... | collective-permute-start | bytes 12296 | tf_op jit(solution)/shard_map/ppermute | solution.py:533
  3.0 11.1 %collective-permute-start.4 = (bf16[752,128]{1,0:T(8,128)(2,1)S(1)}, bf16[752,128]{1,0:T(8,128)(2,1)S(1)}, u32[]{:S(2)}, u32[]{:S(2)}) collective-permute-start(bf16[752,128]{1,0:T(8,128)(2,1)S(1)} %get-tuple-element.19), channel_id=1, source_target_pairs={{0,8},{8,16},{16,24},{24,0},{1,9},{9,17},{17,25},{25,1},{2,10},{10... | collective-permute-start | bytes 577544 | tf_op jit(solution)/shard_map/ppermute | solution.py:552
  4.3 10.2 %collective-permute-start.5 = (bf16[752,128]{1,0:T(8,128)(2,1)S(1)}, bf16[752,128]{1,0:T(8,128)(2,1)S(1)}, u32[]{:S(2)}, u32[]{:S(2)}) collective-permute-start(bf16[752,128]{1,0:T(8,128)(2,1)S(1)} %get-tuple-element.20), channel_id=1, source_target_pairs={{8,0},{16,8},{24,16},{0,24},{9,1},{17,9},{25,17},{1,25},{10,2},{18... | collective-permute-start | bytes 577544 | tf_op jit(solution)/shard_map/ppermute | solution.py:553
  10.7 3.9 %collective-permute-start.2 = (bf16[144,128]{1,0:T(8,128)(2,1)S(1)}, bf16[144,128]{1,0:T(8,128)(2,1)S(1)}, u32[]{:S(2)}, u32[]{:S(2)}) collective-permute-start(bf16[144,128]{1,0:T(8,128)(2,1)S(1)} %get-tuple-element.17), channel_id=1, source_target_pairs={{0,2},{4,6},{2,0},{6,4},{1,3},{5,7},{3,1},{7,5},{8,10},{12,14},{10... | collective-permute-start | bytes 110600 | tf_op jit(solution)/shard_map/ppermute | solution.py:581
  12.0 5.6 %collective-permute-start.3 = (bf16[144,128]{1,0:T(8,128)(2,1)S(1)}, bf16[144,128]{1,0:T(8,128)(2,1)S(1)}, u32[]{:S(2)}, u32[]{:S(2)}) collective-permute-start(bf16[144,128]{1,0:T(8,128)(2,1)S(1)} %get-tuple-element.18), channel_id=1, source_target_pairs={{2,4},{4,2},{3,5},{5,3},{10,12},{12,10},{11,13},{13,11},{18,20},{2... | collective-permute-start | bytes 110600 | tf_op jit(solution)/shard_map/ppermute | solution.py:582
  18.2 5.8 %collective-permute-start.6 = (bf16[1152,128]{1,0:T(8,128)(2,1)S(1)}, bf16[1152,128]{1,0:T(8,128)(2,1)S(1)}, u32[]{:S(2)}, u32[]{:S(2)}) collective-permute-start(bf16[1152,128]{1,0:T(8,128)(2,1)S(1)} %get-tuple-element.21.sides_own), channel_id=1, source_target_pairs={{0,1},{1,0},{2,3},{3,2},{4,5},{5,4},{6,7},{7,6},{8,9},{9,8},{10,11... | collective-permute-start | bytes 884744 | tf_op jit(solution)/shard_map/ppermute | solution.py:596
  20.7 10.2 %collective-permute-start.7 = (bf16[272,128]{1,0:T(8,128)(2,1)S(1)}, bf16[272,128]{1,0:T(8,128)(2,1)S(1)}, u32[]{:S(2)}, u32[]{:S(2)}) collective-permute-start(bf16[272,128]{1,0:T(8,128)(2,1)S(1)} %get-tuple-element.25), channel_id=1, source_target_pairs={{0,8},{8,16},{16,24},{24,0},{1,9},{9,17},{17,25},{25,1},{2,10},{10... | collective-permute-start | bytes 208904 | tf_op jit(solution)/shard_map/ppermute | solution.py:597
  20.8 10.3 %copy-start.3 = (f32[32]{0:T(128)S(1)}, f32[32]{0:T(128)}, u32[]{:S(2)}) copy-start(f32[32]{0:T(128)} %drag.1) | copy-start | bytes 388
  20.8 10.2 %collective-permute-start.8 = (bf16[272,128]{1,0:T(8,128)(2,1)S(1)}, bf16[272,128]{1,0:T(8,128)(2,1)S(1)}, u32[]{:S(2)}, u32[]{:S(2)}) collective-permute-start(bf16[272,128]{1,0:T(8,128)(2,1)S(1)} %get-tuple-element.26), channel_id=1, source_target_pairs={{8,0},{16,8},{24,16},{0,24},{9,1},{17,9},{25,17},{1,25},{10,2},{18... | collective-permute-start | bytes 208904 | tf_op jit(solution)/shard_map/ppermute | solution.py:598

commit v5 on v4

--- a/solution.py
+++ b/solution.py
@@ -19,6 +19,9 @@
 MASK_ROWS = 16
 SLOT = 8
 CHUNK = 128
+TILE_ROWS = 16
+EARLY_PAIRS = 4
+TILE = 8
 PARTS = 5
 
 
@@ -43,17 +46,6 @@
 
 def chunks_of(bins):
     return [slice(j * CHUNK, (j + 1) * CHUNK) for j in range(bins // CHUNK)]
-
-
-def load_currents(currents, rows, cur, sem):
-    levels = currents.shape[1]
-    return [
-        pltpu.make_async_copy(
-            currents.at[c, :, x, :], cur.at[i, pl.ds(c * levels, levels), :], sem.at[i, c]
-        )
-        for i, x in enumerate(rows)
-        for c in range(2)
-    ]
 
 
 def sea_row(mask, x, rows):
@@ -118,16 +110,14 @@
 
 def project_kernel(
     f_own, f_oth, courant_own, courant_oth, stokes_proj, currents, mask,
-    s_main, s_aux, s_edge, msg_a, msg_b,
-    proj, wt_own, wt_oth, cur, sem,
+    s_main, s_aux, s_edge, state, msg_a, msg_b, token,
+    proj, wt_own, wt_oth,
 ):
     cells_x, width, bins = f_own.shape
     chans = s_main.shape[1]
     fields = chans + MASK_ROWS
     core = lax.axis_index("comp")
-    copies = load_currents(currents, range(cells_x), cur, sem)
-    for copy in copies:
-        copy.start()
+    token[...] = jnp.zeros_like(token)
     stokes_weights(stokes_proj, courant_own, core, core, wt_own)
     stokes_weights(stokes_proj, courant_oth, core, 1 - core, wt_oth)
     contract = (((1,), (1,)), ((), ()))
@@ -138,9 +128,6 @@
             both += lax.dot_general(wt[...], cells, contract, preferred_element_type=F32)
         proj[2 * pair] = both[:, :width]
         proj[2 * pair + 1] = both[:, width:]
-    for copy in copies:
-        copy.wait()
-
     lane = lane_of(chans, width)
     lane_f = lane_of(fields, width)
 
@@ -174,7 +161,10 @@
         pack_n = jnp.where(window, ring_n, pack_n)
         pack_s = jnp.where(window, ring_s, pack_s)
         if 0 <= x < cells_x:
-            row = jnp.concatenate([cur[x], sea_row(mask, x, MASK_ROWS)], 0)
+            row = jnp.concatenate(
+                [currents[0, :, x, :], currents[1, :, x, :], sea_row(mask, x, MASK_ROWS)], 0
+            )
+            state[x] = row
             start = current_lane(x, cells_x)
             window = between(lane_f, start, start + 3)
             cur_n = jnp.where(window, pltpu.roll(row, (3 + start) % width, 1), cur_n)
@@ -236,7 +226,8 @@
     return main, aux + halo_lanes(lane, low, high, width)
 
 
-def relay_kernel(cells_x, s_edge, from_a, from_b, side_w, side_e, msg_e, msg_w, spectra):
+def relay_kernel(cells_x, s_edge, from_a, from_b, side_w, side_e, token, msg_e, msg_w, spectra):
+    del token
     chans, width = s_edge.shape[1], s_edge.shape[2] // 2
     fields = chans + MASK_ROWS
     rows, edges = side_w.shape[0] - EDGE * fields, from_a.shape[0] - fields
@@ -280,9 +271,9 @@
 
 
 def momentum_kernel(
-    s_main, s_aux, currents, mask_in, side_w, side_e, from_a, from_b, from_w, from_e, token, drag,
+    s_main, s_aux, state, side_w, side_e, from_a, from_b, from_w, from_e, token, drag,
     out,
-    cur, mask, flow_a, flow_b, stokes, result, mask_sem, in_sem, sem,
+    flow_a, flow_b, stokes, result, sem,
 ):
     del token
     cells_x, chans, width = s_aux.shape
@@ -291,11 +282,6 @@
     half = width // 2
     lane = lane_of(chans, width)
     lane_f = lane_of(fields, width)
-    copies = load_currents(currents, range(cells_x), cur, in_sem)
-    mask_copy = pltpu.make_async_copy(mask_in, mask, mask_sem)
-    for copy in (mask_copy, *copies):
-        copy.start()
-
     side_base = side_w.shape[0] - EDGE * fields
     corner_w, corner_e = from_w[EDGE * chans :].astype(F32), from_e[EDGE * chans :].astype(F32)
     tile_s, tile_n = from_sides(from_a, from_b, slice(0, fields))
@@ -304,10 +290,9 @@
         ring = pltpu.roll(tile, (-at - 3) % width, 1)
         return halo_lanes(lanes, ring, ring, width)
 
-    mask_copy.wait()
     for x in range(-SUBSTEPS, cells_x + SUBSTEPS):
         if 0 <= x < cells_x:
-            flow_a[x + SUBSTEPS, chans:, :width] = sea_row(mask, x, MASK_ROWS)
+            flow_a[x + SUBSTEPS, :, :width] = state[x]
             aux = current_halo(tile_s, tile_n, x, cells_x, lane_f, width)
         else:
             side, tile, i = (side_w, corner_w, x + SUBSTEPS) if x < 0 else (side_e, corner_e, x - cells_x)
@@ -333,14 +318,16 @@
         stokes[x + margin, :, :width] = main * sea[:, :width]
         stokes[x + margin, :, width:] = aux * sea[:, width:]
 
-    for copy in copies:
-        copy.wait()
-    for x in range(cells_x):
-        flow_a[x + SUBSTEPS, :chans, :width] = cur[x]
     at_level = lax.broadcasted_iota(jnp.int32, (levels, 1), 0)
     drag_col = jnp.zeros((levels, 1), F32)
     for level in range(levels):
         drag_col = jnp.where(at_level == level, drag[level], drag_col)
+    def copy_out(block):
+        rows = pl.ds(block * TILE, TILE)
+        return pltpu.make_async_copy(
+            result.at[:, :, rows, :], out.at[:, :, rows, :], sem.at[block]
+        )
+
     half_cor = time_step * lat_coriolis(width)
     keep = 1.0 - 4.0 * time_step * viscosity - time_step * drag_col
     ring = 2 * width
@@ -368,31 +355,44 @@
             u_new = sea * (u_new + time_step * viscosity * ((u_e + u_w) + (u_n + u_s)))
             v_new = sea * (v_new + time_step * viscosity * ((v_e + v_w) + (v_n + v_s)))
             if last:
-                result[x, :levels] = u_new
-                result[x, levels:] = v_new
-                for c in range(2):
-                    pltpu.make_async_copy(
-                        result.at[x, pl.ds(c * levels, levels), :], out.at[c, :, x, :], sem.at[c, x]
-                    ).start()
+                result[0, :, x, :] = u_new
+                result[1, :, x, :] = v_new
+                if x % TILE == TILE - 1:
+                    copy_out(x // TILE).start()
             else:
                 target[at, :levels] = u_new
                 target[at, levels:chans] = v_new
         source, target = target, source
-    for x in range(cells_x):
-        for c in range(2):
-            pltpu.make_async_copy(
-                result.at[x, pl.ds(c * levels, levels), :], out.at[c, :, x, :], sem.at[c, x]
-            ).wait()
-
-
-def wave_kernel(
-    rows_own, rows_oth, courant_own, courant_oth, mask, interaction,
-    sides_own, sides_oth,
-    out, token,
-    inter, adv_a, adv_b, shifted, slots, inter_sem, out_sem,
+    for block in range(cells_x // TILE):
+        copy_out(block).wait()
+
+
+def wave_groups(cells_x, width, early_pairs):
+    inner = [[(x, TILE_ROWS, width - TILE_ROWS) for x in (1 + 2 * p, 2 + 2 * p)] for p in range(early_pairs)]
+    outer = [[(0, 0, width), (cells_x - 1, 0, width)]]
+    for x in range(1 + 2 * early_pairs, cells_x - 1, 2):
+        outer.append([(i, 0, width) for i in range(x, min(x + 2, cells_x - 1))])
+    seams = [
+        block
+        for x in range(1, 1 + 2 * early_pairs)
+        for block in ((x, 0, TILE_ROWS), (x, width - TILE_ROWS, width))
+    ]
+    step = 2 * width // TILE_ROWS
+    outer += [seams[i : i + step] for i in range(0, len(seams), step)]
+    return inner, outer
+
+
+def rows_of(group):
+    return sum(last - first for _, first, last in group)
+
+
+def wave_body(
+    groups, sides,
+    f_own, f_oth, courant_own, courant_oth, mask, interaction,
+    slots, send,
+    inter, adv, sea, moved, inter_sem,
 ):
-    cells_x, width, bins = rows_own.shape
-    pairs = cells_x // 2
+    cells_x, width, bins = f_own.shape
     core = lax.axis_index("comp")
     own_at, oth_at = pl.multiple_of(core * bins, bins), pl.multiple_of((1 - core) * bins, bins)
     inter_copies = [
@@ -407,74 +407,77 @@
         copy.start()
 
     even = is_even("gy")
+    per_core = bins // CHUNK
     halves = []
-    for rows, sides, courant in (
-        (rows_own, sides_own, courant_own),
-        (rows_oth, sides_oth, courant_oth),
-    ):
+    for rows, side, courant in zip((f_own, f_oth), sides, (courant_own, courant_oth), strict=True):
         for j, cols in enumerate(chunks_of(bins)):
             cour_x, cour_y = courant[0:1, cols], courant[1:2, cols]
             size_x, size_y = jnp.abs(cour_x), jnp.abs(cour_y)
-            base = bins // CHUNK * 2 * width + j * cells_x
-            edge_a = sides[base : base + cells_x].astype(F32)
-            base += bins // CHUNK * cells_x
-            edge_b = sides[base : base + cells_x].astype(F32)
+            south = north = None
+            if side is not None:
+                base = 2 * per_core * width + j * cells_x
+                edge_a = side[base : base + cells_x].astype(F32)
+                base += per_core * cells_x
+                edge_b = side[base : base + cells_x].astype(F32)
+                south, north = jnp.where(even, edge_b, edge_a), jnp.where(even, edge_a, edge_b)
             halves.append(
                 (
-                    rows, sides, j, cols, jnp.where(even, edge_b, edge_a), jnp.where(even, edge_a, edge_b),
+                    rows, side, j, cols, south, north,
                     1.0 - size_x - size_y, size_x, size_y, cour_x > 0.0, cour_y > 0.0,
                 )
             )
 
-    token[...] = jnp.zeros_like(token)
-
-    def sea_column(x):
-        return jnp.transpose(sea_row(mask, x, CHUNK))
-
-    adv = (adv_a, adv_b)
-
-    def advect(pair, n):
-        rows, sides, j, cols, south, north, c_mid, c_x, c_y, up_x, up_y = halves[n]
-        first = 2 * pair
-        cells = []
-        for x in range(first - 1, first + 3):
-            if x < 0:
-                cells.append(sides[j * width : (j + 1) * width].astype(F32))
-            elif x == cells_x:
-                base = bins // CHUNK * width
-                cells.append(sides[base + j * width : base + (j + 1) * width].astype(F32))
-            else:
-                cells.append(rows[x, :, cols].astype(F32))
-        for i in range(2):
-            x = first + i
-            mid = cells[i + 1]
-            moved = shifted.at[2 * n + i]
-            moved[8 : 8 + width] = mid
-            moved[7:8] = south[x : x + 1]
-            moved[8 + width : 9 + width] = north[x : x + 1]
-            low, high = moved[7 : 7 + width], moved[9 : 9 + width]
-            beside = jnp.where(up_x, cells[i], cells[i + 2])
-            value = c_mid * mid + c_x * beside + c_y * jnp.where(up_y, low, high)
-            adv[pair % 2][i * width : (i + 1) * width, n * CHUNK : (n + 1) * CHUNK] = value.astype(BF16)
-
-    def copy_out(pair):
-        return pltpu.make_async_copy(
-            slots.at[pl.ds(2 * pair, 2)], out.at[pl.ds(2 * pair, 2)], out_sem.at[pair]
-        )
-
-    def finish(pair, seas, piece):
-        done = adv[pair % 2]
-        i, block = piece // blocks, piece % blocks
-        rows = slice(i * width, (i + 1) * width)
+    def cell(rows, side, j, cols, x, first, last):
+        if 0 <= x < cells_x:
+            return rows[x, first:last, cols].astype(F32)
+        base = (0 if x < 0 else per_core * width) + j * width
+        return side[base + first : base + last].astype(F32)
+
+    def advect(at, n):
+        rows, side, j, cols, south, north, c_mid, c_x, c_y, up_x, up_y = halves[n]
+        row = 0
+        for i, (x, first, last) in enumerate(groups[at]):
+            low_end, high_end = max(first - TILE_ROWS, 0), min(last + TILE_ROWS, width)
+            wide = cell(rows, side, j, cols, x, low_end, high_end)
+            mid = wide[first - low_end : last - low_end]
+            shifted = moved.at[(len(groups[at]) * n + i) % moved.shape[0]]
+            shifted[8 + low_end : 8 + high_end] = wide
+            if first == 0:
+                shifted[7:8] = south[x : x + 1]
+            if last == width:
+                shifted[8 + width : 9 + width] = north[x : x + 1]
+            low, high = shifted[7 + first : 7 + last], shifted[9 + first : 9 + last]
+            west = cell(rows, side, j, cols, x - 1, first, last)
+            east = cell(rows, side, j, cols, x + 1, first, last)
+            value = c_mid * mid + c_x * jnp.where(up_x, west, east) + c_y * jnp.where(up_y, low, high)
+            height = last - first
+            adv[at % 2][row : row + height, n * CHUNK : (n + 1) * CHUNK] = value.astype(BF16)
+            row += height
+
+    def put_sea(at):
+        row = 0
+        for x, first, last in groups[at]:
+            column = jnp.transpose(sea_row(mask, x, CHUNK))
+            sea[at % 2][row : row + last - first] = column[first:last]
+            row += last - first
+
+    def finish(at, piece):
+        done, mine = adv[at % 2], sea[at % 2]
+        half, block = piece // blocks, piece % blocks
+        middle = rows_of(groups[at]) // 2 // TILE_ROWS * TILE_ROWS
+        low, high = (0, middle) if half == 0 else (middle, rows_of(groups[at]))
         cols = slice(block * bins // blocks, (block + 1) * bins // blocks)
-        gain = jnp.dot(done[rows, :], inter[:, cols], preferred_element_type=F32)
-        for c in chunks_of(bins // blocks):
-            own = slice(cols.start + c.start, cols.start + c.stop)
-            total = done[rows, own].astype(F32) + gain[:, c]
-            slots[2 * pair + i, :, own] = (total * seas[i]).astype(BF16)
-
-    def both_seas(pair):
-        return [sea_column(2 * pair + i) for i in range(2)]
+        gain = jnp.dot(done[low:high, :], inter[:, cols], preferred_element_type=F32)
+        row = 0
+        for x, first, last in groups[at]:
+            begin, end = max(low, row), min(high, row + last - first)
+            if begin < end:
+                lats = slice(first + begin - row, first + end - row)
+                for c in chunks_of(bins // blocks):
+                    own = slice(cols.start + c.start, cols.start + c.stop)
+                    total = done[begin:end, own].astype(F32) + gain[begin - low : end - low, c]
+                    slots[x, lats, own] = (total * mine[begin:end]).astype(BF16)
+            row += last - first
 
     blocks = 2
     pieces = 2 * blocks
@@ -483,16 +486,58 @@
         advect(0, n)
     for copy in inter_copies:
         copy.wait()
-    for pair in range(1, pairs + 1):
-        seas = both_seas(pair - 1)
+    for at in range(1, len(groups) + 1):
+        put_sea(at - 1)
         for piece in range(pieces):
-            if pair < pairs:
+            if at < len(groups):
                 for n in range(piece * parts // pieces, (piece + 1) * parts // pieces):
-                    advect(pair, n)
-            finish(pair - 1, seas, piece)
-        copy_out(pair - 1).start()
-    for pair in range(pairs):
-        copy_out(pair).wait()
+                    advect(at, n)
+            finish(at - 1, piece)
+        send(at - 1)
+
+
+def inner_kernel(
+    groups,
+    f_own, f_oth, courant_own, courant_oth, mask, interaction, token_in,
+    wave, token,
+    inter, adv_a, adv_b, sea_a, sea_b, moved, inter_sem,
+):
+    token[...] = token_in[...]
+    wave_body(
+        groups, (None, None),
+        f_own, f_oth, courant_own, courant_oth, mask, interaction,
+        wave, lambda n: None,
+        inter, (adv_a, adv_b), (sea_a, sea_b), moved, inter_sem,
+    )
+
+
+def outer_kernel(
+    groups, groups_before,
+    f_own, f_oth, courant_own, courant_oth, mask, interaction, sides_own, sides_oth, wave,
+    out, token,
+    slots, inter, adv_a, adv_b, sea_a, sea_b, moved, inter_sem, out_sem,
+):
+    token[...] = jnp.zeros_like(token)
+    copies = []
+
+    def send(source, blocks):
+        for x, first, last in blocks:
+            lats = pl.ds(first, last - first)
+            copies.append(
+                pltpu.make_async_copy(source.at[x, lats], out.at[x, lats], out_sem.at[len(copies)])
+            )
+            copies[-1].start()
+
+    for group in groups_before:
+        send(wave, group)
+    wave_body(
+        groups, (sides_own, sides_oth),
+        f_own, f_oth, courant_own, courant_oth, mask, interaction,
+        slots, lambda n: send(slots, groups[n]),
+        inter, (adv_a, adv_b), (sea_a, sea_b), moved, inter_sem,
+    )
+    for copy in copies:
+        copy.wait()
 
 
 VMEM = pl.BlockSpec(memory_space=pltpu.VMEM)
@@ -532,6 +577,7 @@
     f_oth = lax.ppermute(spectrum, "comp", swap)
     courant_oth = lax.ppermute(courant, "comp", swap)
     stokes_proj = jnp.transpose(stokes_proj, (0, 2, 1))
+    token_type = jax.ShapeDtypeStruct((8, CHUNK), F32)
     side_rows = bins // CHUNK * cells_y + EDGE * fields
     to_e, to_w, stokes_proj = call(
         outgoing_kernel,
@@ -553,24 +599,24 @@
     east_own = lax.ppermute(to_w, "gx", west)
 
     edge_rows = fields + bins // CHUNK * cells_x
-    s_main, s_aux, s_edge, to_a, to_b = call(
+    s_main, s_aux, s_edge, state, to_a, to_b, token = call(
         project_kernel,
         "project",
         (
             jax.ShapeDtypeStruct((cells_x + 2, chans, cells_y), F32),
             jax.ShapeDtypeStruct((cells_x, chans, cells_y), F32),
             jax.ShapeDtypeStruct((2 * EDGE, chans, 2 * cells_y), F32),
+            jax.ShapeDtypeStruct((cells_x, fields, cells_y), F32),
             message(edge_rows),
             message(edge_rows),
+            token_type,
         ),
         [VMEM] * 7,
-        (VMEM,) * 5,
+        (VMEM,) * 7,
         [
             pltpu.VMEM((cells_x, PARTS * chans, cells_y), F32),
             pltpu.VMEM((PARTS * chans, bins), BF16),
             pltpu.VMEM((PARTS * chans, bins), BF16),
-            pltpu.VMEM((cells_x, chans, cells_y), F32),
-            DMA((cells_x, 2)),
         ],
         3 * 10**9,
         8 * MIB,
@@ -581,66 +627,82 @@
     from_a = lax.ppermute(to_a, "gy", pairing("gy", 0))
     from_b = lax.ppermute(to_b, "gy", pairing("gy", 1))
 
+    inner, outer = wave_groups(cells_x, cells_y, EARLY_PAIRS)
+    wave_type = jax.ShapeDtypeStruct(spectrum.shape, BF16)
+
+    def wave_scratch(groups):
+        height = max(map(rows_of, groups))
+        return [
+            pltpu.VMEM((2 * bins, bins), BF16),
+            *[pltpu.VMEM((height, 2 * bins), BF16)] * 2,
+            *[pltpu.VMEM((height, CHUNK), F32)] * 2,
+            pltpu.VMEM((16, cells_y + 16, CHUNK), F32),
+            DMA((2,)),
+        ]
+
+    wave, token = call(
+        functools.partial(inner_kernel, inner),
+        "inner",
+        (wave_type, token_type),
+        [VMEM] * 5 + [HBM, VMEM],
+        (VMEM,) * 2,
+        wave_scratch(inner),
+        2 * 10**9,
+        5 * MIB,
+        20,
+    )(spectrum, f_oth, courant, courant_oth, sea_mask, in_hbm(interaction), token)
+
     to_e, to_w, sides_own = call(
         functools.partial(relay_kernel, cells_x),
         "relay",
         (message(EDGE * chans + fields),) * 2
         + (message(2 * bins // CHUNK * (cells_y + cells_x)),),
-        [VMEM] * 5,
+        [VMEM] * 6,
         (VMEM,) * 3,
         [],
         10**6,
         MIB,
         4,
-    )(s_edge, from_a, from_b, west_own, east_own)
+    )(s_edge, from_a, from_b, west_own, east_own, token)
     sides_oth = lax.ppermute(sides_own, "comp", swap)
     from_w = lax.ppermute(to_e, "gx", east)
     from_e = lax.ppermute(to_w, "gx", west)
 
     wave_out, token = call(
-        wave_kernel,
-        "wave",
-        (jax.ShapeDtypeStruct(spectrum.shape, BF16), jax.ShapeDtypeStruct((8, CHUNK), F32)),
-        [VMEM] * 5 + [HBM] + [VMEM] * 2,
+        functools.partial(outer_kernel, outer, inner),
+        "outer",
+        (wave_type, token_type),
+        [VMEM] * 5 + [HBM] + [VMEM] * 3,
         (HBM, VMEM),
         [
-            pltpu.VMEM((2 * bins, bins), BF16),
-            pltpu.VMEM((2 * cells_y, 2 * bins), BF16),
-            pltpu.VMEM((2 * cells_y, 2 * bins), BF16),
-            pltpu.VMEM((4 * bins // CHUNK, cells_y + 16, CHUNK), F32),
             pltpu.VMEM(spectrum.shape, BF16),
-            DMA((2,)),
-            DMA((cells_x // 2,)),
+            *wave_scratch(outer),
+            DMA((sum(map(len, inner + outer)),)),
         ],
-        4 * 10**9,
-        10 * MIB,
+        2 * 10**9,
+        5 * MIB,
         20,
     )(
-        spectrum, f_oth, courant, courant_oth, sea_mask, in_hbm(interaction),
-        sides_own, sides_oth,
+        spectrum, f_oth, courant, courant_oth, sea_mask, in_hbm(interaction), sides_own, sides_oth, wave
     )
     currents_out = call(
         momentum_kernel,
         "momentum",
         jax.ShapeDtypeStruct(currents.shape, F32),
-        [VMEM] * 2 + [HBM] * 2 + [VMEM] * 7 + [SMEM],
+        [VMEM] * 10 + [SMEM],
         HBM,
         [
-            pltpu.VMEM((cells_x, chans, cells_y), F32),
-            pltpu.VMEM(sea_mask.shape, jnp.int32),
             pltpu.VMEM((cells_x + 2 * SUBSTEPS, fields, 2 * cells_y), F32),
             pltpu.VMEM((cells_x + 2 * SUBSTEPS, chans, 2 * cells_y), F32),
             pltpu.VMEM((cells_x + 2 * SUBSTEPS - 2, chans, 2 * cells_y), F32),
-            pltpu.VMEM((cells_x, chans, cells_y), F32),
-            DMA,
-            DMA((cells_x, 2)),
-            DMA((2, cells_x)),
+            pltpu.VMEM(currents.shape, F32),
+            DMA((cells_x // TILE,)),
         ],
         10**8,
         4 * MIB,
         10,
     )(
-        s_main, s_aux, in_hbm(currents), in_hbm(sea_mask), west_own, east_own, from_a, from_b, from_w, from_e, token,
+        s_main, s_aux, state, west_own, east_own, from_a, from_b, from_w, from_e, token,
         level_drag,
     )
     return (wave_out, currents_out)

time: 37.1 us -> 32.3 us (0.87)
  waiting for transfers between devices: 3.49 us -> 0.02 us
  Pallas kernels: 19 us -> 17.7 us
    ppermute x1, waiting for transfers between devices: 2.99 us -> 0.01 us  [local(): from_b = lax.ppermute(to_b, 'gy', pairing('gy', 1))]
    pallas_call x1 -> x2, Pallas kernels: 6.96 us -> 9.72 us  [the longest x1 6.12 us: local(): call(functools.partial(outer_kernel, outer, inner), 'outer', (wave_type,...]
    pallas_call x1, Pallas kernels: 4.23 us -> 2.05 us  [local(): call(project_kernel, 'project', (jax.ShapeDtypeStruct((cells_x + 2, chans...]
    pallas_call x1, Pallas kernels: 5.67 us -> 3.83 us  [local(): call(momentum_kernel, 'momentum', jax.ShapeDtypeStruct(currents.shape, F3...]
    ppermute x1, waiting for transfers between devices: 0.48 us -> 0.01 us  [local(): east_own = lax.ppermute(to_w, 'gx', west)]
  transfers between devices with their start and end apart: 9 -> 9, of which waited for: 2 -> 0; matrix products, arithmetic and copies ran while one was open for 0% -> 0% of each run, Pallas kernels for 34% -> 42%
where the time goes in v5:
time: 32.3 us; the launch traced here: 31.8 us
  Pallas kernels  17.7 us (55%)
  starting transfers between devices  13.3 us (41%)
  between operations  0.8 us (2%)
    pallas_call x1, Pallas kernels, local(): call(functools.partial(outer_kernel, outer, inner), 'outer', (wave_type,...  6.12 us
    pallas_call x1, Pallas kernels, local(): call(momentum_kernel, 'momentum', jax.ShapeDtypeStruct(currents.shape, F3...  3.83 us
    pallas_call x1, Pallas kernels, local(): call(functools.partial(inner_kernel, inner), 'inner', (wave_type, token_t...  3.6 us
    ppermute x1, starting transfers between devices, local(): from_e = lax.ppermute(to_w, 'gx', west)  3.26 us
    ppermute x1, starting transfers between devices, local(): sides_oth = lax.ppermute(sides_own, 'comp', swap)  2.38 us
    ppermute x1, starting transfers between devices, local(): east_own = lax.ppermute(to_w, 'gx', west)  2.09 us
    ppermute x1, starting transfers between devices, local(): from_b = lax.ppermute(to_b, 'gy', pairing('gy', 1))  2.09 us
    pallas_call x1, Pallas kernels, local(): call(project_kernel, 'project', (jax.ShapeDtypeStruct((cells_x + 2, chans...  2.05 us
  transfers between devices with their start and end apart: 9, of which 0 were waited for; matrix products, arithmetic and copies ran while one was open for 0% of the time, Pallas kernels for 42%

profile of v5, /device:TPU:5, one launch (start us, length us, event | category | flops | bytes accessed | tf_op | source)
XLA Modules:
  0.0 31.8 jit_solution(8114163942441406441)
XLA Ops:
  0.6 0.0 copy-start
  0.6 0.0 copy-start.3
  0.7 0.0 copy-start.2
  0.7 0.0 copy-start.1
  0.7 0.7 %collective-permute-start = (bf16[16,128,512]{2,1,0:T(8,128)(2,1)}, bf16[16,128,512]{2,1,0:T(8,128)(2,1)S(1)}, u32[]{:S(2)}, u32[]{:S(2)}) collective-permute-start(bf16[16,128,512]{2,1,0:T(8,128)(2,1)} %f_own.5), channel_id=1, source_target_pairs={{0,1},{1,0},{2,3},{3,2},{4,5},{5,4},{6,7},{7,6},{8,9},{9,8},{10,11... | collective-permute-start | bytes 6291464 | tf_op jit(solution)/shard_map/ppermute | solution.py:577
  1.4 0.1 collective-permute-start.1
  1.5 1.5 %outgoing.1 = (bf16[752,128]{1,0:T(8,128)(2,1)S(1)}, bf16[752,128]{1,0:T(8,128)(2,1)S(1)}, bf16[2,64,1024]{2,1,0:T(8,128)(2,1)S(1)}) custom-call(bf16[16,128,512]{2,1,0:T(8,128)(2,1)} %f_own.5, f32[2,32,16,128]{3,2,1,0:T(8,128)} %currents.3, s32[16,128]{1,0:T(8,128)} %mask.5, bf16[2,64,1024]{2,1,0:T(8,128)(2,1)} %bitcast.1), custom_call_target="tpu_custom_call" | custom-call | flops 1000000 | bytes 1048576 | tf_op jit(solution)/shard_map/outgoing/pallas_call | solution.py:582
  3.0 1.3 %collective-permute-start.4 = (bf16[752,128]{1,0:T(8,128)(2,1)S(1)}, bf16[752,128]{1,0:T(8,128)(2,1)S(1)}, u32[]{:S(2)}, u32[]{:S(2)}) collective-permute-start(bf16[752,128]{1,0:T(8,128)(2,1)S(1)} %get-tuple-element.23), channel_id=1, source_target_pairs={{0,8},{8,16},{16,24},{24,0},{1,9},{9,17},{17,25},{25,1},{2,10},{10... | collective-permute-start | bytes 577544 | tf_op jit(solution)/shard_map/ppermute | solution.py:598
  4.3 2.1 %collective-permute-start.5 = (bf16[752,128]{1,0:T(8,128)(2,1)S(1)}, bf16[752,128]{1,0:T(8,128)(2,1)S(1)}, u32[]{:S(2)}, u32[]{:S(2)}) collective-permute-start(bf16[752,128]{1,0:T(8,128)(2,1)S(1)} %get-tuple-element.24), channel_id=1, source_target_pairs={{8,0},{16,8},{24,16},{0,24},{9,1},{17,9},{25,17},{1,25},{10,2},{18... | collective-permute-start | bytes 577544 | tf_op jit(solution)/shard_map/ppermute | solution.py:599
  6.4 0.0 collective-permute-done.1.courant_oth
  6.4 0.0 collective-permute-done.f_oth
  6.4 0.0 copy-done
  6.4 0.0 copy-done.3
  6.4 0.0 copy-done.2
  6.4 2.0 %project.1 = (f32[18,64,128]{2,1,0:T(8,128)S(1)}, f32[16,64,128]{2,1,0:T(8,128)S(1)}, f32[6,64,256]{2,1,0:T(8,128)S(1)}, f32[16,80,128]{2,1,0:T(8,128)S(1)}, bf1...) custom-call(bf16[16,128,512]{2,1,0:T(8,128)(2,1)S(1)} %copy-done, ...), custom_call_target="tpu_custom_call" | custom-call | flops 3000000000 | bytes 8388608 | tf_op jit(solution)/shard_map/project/pallas_call | solution.py:602
  8.5 1.3 %collective-permute-start.2 = (bf16[144,128]{1,0:T(8,128)(2,1)S(1)}, bf16[144,128]{1,0:T(8,128)(2,1)S(1)}, u32[]{:S(2)}, u32[]{:S(2)}) collective-permute-start(bf16[144,128]{1,0:T(8,128)(2,1)S(1)} %get-tuple-element.21), channel_id=1, source_target_pairs={{0,2},{4,6},{2,0},{6,4},{1,3},{5,7},{3,1},{7,5},{8,10},{12,14},{10... | collective-permute-start | bytes 110600 | tf_op jit(solution)/shard_map/ppermute | solution.py:627
  9.8 2.1 %collective-permute-start.3 = (bf16[144,128]{1,0:T(8,128)(2,1)S(1)}, bf16[144,128]{1,0:T(8,128)(2,1)S(1)}, u32[]{:S(2)}, u32[]{:S(2)}) collective-permute-start(bf16[144,128]{1,0:T(8,128)(2,1)S(1)} %get-tuple-element.22), channel_id=1, source_target_pairs={{2,4},{4,2},{3,5},{5,3},{10,12},{12,10},{11,13},{13,11},{18,20},{2... | collective-permute-start | bytes 110600 | tf_op jit(solution)/shard_map/ppermute | solution.py:628
  11.9 3.6 %inner.1 = (bf16[16,128,512]{2,1,0:T(8,128)(2,1)S(1)}, f32[8,128]{1,0:T(8,128)S(1)}) custom-call(bf16[16,128,512]{2,1,0:T(8,128)(2,1)S(1)} %copy-done, bf16[16,128,512]{2,1,0:T(8,128)(2,1)S(1)} %collective-permute-done.f_oth, f32[2,512]{1,0:T(2,128)S(1)} %copy-done.3, f32[2,512]{1,0:T(2,128)S(1)} %collective-permute-done.1.courant_oth, ...), custom_call_target="tpu_custom_call" | custom-call | flops 2000000000 | bytes 5242880 | tf_op jit(solution)/shard_map/inner/pallas_call | solution.py:643
  15.5 0.0 collective-permute-done.4.side_w
  15.5 0.0 collective-permute-done.5.side_e
  15.5 0.0 collective-permute-done.2.from_a
  15.5 0.0 collective-permute-done.3.from_b
  15.5 0.7 %relay.1 = (bf16[272,128]{1,0:T(8,128)(2,1)S(1)}, bf16[272,128]{1,0:T(8,128)(2,1)S(1)}, bf16[1152,128]{1,0:T(8,128)(2,1)S(1)}) custom-call(f32[6,64,256]{2,1,0:T(8,128)S(1)} %get-tuple-element.20.s_edge, bf16[144,128]{1,0:T(8,128)(2,1)S(1)} %collective-permute-done.2.from_a, bf16[144,128]{1,0:T(8,128)(2,1)S(1)} %collective-permute-done.3.from_b, ...), custom_call_target="tpu_custom_call" | custom-call | flops 1000000 | bytes 1048576 | tf_op jit(solution)/shard_map/relay/pallas_call | solution.py:655
  16.2 2.4 %collective-permute-start.6 = (bf16[1152,128]{1,0:T(8,128)(2,1)S(1)}, bf16[1152,128]{1,0:T(8,128)(2,1)S(1)}, u32[]{:S(2)}, u32[]{:S(2)}) collective-permute-start(bf16[1152,128]{1,0:T(8,128)(2,1)S(1)} %get-tuple-element.27.sides_own), channel_id=1, source_target_pairs={{0,1},{1,0},{2,3},{3,2},{4,5},{5,4},{6,7},{7,6},{8,9},{9,8},{10,11... | collective-permute-start | bytes 884744 | tf_op jit(solution)/shard_map/ppermute | solution.py:667
  18.6 0.0 collective-permute-start.7
  18.6 3.3 %collective-permute-start.8 = (bf16[272,128]{1,0:T(8,128)(2,1)S(1)}, bf16[272,128]{1,0:T(8,128)(2,1)S(1)}, u32[]{:S(2)}, u32[]{:S(2)}) collective-permute-start(bf16[272,128]{1,0:T(8,128)(2,1)S(1)} %get-tuple-element.34), channel_id=1, source_target_pairs={{8,0},{16,8},{24,16},{0,24},{9,1},{17,9},{25,17},{1,25},{10,2},{18... | collective-permute-start | bytes 208904 | tf_op jit(solution)/shard_map/ppermute | solution.py:669
  21.8 0.0 collective-permute-done.6.sides_oth
  21.8 6.1 %outer.1 = (bf16[16,128,512]{2,1,0:T(8,128)(2,1)}, f32[8,128]{1,0:T(8,128)S(1)}) custom-call(bf16[16,128,512]{2,1,0:T(8,128)(2,1)S(1)} %copy-done, bf16[16,128,512]{2,1,0:T(8,128)(2,1)S(1)} %collective-permute-done.f_oth, f32[2,512]{1,0:T(2,128)S(1)} %copy-done.3, f32[2,512]{1,0:T(2,128)S(1)} %collective-permute-done.1.courant_oth, s32[16,128]{1,0:T(8,128)S(1)} %copy-done.2, ...), custom_call_target="tpu_custom_call" | custom-call | flops 2000000000 | bytes 5242880 | tf_op jit(solution)/shard_map/outer/pallas_call | solution.py:671
  28.0 0.0 collective-permute-done.7.from_w
  28.0 0.0 collective-permute-done.8.from_e
  28.0 0.0 copy-done.4
  28.0 3.8 %momentum.1 = f32[2,32,16,128]{3,2,1,0:T(8,128)} custom-call(f32[18,64,128]{2,1,0:T(8,128)S(1)} %get-tuple-element.30.s_main, f32[16,64,128]{2,1,0:T(8,128)S(1)} %get-tuple-element.31.s_aux, f32[16,80,128]{2,1,0:T(8,128)S(1)} %get-tuple-element.32.state, bf16[752,128]{1,0:T(8,128)(2,1)S(1)} %collective-permute-done.4.side_w, ...), custom_call_target="tpu_custom_call" | custom-call | flops 100000000 | bytes 4194304 | tf_op jit(solution)/shard_map/momentum/pallas_call | solution.py:688
  (2 shorter events, 0.0 us)
Async XLA Ops:
  0.6 5.8 %copy-start = (bf16[16,128,512]{2,1,0:T(8,128)(2,1)S(1)}, bf16[16,128,512]{2,1,0:T(8,128)(2,1)}, u32[]{:S(2)}) copy-start(bf16[16,128,512]{2,1,0:T(8,128)(2,1)} %f_own.5) | copy-start | bytes 6291460
  0.6 5.8 %copy-start.3 = (f32[2,512]{1,0:T(2,128)S(1)}, f32[2,512]{1,0:T(2,128)}, u32[]{:S(2)}) copy-start(f32[2,512]{1,0:T(2,128)} %courant_own.5) | copy-start | bytes 12292
  0.7 5.8 %copy-start.2 = (s32[16,128]{1,0:T(8,128)S(1)}, s32[16,128]{1,0:T(8,128)}, u32[]{:S(2)}) copy-start(s32[16,128]{1,0:T(8,128)} %mask.5) | copy-start | bytes 24580
  0.7 5.8 %copy-start.1 = (f32[2,32,16,128]{3,2,1,0:T(8,128)S(1)}, f32[2,32,16,128]{3,2,1,0:T(8,128)}, u32[]{:S(2)}) copy-start(f32[2,32,16,128]{3,2,1,0:T(8,128)} %currents.3) | copy-start | bytes 1572868
  0.7 5.7 %collective-permute-start = (bf16[16,128,512]{2,1,0:T(8,128)(2,1)}, bf16[16,128,512]{2,1,0:T(8,128)(2,1)S(1)}, u32[]{:S(2)}, u32[]{:S(2)}) collective-permute-start(bf16[16,128,512]{2,1,0:T(8,128)(2,1)} %f_own.5), channel_id=1, source_target_pairs={{0,1},{1,0},{2,3},{3,2},{4,5},{5,4},{6,7},{7,6},{8,9},{9,8},{10,11... | collective-permute-start | bytes 6291464 | tf_op jit(solution)/shard_map/ppermute | solution.py:577
  1.4 5.0 %collective-permute-start.1 = (f32[2,512]{1,0:T(2,128)}, f32[2,512]{1,0:T(2,128)S(1)}, u32[]{:S(2)}, u32[]{:S(2)}) collective-permute-start(f32[2,512]{1,0:T(2,128)} %courant_own.5), channel_id=1, source_target_pairs={{0,1},{1,0},{2,3},{3,2},{4,5},{5,4},{6,7},{7,6},{8,9},{9,8},{10,11... | collective-permute-start | bytes 12296 | tf_op jit(solution)/shard_map/ppermute | solution.py:578
  3.0 12.5 %collective-permute-start.4 = (bf16[752,128]{1,0:T(8,128)(2,1)S(1)}, bf16[752,128]{1,0:T(8,128)(2,1)S(1)}, u32[]{:S(2)}, u32[]{:S(2)}) collective-permute-start(bf16[752,128]{1,0:T(8,128)(2,1)S(1)} %get-tuple-element.23), channel_id=1, source_target_pairs={{0,8},{8,16},{16,24},{24,0},{1,9},{9,17},{17,25},{25,1},{2,10},{10... | collective-permute-start | bytes 577544 | tf_op jit(solution)/shard_map/ppermute | solution.py:598
  4.3 11.2 %collective-permute-start.5 = (bf16[752,128]{1,0:T(8,128)(2,1)S(1)}, bf16[752,128]{1,0:T(8,128)(2,1)S(1)}, u32[]{:S(2)}, u32[]{:S(2)}) collective-permute-start(bf16[752,128]{1,0:T(8,128)(2,1)S(1)} %get-tuple-element.24), channel_id=1, source_target_pairs={{8,0},{16,8},{24,16},{0,24},{9,1},{17,9},{25,17},{1,25},{10,2},{18... | collective-permute-start | bytes 577544 | tf_op jit(solution)/shard_map/ppermute | solution.py:599
  8.5 7.0 %collective-permute-start.2 = (bf16[144,128]{1,0:T(8,128)(2,1)S(1)}, bf16[144,128]{1,0:T(8,128)(2,1)S(1)}, u32[]{:S(2)}, u32[]{:S(2)}) collective-permute-start(bf16[144,128]{1,0:T(8,128)(2,1)S(1)} %get-tuple-element.21), channel_id=1, source_target_pairs={{0,2},{4,6},{2,0},{6,4},{1,3},{5,7},{3,1},{7,5},{8,10},{12,14},{10... | collective-permute-start | bytes 110600 | tf_op jit(solution)/shard_map/ppermute | solution.py:627
  9.8 5.7 %collective-permute-start.3 = (bf16[144,128]{1,0:T(8,128)(2,1)S(1)}, bf16[144,128]{1,0:T(8,128)(2,1)S(1)}, u32[]{:S(2)}, u32[]{:S(2)}) collective-permute-start(bf16[144,128]{1,0:T(8,128)(2,1)S(1)} %get-tuple-element.22), channel_id=1, source_target_pairs={{2,4},{4,2},{3,5},{5,3},{10,12},{12,10},{11,13},{13,11},{18,20},{2... | collective-permute-start | bytes 110600 | tf_op jit(solution)/shard_map/ppermute | solution.py:628
  16.2 5.6 %collective-permute-start.6 = (bf16[1152,128]{1,0:T(8,128)(2,1)S(1)}, bf16[1152,128]{1,0:T(8,128)(2,1)S(1)}, u32[]{:S(2)}, u32[]{:S(2)}) collective-permute-start(bf16[1152,128]{1,0:T(8,128)(2,1)S(1)} %get-tuple-element.27.sides_own), channel_id=1, source_target_pairs={{0,1},{1,0},{2,3},{3,2},{4,5},{5,4},{6,7},{7,6},{8,9},{9,8},{10,11... | collective-permute-start | bytes 884744 | tf_op jit(solution)/shard_map/ppermute | solution.py:667
  18.6 9.4 %collective-permute-start.7 = (bf16[272,128]{1,0:T(8,128)(2,1)S(1)}, bf16[272,128]{1,0:T(8,128)(2,1)S(1)}, u32[]{:S(2)}, u32[]{:S(2)}) collective-permute-start(bf16[272,128]{1,0:T(8,128)(2,1)S(1)} %get-tuple-element.33), channel_id=1, source_target_pairs={{0,8},{8,16},{16,24},{24,0},{1,9},{9,17},{17,25},{25,1},{2,10},{10... | collective-permute-start | bytes 208904 | tf_op jit(solution)/shard_map/ppermute | solution.py:668
  18.6 9.4 %collective-permute-start.8 = (bf16[272,128]{1,0:T(8,128)(2,1)S(1)}, bf16[272,128]{1,0:T(8,128)(2,1)S(1)}, u32[]{:S(2)}, u32[]{:S(2)}) collective-permute-start(bf16[272,128]{1,0:T(8,128)(2,1)S(1)} %get-tuple-element.34), channel_id=1, source_target_pairs={{8,0},{16,8},{24,16},{0,24},{9,1},{17,9},{25,17},{1,25},{10,2},{18... | collective-permute-start | bytes 208904 | tf_op jit(solution)/shard_map/ppermute | solution.py:669
  21.8 6.2 %copy-start.4 = (f32[32]{0:T(128)S(1)}, f32[32]{0:T(128)}, u32[]{:S(2)}) copy-start(f32[32]{0:T(128)} %drag.1) | copy-start | bytes 388

commit v6 on v5

--- a/solution.py
+++ b/solution.py
@@ -21,6 +21,7 @@
 CHUNK = 128
 TILE_ROWS = 16
 EARLY_PAIRS = 4
+SEAM_GROUP = 1
 TILE = 8
 PARTS = 5
 
@@ -368,17 +369,11 @@
 
 
 def wave_groups(cells_x, width, early_pairs):
-    inner = [[(x, TILE_ROWS, width - TILE_ROWS) for x in (1 + 2 * p, 2 + 2 * p)] for p in range(early_pairs)]
+    early = 1 + 2 * early_pairs
+    inner = [[(x, 0, width), (x + 1, 0, width)] for x in range(1, early, 2)]
     outer = [[(0, 0, width), (cells_x - 1, 0, width)]]
-    for x in range(1 + 2 * early_pairs, cells_x - 1, 2):
+    for x in range(early, cells_x - 1, 2):
         outer.append([(i, 0, width) for i in range(x, min(x + 2, cells_x - 1))])
-    seams = [
-        block
-        for x in range(1, 1 + 2 * early_pairs)
-        for block in ((x, 0, TILE_ROWS), (x, width - TILE_ROWS, width))
-    ]
-    step = 2 * width // TILE_ROWS
-    outer += [seams[i : i + step] for i in range(0, len(seams), step)]
     return inner, outer
 
 
@@ -387,25 +382,12 @@
 
 
 def wave_body(
-    groups, sides,
-    f_own, f_oth, courant_own, courant_oth, mask, interaction,
+    groups, sides, seam, wave, arriving,
+    f_own, f_oth, courant_own, courant_oth, mask, inter,
     slots, send,
-    inter, adv, sea, moved, inter_sem,
+    adv, sea, moved,
 ):
     cells_x, width, bins = f_own.shape
-    core = lax.axis_index("comp")
-    own_at, oth_at = pl.multiple_of(core * bins, bins), pl.multiple_of((1 - core) * bins, bins)
-    inter_copies = [
-        pltpu.make_async_copy(
-            interaction.at[pl.ds(at, bins), pl.ds(own_at, bins)],
-            inter.at[pl.ds(n * bins, bins)],
-            inter_sem.at[n],
-        )
-        for n, at in enumerate((own_at, oth_at))
-    ]
-    for copy in inter_copies:
-        copy.start()
-
     even = is_even("gy")
     per_core = bins // CHUNK
     halves = []
@@ -437,15 +419,12 @@
         rows, side, j, cols, south, north, c_mid, c_x, c_y, up_x, up_y = halves[n]
         row = 0
         for i, (x, first, last) in enumerate(groups[at]):
-            low_end, high_end = max(first - TILE_ROWS, 0), min(last + TILE_ROWS, width)
-            wide = cell(rows, side, j, cols, x, low_end, high_end)
-            mid = wide[first - low_end : last - low_end]
+            mid = cell(rows, side, j, cols, x, first, last)
             shifted = moved.at[(len(groups[at]) * n + i) % moved.shape[0]]
-            shifted[8 + low_end : 8 + high_end] = wide
-            if first == 0:
-                shifted[7:8] = south[x : x + 1]
-            if last == width:
-                shifted[8 + width : 9 + width] = north[x : x + 1]
+            shifted[8 + first : 8 + last] = mid
+            none = jnp.zeros((1, CHUNK), F32)
+            shifted[7:8] = none if south is None else south[x : x + 1]
+            shifted[8 + width : 9 + width] = none if north is None else north[x : x + 1]
             low, high = shifted[7 + first : 7 + last], shifted[9 + first : 9 + last]
             west = cell(rows, side, j, cols, x - 1, first, last)
             east = cell(rows, side, j, cols, x + 1, first, last)
@@ -454,18 +433,46 @@
             adv[at % 2][row : row + height, n * CHUNK : (n + 1) * CHUNK] = value.astype(BF16)
             row += height
 
+    def advect_seam(n):
+        rows, _, _, cols, south, north, c_mid, c_x, c_y, up_x, up_y = halves[n]
+        around = range(seam[0] - 1, seam[-1] + 2)
+        own = slice(seam[0], seam[-1] + 1)
+        row = rows_of(groups[SEAM_GROUP])
+        for first, edge, beside in ((0, 0, 1), (width - TILE_ROWS, TILE_ROWS - 1, TILE_ROWS - 2)):
+            tiles = [rows[x, first : first + TILE_ROWS, cols].astype(F32) for x in around]
+            line = jnp.concatenate([tile[edge : edge + 1] for tile in tiles], 0)
+            inward = jnp.concatenate([tile[beside : beside + 1] for tile in tiles[1:-1]], 0)
+            low, high = (south[own], inward) if first == 0 else (inward, north[own])
+            value = (
+                c_mid * line[1:-1]
+                + c_x * jnp.where(up_x, line[:-2], line[2:])
+                + c_y * jnp.where(up_y, low, high)
+            )
+            value = jnp.concatenate([value, jnp.zeros((TILE_ROWS - len(seam), CHUNK), F32)], 0)
+            adv[SEAM_GROUP % 2][row : row + TILE_ROWS, n * CHUNK : (n + 1) * CHUNK] = value.astype(BF16)
+            row += TILE_ROWS
+
+    def height_of(at):
+        return rows_of(groups[at]) + (2 * TILE_ROWS if seam and at == SEAM_GROUP else 0)
+
     def put_sea(at):
         row = 0
         for x, first, last in groups[at]:
             column = jnp.transpose(sea_row(mask, x, CHUNK))
             sea[at % 2][row : row + last - first] = column[first:last]
             row += last - first
+        if seam and at == SEAM_GROUP:
+            for lat in (0, width - 1):
+                column = mask[seam[0] : seam[-1] + 1, lat : lat + 1].astype(F32)
+                column = jnp.concatenate([column, jnp.zeros((TILE_ROWS - len(seam), 1), F32)], 0)
+                sea[at % 2][row : row + TILE_ROWS] = jnp.broadcast_to(column, (TILE_ROWS, CHUNK))
+                row += TILE_ROWS
 
     def finish(at, piece):
         done, mine = adv[at % 2], sea[at % 2]
         half, block = piece // blocks, piece % blocks
-        middle = rows_of(groups[at]) // 2 // TILE_ROWS * TILE_ROWS
-        low, high = (0, middle) if half == 0 else (middle, rows_of(groups[at]))
+        middle = height_of(at) // 2 // TILE_ROWS * TILE_ROWS
+        low, high = (0, middle) if half == 0 else (middle, height_of(at))
         cols = slice(block * bins // blocks, (block + 1) * bins // blocks)
         gain = jnp.dot(done[low:high, :], inter[:, cols], preferred_element_type=F32)
         row = 0
@@ -478,13 +485,26 @@
                     total = done[begin:end, own].astype(F32) + gain[begin - low : end - low, c]
                     slots[x, lats, own] = (total * mine[begin:end]).astype(BF16)
             row += last - first
+        if seam and at == SEAM_GROUP and half == 1:
+            at_row = lax.broadcasted_iota(jnp.int32, (TILE_ROWS, CHUNK), 0)
+            for first, edge in ((0, 0), (width - TILE_ROWS, TILE_ROWS - 1)):
+                end = row + TILE_ROWS
+                for c in chunks_of(bins // blocks):
+                    own = slice(cols.start + c.start, cols.start + c.stop)
+                    total = done[row:end, own].astype(F32) + gain[row - low : end - low, c]
+                    total *= mine[row:end]
+                    for i, x in enumerate(seam):
+                        tile = wave[x, first : first + TILE_ROWS, own].astype(F32)
+                        tile = jnp.where(at_row == edge, total[i : i + 1], tile)
+                        slots[x, first : first + TILE_ROWS, own] = tile.astype(BF16)
+                row = end
 
     blocks = 2
     pieces = 2 * blocks
     parts = len(halves)
     for n in range(parts):
         advect(0, n)
-    for copy in inter_copies:
+    for copy in arriving:
         copy.wait()
     for at in range(1, len(groups) + 1):
         put_sea(at - 1)
@@ -492,6 +512,8 @@
             if at < len(groups):
                 for n in range(piece * parts // pieces, (piece + 1) * parts // pieces):
                     advect(at, n)
+                    if seam and at == SEAM_GROUP:
+                        advect_seam(n)
             finish(at - 1, piece)
         send(at - 1)
 
@@ -499,23 +521,36 @@
 def inner_kernel(
     groups,
     f_own, f_oth, courant_own, courant_oth, mask, interaction, token_in,
-    wave, token,
-    inter, adv_a, adv_b, sea_a, sea_b, moved, inter_sem,
+    wave, inter, token,
+    adv_a, adv_b, sea_a, sea_b, moved, inter_sem,
 ):
     token[...] = token_in[...]
+    bins = f_own.shape[2]
+    core = lax.axis_index("comp")
+    own_at, oth_at = pl.multiple_of(core * bins, bins), pl.multiple_of((1 - core) * bins, bins)
+    inter_copies = [
+        pltpu.make_async_copy(
+            interaction.at[pl.ds(at, bins), pl.ds(own_at, bins)],
+            inter.at[pl.ds(n * bins, bins)],
+            inter_sem.at[n],
+        )
+        for n, at in enumerate((own_at, oth_at))
+    ]
+    for copy in inter_copies:
+        copy.start()
     wave_body(
-        groups, (None, None),
-        f_own, f_oth, courant_own, courant_oth, mask, interaction,
+        groups, (None, None), (), None, inter_copies,
+        f_own, f_oth, courant_own, courant_oth, mask, inter,
         wave, lambda n: None,
-        inter, (adv_a, adv_b), (sea_a, sea_b), moved, inter_sem,
+        (adv_a, adv_b), (sea_a, sea_b), moved,
     )
 
 
 def outer_kernel(
     groups, groups_before,
-    f_own, f_oth, courant_own, courant_oth, mask, interaction, sides_own, sides_oth, wave,
+    f_own, f_oth, courant_own, courant_oth, mask, inter, sides_own, sides_oth, wave,
     out, token,
-    slots, inter, adv_a, adv_b, sea_a, sea_b, moved, inter_sem, out_sem,
+    slots, adv_a, adv_b, sea_a, sea_b, moved, out_sem,
 ):
     token[...] = jnp.zeros_like(token)
     copies = []
@@ -528,13 +563,21 @@
             )
             copies[-1].start()
 
-    for group in groups_before:
-        send(wave, group)
+    seam = [x for group in groups_before for x, _, _ in group]
+    width = wave.shape[1]
+    send(wave, [(x, TILE_ROWS, width - TILE_ROWS) for x in seam])
+    rims = [(0, TILE_ROWS), (width - TILE_ROWS, width)]
+
+    def sent(n):
+        send(slots, groups[n])
+        if n == SEAM_GROUP:
+            send(slots, [(x, first, last) for x in seam for first, last in rims])
+
     wave_body(
-        groups, (sides_own, sides_oth),
-        f_own, f_oth, courant_own, courant_oth, mask, interaction,
-        slots, lambda n: send(slots, groups[n]),
-        inter, (adv_a, adv_b), (sea_a, sea_b), moved, inter_sem,
+        groups, (sides_own, sides_oth), seam, wave, (),
+        f_own, f_oth, courant_own, courant_oth, mask, inter,
+        slots, sent,
+        (adv_a, adv_b), (sea_a, sea_b), moved,
     )
     for copy in copies:
         copy.wait()
@@ -631,22 +674,20 @@
     wave_type = jax.ShapeDtypeStruct(spectrum.shape, BF16)
 
     def wave_scratch(groups):
-        height = max(map(rows_of, groups))
+        height = max(map(rows_of, groups)) + 2 * TILE_ROWS
         return [
-            pltpu.VMEM((2 * bins, bins), BF16),
             *[pltpu.VMEM((height, 2 * bins), BF16)] * 2,
             *[pltpu.VMEM((height, CHUNK), F32)] * 2,
             pltpu.VMEM((16, cells_y + 16, CHUNK), F32),
-            DMA((2,)),
         ]
 
-    wave, token = call(
+    wave, inter, token = call(
         functools.partial(inner_kernel, inner),
         "inner",
-        (wave_type, token_type),
+        (wave_type, jax.ShapeDtypeStruct((2 * bins, bins), BF16), token_type),
         [VMEM] * 5 + [HBM, VMEM],
-        (VMEM,) * 2,
-        wave_scratch(inner),
+        (VMEM,) * 3,
+        [*wave_scratch(inner), DMA((2,))],
         2 * 10**9,
         5 * MIB,
         20,
@@ -672,18 +713,18 @@
         functools.partial(outer_kernel, outer, inner),
         "outer",
         (wave_type, token_type),
-        [VMEM] * 5 + [HBM] + [VMEM] * 3,
+        [VMEM] * 9,
         (HBM, VMEM),
         [
             pltpu.VMEM(spectrum.shape, BF16),
             *wave_scratch(outer),
-            DMA((sum(map(len, inner + outer)),)),
+            DMA((sum(map(len, outer)) + 3 * sum(map(len, inner)),)),
         ],
         2 * 10**9,
         5 * MIB,
         20,
     )(
-        spectrum, f_oth, courant, courant_oth, sea_mask, in_hbm(interaction), sides_own, sides_oth, wave
+        spectrum, f_oth, courant, courant_oth, sea_mask, inter, sides_own, sides_oth, wave
     )
     currents_out = call(
         momentum_kernel,

time: 32.3 us -> 31.3 us (0.969)
  the two profiles are of different devices: /device:TPU:5 before, /device:TPU:3 now
where the time goes in v6:
time: 31.3 us; the launch traced here: 31.1 us
  Pallas kernels  16.7 us (53%)
  starting transfers between devices  13.6 us (43%)
  between operations  0.8 us (3%)
    pallas_call x1, Pallas kernels, local(): call(functools.partial(outer_kernel, outer, inner), 'outer', (wave_type,...  4.54 us
    pallas_call x1, Pallas kernels, local(): call(functools.partial(inner_kernel, inner), 'inner', (wave_type, jax.Sha...  4.14 us
    ppermute x1, starting transfers between devices, local(): from_b = lax.ppermute(to_b, 'gy', pairing('gy', 1))  4.07 us
    pallas_call x1, Pallas kernels, local(): call(momentum_kernel, 'momentum', jax.ShapeDtypeStruct(currents.shape, F3...  3.83 us
    ppermute x1, starting transfers between devices, local(): from_e = lax.ppermute(to_w, 'gx', west)  3.26 us
    ppermute x1, starting transfers between devices, local(): east_own = lax.ppermute(to_w, 'gx', west)  2.09 us
    pallas_call x1, Pallas kernels, local(): call(project_kernel, 'project', (jax.ShapeDtypeStruct((cells_x + 2, chans...  2.05 us
    ppermute x1, starting transfers between devices, local(): sides_oth = lax.ppermute(sides_own, 'comp', swap)  1.66 us
  transfers between devices with their start and end apart: 9, of which 0 were waited for; matrix products, arithmetic and copies ran while one was open for 0% of the time, Pallas kernels for 39%

profile of v6, /device:TPU:3, one launch (start us, length us, event | category | flops | bytes accessed | tf_op | source)
XLA Modules:
  0.0 31.1 jit_solution(12289079965480473468)
XLA Ops:
  0.6 0.0 copy-start
  0.6 0.0 copy-start.3
  0.7 0.0 copy-start.2
  0.7 0.0 copy-start.1
  0.7 0.7 %collective-permute-start = (bf16[16,128,512]{2,1,0:T(8,128)(2,1)}, bf16[16,128,512]{2,1,0:T(8,128)(2,1)S(1)}, u32[]{:S(2)}, u32[]{:S(2)}) collective-permute-start(bf16[16,128,512]{2,1,0:T(8,128)(2,1)} %f_own.5), channel_id=1, source_target_pairs={{0,1},{1,0},{2,3},{3,2},{4,5},{5,4},{6,7},{7,6},{8,9},{9,8},{10,11... | collective-permute-start | bytes 6291464 | tf_op jit(solution)/shard_map/ppermute | solution.py:620
  1.4 0.1 collective-permute-start.1
  1.5 1.5 %outgoing.1 = (bf16[752,128]{1,0:T(8,128)(2,1)S(1)}, bf16[752,128]{1,0:T(8,128)(2,1)S(1)}, bf16[2,64,1024]{2,1,0:T(8,128)(2,1)S(1)}) custom-call(bf16[16,128,512]{2,1,0:T(8,128)(2,1)} %f_own.5, f32[2,32,16,128]{3,2,1,0:T(8,128)} %currents.3, s32[16,128]{1,0:T(8,128)} %mask.5, bf16[2,64,1024]{2,1,0:T(8,128)(2,1)} %bitcast.1), custom_call_target="tpu_custom_call" | custom-call | flops 1000000 | bytes 1048576 | tf_op jit(solution)/shard_map/outgoing/pallas_call | solution.py:625
  3.0 1.3 %collective-permute-start.4 = (bf16[752,128]{1,0:T(8,128)(2,1)S(1)}, bf16[752,128]{1,0:T(8,128)(2,1)S(1)}, u32[]{:S(2)}, u32[]{:S(2)}) collective-permute-start(bf16[752,128]{1,0:T(8,128)(2,1)S(1)} %get-tuple-element.26), channel_id=1, source_target_pairs={{0,8},{8,16},{16,24},{24,0},{1,9},{9,17},{17,25},{25,1},{2,10},{10... | collective-permute-start | bytes 577544 | tf_op jit(solution)/shard_map/ppermute | solution.py:641
  4.3 2.1 %collective-permute-start.5 = (bf16[752,128]{1,0:T(8,128)(2,1)S(1)}, bf16[752,128]{1,0:T(8,128)(2,1)S(1)}, u32[]{:S(2)}, u32[]{:S(2)}) collective-permute-start(bf16[752,128]{1,0:T(8,128)(2,1)S(1)} %get-tuple-element.27), channel_id=1, source_target_pairs={{8,0},{16,8},{24,16},{0,24},{9,1},{17,9},{25,17},{1,25},{10,2},{18... | collective-permute-start | bytes 577544 | tf_op jit(solution)/shard_map/ppermute | solution.py:642
  6.4 0.0 collective-permute-done.1.courant_oth
  6.4 0.0 collective-permute-done.f_oth
  6.4 0.0 copy-done
  6.4 0.0 copy-done.3
  6.4 0.0 copy-done.2
  6.4 0.0 copy-done.1
  6.4 2.1 %project.1 = (f32[18,64,128]{2,1,0:T(8,128)S(1)}, f32[16,64,128]{2,1,0:T(8,128)S(1)}, f32[6,64,256]{2,1,0:T(8,128)S(1)}, f32[16,80,128]{2,1,0:T(8,128)S(1)}, bf1...) custom-call(bf16[16,128,512]{2,1,0:T(8,128)(2,1)S(1)} %copy-done, ...), custom_call_target="tpu_custom_call" | custom-call | flops 3000000000 | bytes 8388608 | tf_op jit(solution)/shard_map/project/pallas_call | solution.py:645
  8.5 0.3 %collective-permute-start.2 = (bf16[144,128]{1,0:T(8,128)(2,1)S(1)}, bf16[144,128]{1,0:T(8,128)(2,1)S(1)}, u32[]{:S(2)}, u32[]{:S(2)}) collective-permute-start(bf16[144,128]{1,0:T(8,128)(2,1)S(1)} %get-tuple-element.24), channel_id=1, source_target_pairs={{0,2},{4,6},{2,0},{6,4},{1,3},{5,7},{3,1},{7,5},{8,10},{12,14},{10... | collective-permute-start | bytes 110600 | tf_op jit(solution)/shard_map/ppermute | solution.py:670
  8.8 4.1 %collective-permute-start.3 = (bf16[144,128]{1,0:T(8,128)(2,1)S(1)}, bf16[144,128]{1,0:T(8,128)(2,1)S(1)}, u32[]{:S(2)}, u32[]{:S(2)}) collective-permute-start(bf16[144,128]{1,0:T(8,128)(2,1)S(1)} %get-tuple-element.25), channel_id=1, source_target_pairs={{2,4},{4,2},{3,5},{5,3},{10,12},{12,10},{11,13},{13,11},{18,20},{2... | collective-permute-start | bytes 110600 | tf_op jit(solution)/shard_map/ppermute | solution.py:671
  12.9 4.1 %inner.1 = (bf16[16,128,512]{2,1,0:T(8,128)(2,1)S(1)}, bf16[1024,512]{1,0:T(8,128)(2,1)S(1)}, f32[8,128]{1,0:T(8,128)S(1)}) custom-call(bf16[16,128,512]{2,1,0:T(8,128)(2,1)S(1)} %copy-done, bf16[16,128,512]{2,1,0:T(8,128)(2,1)S(1)} %collective-permute-done.f_oth, f32[2,512]{1,0:T(2,128)S(1)} %copy-done.3, f32[2,512]{1,0:T(2,128)S(1)} %collective-permute-done.1.courant_oth, ...), custom_call_target="tpu_custom_call" | custom-call | flops 2000000000 | bytes 5242880 | tf_op jit(solution)/shard_map/inner/pallas_call | solution.py:684
  17.0 0.0 collective-permute-done.4.side_w
  17.1 0.0 collective-permute-done.5.side_e
  17.1 0.0 collective-permute-done.2.from_a
  17.1 0.0 collective-permute-done.3.from_b
  17.1 0.7 %relay.1 = (bf16[272,128]{1,0:T(8,128)(2,1)S(1)}, bf16[272,128]{1,0:T(8,128)(2,1)S(1)}, bf16[1152,128]{1,0:T(8,128)(2,1)S(1)}) custom-call(f32[6,64,256]{2,1,0:T(8,128)S(1)} %get-tuple-element.23.s_edge, bf16[144,128]{1,0:T(8,128)(2,1)S(1)} %collective-permute-done.2.from_a, bf16[144,128]{1,0:T(8,128)(2,1)S(1)} %collective-permute-done.3.from_b, ...), custom_call_target="tpu_custom_call" | custom-call | flops 1000000 | bytes 1048576 | tf_op jit(solution)/shard_map/relay/pallas_call | solution.py:696
  17.7 1.7 %collective-permute-start.6 = (bf16[1152,128]{1,0:T(8,128)(2,1)S(1)}, bf16[1152,128]{1,0:T(8,128)(2,1)S(1)}, u32[]{:S(2)}, u32[]{:S(2)}) collective-permute-start(bf16[1152,128]{1,0:T(8,128)(2,1)S(1)} %get-tuple-element.29.sides_own), channel_id=1, source_target_pairs={{0,1},{1,0},{2,3},{3,2},{4,5},{5,4},{6,7},{7,6},{8,9},{9,8},{10,11... | collective-permute-start | bytes 884744 | tf_op jit(solution)/shard_map/ppermute | solution.py:708
  19.4 0.0 collective-permute-start.7
  19.4 3.3 %collective-permute-start.8 = (bf16[272,128]{1,0:T(8,128)(2,1)S(1)}, bf16[272,128]{1,0:T(8,128)(2,1)S(1)}, u32[]{:S(2)}, u32[]{:S(2)}) collective-permute-start(bf16[272,128]{1,0:T(8,128)(2,1)S(1)} %get-tuple-element.36), channel_id=1, source_target_pairs={{8,0},{16,8},{24,16},{0,24},{9,1},{17,9},{25,17},{1,25},{10,2},{18... | collective-permute-start | bytes 208904 | tf_op jit(solution)/shard_map/ppermute | solution.py:710
  22.7 0.0 collective-permute-done.6.sides_oth
  22.7 4.5 %outer.1 = (bf16[16,128,512]{2,1,0:T(8,128)(2,1)}, f32[8,128]{1,0:T(8,128)S(1)}) custom-call(bf16[16,128,512]{2,1,0:T(8,128)(2,1)S(1)} %copy-done, bf16[16,128,512]{2,1,0:T(8,128)(2,1)S(1)} %collective-permute-done.f_oth, f32[2,512]{1,0:T(2,128)S(1)} %copy-done.3, f32[2,512]{1,0:T(2,128)S(1)} %collective-permute-done.1.courant_oth, s32[16,128]{1,0:T(8,128)S(1)} %copy-done.2, ...), custom_call_target="tpu_custom_call" | custom-call | flops 2000000000 | bytes 5242880 | tf_op jit(solution)/shard_map/outer/pallas_call | solution.py:712
  27.2 0.0 collective-permute-done.7.from_w
  27.2 0.0 collective-permute-done.8.from_e
  27.3 3.8 %momentum.1 = f32[2,32,16,128]{3,2,1,0:T(8,128)} custom-call(f32[18,64,128]{2,1,0:T(8,128)S(1)} %get-tuple-element.32.s_main, f32[16,64,128]{2,1,0:T(8,128)S(1)} %get-tuple-element.33.s_aux, f32[16,80,128]{2,1,0:T(8,128)S(1)} %get-tuple-element.34.state, bf16[752,128]{1,0:T(8,128)(2,1)S(1)} %collective-permute-done.4.side_w, ...), custom_call_target="tpu_custom_call" | custom-call | flops 100000000 | bytes 4194304 | tf_op jit(solution)/shard_map/momentum/pallas_call | solution.py:729
  (2 shorter events, 0.0 us)
Async XLA Ops:
  0.6 5.8 %copy-start = (bf16[16,128,512]{2,1,0:T(8,128)(2,1)S(1)}, bf16[16,128,512]{2,1,0:T(8,128)(2,1)}, u32[]{:S(2)}) copy-start(bf16[16,128,512]{2,1,0:T(8,128)(2,1)} %f_own.5) | copy-start | bytes 6291460
  0.6 5.8 %copy-start.3 = (f32[2,512]{1,0:T(2,128)S(1)}, f32[2,512]{1,0:T(2,128)}, u32[]{:S(2)}) copy-start(f32[2,512]{1,0:T(2,128)} %courant_own.5) | copy-start | bytes 12292
  0.7 5.8 %copy-start.2 = (s32[16,128]{1,0:T(8,128)S(1)}, s32[16,128]{1,0:T(8,128)}, u32[]{:S(2)}) copy-start(s32[16,128]{1,0:T(8,128)} %mask.5) | copy-start | bytes 24580
  0.7 5.8 %copy-start.1 = (f32[2,32,16,128]{3,2,1,0:T(8,128)S(1)}, f32[2,32,16,128]{3,2,1,0:T(8,128)}, u32[]{:S(2)}) copy-start(f32[2,32,16,128]{3,2,1,0:T(8,128)} %currents.3) | copy-start | bytes 1572868
  0.7 5.7 %collective-permute-start = (bf16[16,128,512]{2,1,0:T(8,128)(2,1)}, bf16[16,128,512]{2,1,0:T(8,128)(2,1)S(1)}, u32[]{:S(2)}, u32[]{:S(2)}) collective-permute-start(bf16[16,128,512]{2,1,0:T(8,128)(2,1)} %f_own.5), channel_id=1, source_target_pairs={{0,1},{1,0},{2,3},{3,2},{4,5},{5,4},{6,7},{7,6},{8,9},{9,8},{10,11... | collective-permute-start | bytes 6291464 | tf_op jit(solution)/shard_map/ppermute | solution.py:620
  1.4 5.0 %collective-permute-start.1 = (f32[2,512]{1,0:T(2,128)}, f32[2,512]{1,0:T(2,128)S(1)}, u32[]{:S(2)}, u32[]{:S(2)}) collective-permute-start(f32[2,512]{1,0:T(2,128)} %courant_own.5), channel_id=1, source_target_pairs={{0,1},{1,0},{2,3},{3,2},{4,5},{5,4},{6,7},{7,6},{8,9},{9,8},{10,11... | collective-permute-start | bytes 12296 | tf_op jit(solution)/shard_map/ppermute | solution.py:621
  3.0 14.1 %collective-permute-start.4 = (bf16[752,128]{1,0:T(8,128)(2,1)S(1)}, bf16[752,128]{1,0:T(8,128)(2,1)S(1)}, u32[]{:S(2)}, u32[]{:S(2)}) collective-permute-start(bf16[752,128]{1,0:T(8,128)(2,1)S(1)} %get-tuple-element.26), channel_id=1, source_target_pairs={{0,8},{8,16},{16,24},{24,0},{1,9},{9,17},{17,25},{25,1},{2,10},{10... | collective-permute-start | bytes 577544 | tf_op jit(solution)/shard_map/ppermute | solution.py:641
  4.3 12.8 %collective-permute-start.5 = (bf16[752,128]{1,0:T(8,128)(2,1)S(1)}, bf16[752,128]{1,0:T(8,128)(2,1)S(1)}, u32[]{:S(2)}, u32[]{:S(2)}) collective-permute-start(bf16[752,128]{1,0:T(8,128)(2,1)S(1)} %get-tuple-element.27), channel_id=1, source_target_pairs={{8,0},{16,8},{24,16},{0,24},{9,1},{17,9},{25,17},{1,25},{10,2},{18... | collective-permute-start | bytes 577544 | tf_op jit(solution)/shard_map/ppermute | solution.py:642
  8.5 8.6 %collective-permute-start.2 = (bf16[144,128]{1,0:T(8,128)(2,1)S(1)}, bf16[144,128]{1,0:T(8,128)(2,1)S(1)}, u32[]{:S(2)}, u32[]{:S(2)}) collective-permute-start(bf16[144,128]{1,0:T(8,128)(2,1)S(1)} %get-tuple-element.24), channel_id=1, source_target_pairs={{0,2},{4,6},{2,0},{6,4},{1,3},{5,7},{3,1},{7,5},{8,10},{12,14},{10... | collective-permute-start | bytes 110600 | tf_op jit(solution)/shard_map/ppermute | solution.py:670
  8.8 8.3 %collective-permute-start.3 = (bf16[144,128]{1,0:T(8,128)(2,1)S(1)}, bf16[144,128]{1,0:T(8,128)(2,1)S(1)}, u32[]{:S(2)}, u32[]{:S(2)}) collective-permute-start(bf16[144,128]{1,0:T(8,128)(2,1)S(1)} %get-tuple-element.25), channel_id=1, source_target_pairs={{2,4},{4,2},{3,5},{5,3},{10,12},{12,10},{11,13},{13,11},{18,20},{2... | collective-permute-start | bytes 110600 | tf_op jit(solution)/shard_map/ppermute | solution.py:671
  17.7 4.9 %collective-permute-start.6 = (bf16[1152,128]{1,0:T(8,128)(2,1)S(1)}, bf16[1152,128]{1,0:T(8,128)(2,1)S(1)}, u32[]{:S(2)}, u32[]{:S(2)}) collective-permute-start(bf16[1152,128]{1,0:T(8,128)(2,1)S(1)} %get-tuple-element.29.sides_own), channel_id=1, source_target_pairs={{0,1},{1,0},{2,3},{3,2},{4,5},{5,4},{6,7},{7,6},{8,9},{9,8},{10,11... | collective-permute-start | bytes 884744 | tf_op jit(solution)/shard_map/ppermute | solution.py:708
  19.4 7.8 %collective-permute-start.7 = (bf16[272,128]{1,0:T(8,128)(2,1)S(1)}, bf16[272,128]{1,0:T(8,128)(2,1)S(1)}, u32[]{:S(2)}, u32[]{:S(2)}) collective-permute-start(bf16[272,128]{1,0:T(8,128)(2,1)S(1)} %get-tuple-element.35), channel_id=1, source_target_pairs={{0,8},{8,16},{16,24},{24,0},{1,9},{9,17},{17,25},{25,1},{2,10},{10... | collective-permute-start | bytes 208904 | tf_op jit(solution)/shard_map/ppermute | solution.py:709
  19.4 7.8 %collective-permute-start.8 = (bf16[272,128]{1,0:T(8,128)(2,1)S(1)}, bf16[272,128]{1,0:T(8,128)(2,1)S(1)}, u32[]{:S(2)}, u32[]{:S(2)}) collective-permute-start(bf16[272,128]{1,0:T(8,128)(2,1)S(1)} %get-tuple-element.36), channel_id=1, source_target_pairs={{8,0},{16,8},{24,16},{0,24},{9,1},{17,9},{25,17},{1,25},{10,2},{18... | collective-permute-start | bytes 208904 | tf_op jit(solution)/shard_map/ppermute | solution.py:710
  22.7 4.6 %copy-start.4 = (f32[32]{0:T(128)S(1)}, f32[32]{0:T(128)}, u32[]{:S(2)}) copy-start(f32[32]{0:T(128)} %drag.1) | copy-start | bytes 388

commit v7 on v6

--- a/solution.py
+++ b/solution.py
@@ -20,7 +20,7 @@
 SLOT = 8
 CHUNK = 128
 TILE_ROWS = 16
-EARLY_PAIRS = 4
+EARLY_PAIRS = 3
 SEAM_GROUP = 1
 TILE = 8
 PARTS = 5
@@ -32,8 +32,9 @@
     return forward, [(target, source) for source, target in forward]
 
 
-def pairing(axis, first):
-    swaps = [(i, i + 1) for i in range(first, lax.axis_size(axis) - 1, 2)]
+def pairing(axis, first, periodic=False):
+    count = lax.axis_size(axis)
+    swaps = [(i, (i + 1) % count) for i in range(first, count if periodic else count - 1, 2)]
     return swaps + [(target, source) for source, target in swaps]
 
 
@@ -188,8 +189,8 @@
     return lax.rem(lax.axis_index(axis), 2) == 0
 
 
-def from_sides(from_a, from_b, rows):
-    even = is_even("gy")
+def from_sides(from_a, from_b, rows, axis="gy"):
+    even = is_even(axis)
     a, b = from_a[rows].astype(F32), from_b[rows].astype(F32)
     return jnp.where(even, b, a), jnp.where(even, a, b)
 
@@ -227,7 +228,7 @@
     return main, aux + halo_lanes(lane, low, high, width)
 
 
-def relay_kernel(cells_x, s_edge, from_a, from_b, side_w, side_e, token, msg_e, msg_w, spectra):
+def relay_kernel(cells_x, s_edge, from_a, from_b, side_w, side_e, token, msg_b, msg_a, spectra):
     del token
     chans, width = s_edge.shape[1], s_edge.shape[2] // 2
     fields = chans + MASK_ROWS
@@ -240,27 +241,32 @@
     lane = lane_of(chans, width)
     lane_f = lane_of(fields, width)
     tile_s, tile_n = from_sides(from_a, from_b, slice(0, fields))
-    for msg, first, first_cur, first_edge in (
-        (msg_e, cells_x - 2, cells_x - EDGE, EDGE),
-        (msg_w, -1, 0, 0),
-    ):
-        tile = jnp.zeros((chans, width), F32)
-        cur_tile = jnp.zeros((fields, width), F32)
-        for i in range(EDGE):
-            edge = s_edge[first_edge + i]
-            start = stokes_lane(first + i)
-            main, aux = stokes_row(
-                edge[:, :width], edge[:, width:], tile_s[:chans], tile_n[:chans], start, lane, width
-            )
-            msg[i * chans : (i + 1) * chans] = main.astype(BF16)
-            at = SLOT * i
-            tile = jnp.where(between(lane, at, at + 6), pltpu.roll(aux, at + 3, 1), tile)
-            ring = current_halo(tile_s, tile_n, first_cur + i, cells_x, lane_f, width)
-            at += half
-            cur_tile = jnp.where(between(lane_f, at, at + 6), pltpu.roll(ring, at + 3, 1), cur_tile)
-        base = EDGE * chans
-        msg[base : base + chans] = (tile + cur_tile[:chans]).astype(BF16)
-        msg[base + chans : base + fields] = cur_tile[chans:].astype(BF16)
+    def build(east, west):
+        for msg, first, first_cur, first_edge in (
+            (east, cells_x - 2, cells_x - EDGE, EDGE),
+            (west, -1, 0, 0),
+        ):
+            tile = jnp.zeros((chans, width), F32)
+            cur_tile = jnp.zeros((fields, width), F32)
+            for i in range(EDGE):
+                edge = s_edge[first_edge + i]
+                start = stokes_lane(first + i)
+                main, aux = stokes_row(
+                    edge[:, :width], edge[:, width:], tile_s[:chans], tile_n[:chans], start, lane, width
+                )
+                msg[i * chans : (i + 1) * chans] = main.astype(BF16)
+                at = SLOT * i
+                tile = jnp.where(between(lane, at, at + 6), pltpu.roll(aux, at + 3, 1), tile)
+                ring = current_halo(tile_s, tile_n, first_cur + i, cells_x, lane_f, width)
+                at += half
+                cur_tile = jnp.where(between(lane_f, at, at + 6), pltpu.roll(ring, at + 3, 1), cur_tile)
+            base = EDGE * chans
+            msg[base : base + chans] = (tile + cur_tile[:chans]).astype(BF16)
+            msg[base + chans : base + fields] = cur_tile[chans:].astype(BF16)
+
+    even = is_even("gx")
+    pl.when(even)(functools.partial(build, msg_a, msg_b))
+    pl.when(~even)(functools.partial(build, msg_b, msg_a))
 
 
 def lat_coriolis(cells_y):
@@ -272,7 +278,7 @@
 
 
 def momentum_kernel(
-    s_main, s_aux, state, side_w, side_e, from_a, from_b, from_w, from_e, token, drag,
+    s_main, s_aux, state, side_w, side_e, from_a, from_b, beside_b, beside_a, token, drag,
     out,
     flow_a, flow_b, stokes, result, sem,
 ):
@@ -284,7 +290,8 @@
     lane = lane_of(chans, width)
     lane_f = lane_of(fields, width)
     side_base = side_w.shape[0] - EDGE * fields
-    corner_w, corner_e = from_w[EDGE * chans :].astype(F32), from_e[EDGE * chans :].astype(F32)
+    corner_w, corner_e = from_sides(beside_a, beside_b, slice(EDGE * chans, None), "gx")
+    sums_w, sums_e = from_sides(beside_a, beside_b, slice(0, EDGE * chans), "gx")
     tile_s, tile_n = from_sides(from_a, from_b, slice(0, fields))
 
     def corner(tile, at, lanes):
@@ -310,10 +317,10 @@
             main, aux = stokes_row(
                 s_main[x + 1], own_aux, tile_s[:chans], tile_n[:chans], stokes_lane(x), lane, width
             )
-        for message, tile, first in ((from_w, corner_w, -2), (from_e, corner_e, cells_x - 1)):
+        for message, tile, first in ((sums_w, corner_w, -2), (sums_e, corner_e, cells_x - 1)):
             i = x - first
             if 0 <= i < EDGE:
-                main += message[i * chans : (i + 1) * chans].astype(F32)
+                main += message[i * chans : (i + 1) * chans]
                 aux += corner(tile[:chans], SLOT * i, lane)
         sea = flow_a[x + SUBSTEPS, chans : chans + 1, :]
         stokes[x + margin, :, :width] = main * sea[:, :width]
@@ -693,7 +700,7 @@
         20,
     )(spectrum, f_oth, courant, courant_oth, sea_mask, in_hbm(interaction), token)
 
-    to_e, to_w, sides_own = call(
+    to_b, to_a, sides_own = call(
         functools.partial(relay_kernel, cells_x),
         "relay",
         (message(EDGE * chans + fields),) * 2
@@ -706,8 +713,8 @@
         4,
     )(s_edge, from_a, from_b, west_own, east_own, token)
     sides_oth = lax.ppermute(sides_own, "comp", swap)
-    from_w = lax.ppermute(to_e, "gx", east)
-    from_e = lax.ppermute(to_w, "gx", west)
+    beside_b = lax.ppermute(to_b, "gx", pairing("gx", 1, True))
+    beside_a = lax.ppermute(to_a, "gx", pairing("gx", 0, True))
 
     wave_out, token = call(
         functools.partial(outer_kernel, outer, inner),
@@ -743,7 +750,7 @@
         4 * MIB,
         10,
     )(
-        s_main, s_aux, state, west_own, east_own, from_a, from_b, from_w, from_e, token,
+        s_main, s_aux, state, west_own, east_own, from_a, from_b, beside_b, beside_a, token,
         level_drag,
     )
     return (wave_out, currents_out)

time: 31.3 us -> 29.8 us (0.952)
  the two profiles are of different devices: /device:TPU:3 before, /device:TPU:5 now
where the time goes in v7:
time: 29.8 us; the launch traced here: 29.6 us
  Pallas kernels  16.7 us (56%)
  starting transfers between devices  11.8 us (40%)
  between operations  0.78 us (3%)
  waiting for transfers between devices  0.3 us (1%)
    pallas_call x1, Pallas kernels, local(): call(functools.partial(outer_kernel, outer, inner), 'outer', (wave_type,...  5.23 us
    pallas_call x1, Pallas kernels, local(): call(momentum_kernel, 'momentum', jax.ShapeDtypeStruct(currents.shape, F3...  3.87 us
    pallas_call x1, Pallas kernels, local(): call(functools.partial(inner_kernel, inner), 'inner', (wave_type, jax.Sha...  3.35 us
    ppermute x1, starting transfers between devices, local(): sides_oth = lax.ppermute(sides_own, 'comp', swap)  2.54 us
    ppermute x1, starting transfers between devices, local(): east_own = lax.ppermute(to_w, 'gx', west)  2.09 us
    ppermute x1, starting transfers between devices, local(): from_b = lax.ppermute(to_b, 'gy', pairing('gy', 1))  2.09 us
    pallas_call x1, Pallas kernels, local(): call(project_kernel, 'project', (jax.ShapeDtypeStruct((cells_x + 2, chans...  2.05 us
    ppermute x1, starting transfers between devices, local(): beside_b = lax.ppermute(to_b, 'gx', pairing('gx', 1, True))  1.66 us
  transfers between devices with their start and end apart: 9, of which 2 were waited for; matrix products, arithmetic and copies ran while one was open for 0% of the time, Pallas kernels for 41%

profile of v7, /device:TPU:5, one launch (start us, length us, event | category | flops | bytes accessed | tf_op | source)
XLA Modules:
  0.0 29.6 jit_solution(12249169496283502581)
XLA Ops:
  0.6 0.0 copy-start
  0.6 0.0 copy-start.3
  0.7 0.0 copy-start.2
  0.7 0.0 copy-start.1
  0.7 0.7 %collective-permute-start = (bf16[16,128,512]{2,1,0:T(8,128)(2,1)}, bf16[16,128,512]{2,1,0:T(8,128)(2,1)S(1)}, u32[]{:S(2)}, u32[]{:S(2)}) collective-permute-start(bf16[16,128,512]{2,1,0:T(8,128)(2,1)} %f_own.5), channel_id=1, source_target_pairs={{0,1},{1,0},{2,3},{3,2},{4,5},{5,4},{6,7},{7,6},{8,9},{9,8},{10,11... | collective-permute-start | bytes 6291464 | tf_op jit(solution)/shard_map/ppermute | solution.py:627
  1.4 0.1 collective-permute-start.1
  1.5 1.5 %outgoing.1 = (bf16[752,128]{1,0:T(8,128)(2,1)S(1)}, bf16[752,128]{1,0:T(8,128)(2,1)S(1)}, bf16[2,64,1024]{2,1,0:T(8,128)(2,1)S(1)}) custom-call(bf16[16,128,512]{2,1,0:T(8,128)(2,1)} %f_own.5, f32[2,32,16,128]{3,2,1,0:T(8,128)} %currents.3, s32[16,128]{1,0:T(8,128)} %mask.5, bf16[2,64,1024]{2,1,0:T(8,128)(2,1)} %bitcast.1), custom_call_target="tpu_custom_call" | custom-call | flops 1000000 | bytes 1048576 | tf_op jit(solution)/shard_map/outgoing/pallas_call | solution.py:632
  3.0 1.3 %collective-permute-start.4 = (bf16[752,128]{1,0:T(8,128)(2,1)S(1)}, bf16[752,128]{1,0:T(8,128)(2,1)S(1)}, u32[]{:S(2)}, u32[]{:S(2)}) collective-permute-start(bf16[752,128]{1,0:T(8,128)(2,1)S(1)} %get-tuple-element.26), channel_id=1, source_target_pairs={{0,8},{8,16},{16,24},{24,0},{1,9},{9,17},{17,25},{25,1},{2,10},{10... | collective-permute-start | bytes 577544 | tf_op jit(solution)/shard_map/ppermute | solution.py:648
  4.3 2.1 %collective-permute-start.5 = (bf16[752,128]{1,0:T(8,128)(2,1)S(1)}, bf16[752,128]{1,0:T(8,128)(2,1)S(1)}, u32[]{:S(2)}, u32[]{:S(2)}) collective-permute-start(bf16[752,128]{1,0:T(8,128)(2,1)S(1)} %get-tuple-element.27), channel_id=1, source_target_pairs={{8,0},{16,8},{24,16},{0,24},{9,1},{17,9},{25,17},{1,25},{10,2},{18... | collective-permute-start | bytes 577544 | tf_op jit(solution)/shard_map/ppermute | solution.py:649
  6.4 0.0 collective-permute-done.1.courant_oth
  6.4 0.0 collective-permute-done.f_oth
  6.4 0.0 copy-done
  6.4 0.0 copy-done.3
  6.4 0.0 copy-done.2
  6.4 0.0 copy-done.1
  6.4 2.0 %project.1 = (f32[18,64,128]{2,1,0:T(8,128)S(1)}, f32[16,64,128]{2,1,0:T(8,128)S(1)}, f32[6,64,256]{2,1,0:T(8,128)S(1)}, f32[16,80,128]{2,1,0:T(8,128)S(1)}, bf1...) custom-call(bf16[16,128,512]{2,1,0:T(8,128)(2,1)S(1)} %copy-done, ...), custom_call_target="tpu_custom_call" | custom-call | flops 3000000000 | bytes 8388608 | tf_op jit(solution)/shard_map/project/pallas_call | solution.py:652
  8.5 1.3 %collective-permute-start.2 = (bf16[144,128]{1,0:T(8,128)(2,1)S(1)}, bf16[144,128]{1,0:T(8,128)(2,1)S(1)}, u32[]{:S(2)}, u32[]{:S(2)}) collective-permute-start(bf16[144,128]{1,0:T(8,128)(2,1)S(1)} %get-tuple-element.24), channel_id=1, source_target_pairs={{0,2},{4,6},{2,0},{6,4},{1,3},{5,7},{3,1},{7,5},{8,10},{12,14},{10... | collective-permute-start | bytes 110600 | tf_op jit(solution)/shard_map/ppermute | solution.py:677
  9.8 2.1 %collective-permute-start.3 = (bf16[144,128]{1,0:T(8,128)(2,1)S(1)}, bf16[144,128]{1,0:T(8,128)(2,1)S(1)}, u32[]{:S(2)}, u32[]{:S(2)}) collective-permute-start(bf16[144,128]{1,0:T(8,128)(2,1)S(1)} %get-tuple-element.25), channel_id=1, source_target_pairs={{2,4},{4,2},{3,5},{5,3},{10,12},{12,10},{11,13},{13,11},{18,20},{2... | collective-permute-start | bytes 110600 | tf_op jit(solution)/shard_map/ppermute | solution.py:678
  11.9 3.4 %inner.1 = (bf16[16,128,512]{2,1,0:T(8,128)(2,1)S(1)}, bf16[1024,512]{1,0:T(8,128)(2,1)S(1)}, f32[8,128]{1,0:T(8,128)S(1)}) custom-call(bf16[16,128,512]{2,1,0:T(8,128)(2,1)S(1)} %copy-done, bf16[16,128,512]{2,1,0:T(8,128)(2,1)S(1)} %collective-permute-done.f_oth, f32[2,512]{1,0:T(2,128)S(1)} %copy-done.3, f32[2,512]{1,0:T(2,128)S(1)} %collective-permute-done.1.courant_oth, ...), custom_call_target="tpu_custom_call" | custom-call | flops 2000000000 | bytes 5242880 | tf_op jit(solution)/shard_map/inner/pallas_call | solution.py:691
  15.2 0.0 collective-permute-done.4.side_w
  15.2 0.0 collective-permute-done.5.side_e
  15.3 0.0 collective-permute-done.2.from_a
  15.3 0.1 collective-permute-done.3.from_b
  15.4 0.7 %relay.1 = (bf16[272,128]{1,0:T(8,128)(2,1)S(1)}, bf16[272,128]{1,0:T(8,128)(2,1)S(1)}, bf16[1152,128]{1,0:T(8,128)(2,1)S(1)}) custom-call(f32[6,64,256]{2,1,0:T(8,128)S(1)} %get-tuple-element.23.s_edge, bf16[144,128]{1,0:T(8,128)(2,1)S(1)} %collective-permute-done.2.from_a, bf16[144,128]{1,0:T(8,128)(2,1)S(1)} %collective-permute-done.3.from_b, ...), custom_call_target="tpu_custom_call" | custom-call | flops 1000000 | bytes 1048576 | tf_op jit(solution)/shard_map/relay/pallas_call | solution.py:703
  16.1 2.5 %collective-permute-start.6 = (bf16[1152,128]{1,0:T(8,128)(2,1)S(1)}, bf16[1152,128]{1,0:T(8,128)(2,1)S(1)}, u32[]{:S(2)}, u32[]{:S(2)}) collective-permute-start(bf16[1152,128]{1,0:T(8,128)(2,1)S(1)} %get-tuple-element.29.sides_own), channel_id=1, source_target_pairs={{0,1},{1,0},{2,3},{3,2},{4,5},{5,4},{6,7},{7,6},{8,9},{9,8},{10,11... | collective-permute-start | bytes 884744 | tf_op jit(solution)/shard_map/ppermute | solution.py:715
  18.6 1.7 %collective-permute-start.7 = (bf16[272,128]{1,0:T(8,128)(2,1)S(1)}, bf16[272,128]{1,0:T(8,128)(2,1)S(1)}, u32[]{:S(2)}, u32[]{:S(2)}) collective-permute-start(bf16[272,128]{1,0:T(8,128)(2,1)S(1)} %get-tuple-element.35), channel_id=1, source_target_pairs={{8,16},{24,0},{16,8},{0,24},{9,17},{25,1},{17,9},{1,25},{10,18},{2... | collective-permute-start | bytes 208904 | tf_op jit(solution)/shard_map/ppermute | solution.py:716
  20.3 0.0 collective-permute-start.8
  20.3 0.0 collective-permute-done.6.sides_oth
  20.3 5.2 %outer.1 = (bf16[16,128,512]{2,1,0:T(8,128)(2,1)}, f32[8,128]{1,0:T(8,128)S(1)}) custom-call(bf16[16,128,512]{2,1,0:T(8,128)(2,1)S(1)} %copy-done, bf16[16,128,512]{2,1,0:T(8,128)(2,1)S(1)} %collective-permute-done.f_oth, f32[2,512]{1,0:T(2,128)S(1)} %copy-done.3, f32[2,512]{1,0:T(2,128)S(1)} %collective-permute-done.1.courant_oth, s32[16,128]{1,0:T(8,128)S(1)} %copy-done.2, ...), custom_call_target="tpu_custom_call" | custom-call | flops 2000000000 | bytes 5242880 | tf_op jit(solution)/shard_map/outer/pallas_call | solution.py:719
  25.6 0.0 collective-permute-done.7.beside_b
  25.6 0.2 collective-permute-done.8.beside_a
  25.8 3.9 %momentum.1 = f32[2,32,16,128]{3,2,1,0:T(8,128)} custom-call(f32[18,64,128]{2,1,0:T(8,128)S(1)} %get-tuple-element.32.s_main, f32[16,64,128]{2,1,0:T(8,128)S(1)} %get-tuple-element.33.s_aux, f32[16,80,128]{2,1,0:T(8,128)S(1)} %get-tuple-element.34.state, bf16[752,128]{1,0:T(8,128)(2,1)S(1)} %collective-permute-done.4.side_w, ...), custom_call_target="tpu_custom_call" | custom-call | flops 100000000 | bytes 4194304 | tf_op jit(solution)/shard_map/momentum/pallas_call | solution.py:736
  (2 shorter events, 0.0 us)
Async XLA Ops:
  0.6 5.8 %copy-start = (bf16[16,128,512]{2,1,0:T(8,128)(2,1)S(1)}, bf16[16,128,512]{2,1,0:T(8,128)(2,1)}, u32[]{:S(2)}) copy-start(bf16[16,128,512]{2,1,0:T(8,128)(2,1)} %f_own.5) | copy-start | bytes 6291460
  0.6 5.8 %copy-start.3 = (f32[2,512]{1,0:T(2,128)S(1)}, f32[2,512]{1,0:T(2,128)}, u32[]{:S(2)}) copy-start(f32[2,512]{1,0:T(2,128)} %courant_own.5) | copy-start | bytes 12292
  0.7 5.8 %copy-start.2 = (s32[16,128]{1,0:T(8,128)S(1)}, s32[16,128]{1,0:T(8,128)}, u32[]{:S(2)}) copy-start(s32[16,128]{1,0:T(8,128)} %mask.5) | copy-start | bytes 24580
  0.7 5.8 %copy-start.1 = (f32[2,32,16,128]{3,2,1,0:T(8,128)S(1)}, f32[2,32,16,128]{3,2,1,0:T(8,128)}, u32[]{:S(2)}) copy-start(f32[2,32,16,128]{3,2,1,0:T(8,128)} %currents.3) | copy-start | bytes 1572868
  0.7 5.7 %collective-permute-start = (bf16[16,128,512]{2,1,0:T(8,128)(2,1)}, bf16[16,128,512]{2,1,0:T(8,128)(2,1)S(1)}, u32[]{:S(2)}, u32[]{:S(2)}) collective-permute-start(bf16[16,128,512]{2,1,0:T(8,128)(2,1)} %f_own.5), channel_id=1, source_target_pairs={{0,1},{1,0},{2,3},{3,2},{4,5},{5,4},{6,7},{7,6},{8,9},{9,8},{10,11... | collective-permute-start | bytes 6291464 | tf_op jit(solution)/shard_map/ppermute | solution.py:627
  1.4 5.0 %collective-permute-start.1 = (f32[2,512]{1,0:T(2,128)}, f32[2,512]{1,0:T(2,128)S(1)}, u32[]{:S(2)}, u32[]{:S(2)}) collective-permute-start(f32[2,512]{1,0:T(2,128)} %courant_own.5), channel_id=1, source_target_pairs={{0,1},{1,0},{2,3},{3,2},{4,5},{5,4},{6,7},{7,6},{8,9},{9,8},{10,11... | collective-permute-start | bytes 12296 | tf_op jit(solution)/shard_map/ppermute | solution.py:628
  3.0 12.3 %collective-permute-start.4 = (bf16[752,128]{1,0:T(8,128)(2,1)S(1)}, bf16[752,128]{1,0:T(8,128)(2,1)S(1)}, u32[]{:S(2)}, u32[]{:S(2)}) collective-permute-start(bf16[752,128]{1,0:T(8,128)(2,1)S(1)} %get-tuple-element.26), channel_id=1, source_target_pairs={{0,8},{8,16},{16,24},{24,0},{1,9},{9,17},{17,25},{25,1},{2,10},{10... | collective-permute-start | bytes 577544 | tf_op jit(solution)/shard_map/ppermute | solution.py:648
  4.3 10.9 %collective-permute-start.5 = (bf16[752,128]{1,0:T(8,128)(2,1)S(1)}, bf16[752,128]{1,0:T(8,128)(2,1)S(1)}, u32[]{:S(2)}, u32[]{:S(2)}) collective-permute-start(bf16[752,128]{1,0:T(8,128)(2,1)S(1)} %get-tuple-element.27), channel_id=1, source_target_pairs={{8,0},{16,8},{24,16},{0,24},{9,1},{17,9},{25,17},{1,25},{10,2},{18... | collective-permute-start | bytes 577544 | tf_op jit(solution)/shard_map/ppermute | solution.py:649
  8.5 6.8 %collective-permute-start.2 = (bf16[144,128]{1,0:T(8,128)(2,1)S(1)}, bf16[144,128]{1,0:T(8,128)(2,1)S(1)}, u32[]{:S(2)}, u32[]{:S(2)}) collective-permute-start(bf16[144,128]{1,0:T(8,128)(2,1)S(1)} %get-tuple-element.24), channel_id=1, source_target_pairs={{0,2},{4,6},{2,0},{6,4},{1,3},{5,7},{3,1},{7,5},{8,10},{12,14},{10... | collective-permute-start | bytes 110600 | tf_op jit(solution)/shard_map/ppermute | solution.py:677
  9.8 5.6 %collective-permute-start.3 = (bf16[144,128]{1,0:T(8,128)(2,1)S(1)}, bf16[144,128]{1,0:T(8,128)(2,1)S(1)}, u32[]{:S(2)}, u32[]{:S(2)}) collective-permute-start(bf16[144,128]{1,0:T(8,128)(2,1)S(1)} %get-tuple-element.25), channel_id=1, source_target_pairs={{2,4},{4,2},{3,5},{5,3},{10,12},{12,10},{11,13},{13,11},{18,20},{2... | collective-permute-start | bytes 110600 | tf_op jit(solution)/shard_map/ppermute | solution.py:678
  16.1 4.2 %collective-permute-start.6 = (bf16[1152,128]{1,0:T(8,128)(2,1)S(1)}, bf16[1152,128]{1,0:T(8,128)(2,1)S(1)}, u32[]{:S(2)}, u32[]{:S(2)}) collective-permute-start(bf16[1152,128]{1,0:T(8,128)(2,1)S(1)} %get-tuple-element.29.sides_own), channel_id=1, source_target_pairs={{0,1},{1,0},{2,3},{3,2},{4,5},{5,4},{6,7},{7,6},{8,9},{9,8},{10,11... | collective-permute-start | bytes 884744 | tf_op jit(solution)/shard_map/ppermute | solution.py:715
  18.6 6.9 %collective-permute-start.7 = (bf16[272,128]{1,0:T(8,128)(2,1)S(1)}, bf16[272,128]{1,0:T(8,128)(2,1)S(1)}, u32[]{:S(2)}, u32[]{:S(2)}) collective-permute-start(bf16[272,128]{1,0:T(8,128)(2,1)S(1)} %get-tuple-element.35), channel_id=1, source_target_pairs={{8,16},{24,0},{16,8},{0,24},{9,17},{25,1},{17,9},{1,25},{10,18},{2... | collective-permute-start | bytes 208904 | tf_op jit(solution)/shard_map/ppermute | solution.py:716
  20.3 5.4 %collective-permute-start.8 = (bf16[272,128]{1,0:T(8,128)(2,1)S(1)}, bf16[272,128]{1,0:T(8,128)(2,1)S(1)}, u32[]{:S(2)}, u32[]{:S(2)}) collective-permute-start(bf16[272,128]{1,0:T(8,128)(2,1)S(1)} %get-tuple-element.36), channel_id=1, source_target_pairs={{0,8},{16,24},{8,0},{24,16},{1,9},{17,25},{9,1},{25,17},{2,10},{18... | collective-permute-start | bytes 208904 | tf_op jit(solution)/shard_map/ppermute | solution.py:717
  20.3 5.4 %copy-start.4 = (f32[32]{0:T(128)S(1)}, f32[32]{0:T(128)}, u32[]{:S(2)}) copy-start(f32[32]{0:T(128)} %drag.1) | copy-start | bytes 388

commit v8 on v7

--- a/solution.py
+++ b/solution.py
@@ -330,11 +330,15 @@
     drag_col = jnp.zeros((levels, 1), F32)
     for level in range(levels):
         drag_col = jnp.where(at_level == level, drag[level], drag_col)
-    def copy_out(block):
+    def copies_out(block):
         rows = pl.ds(block * TILE, TILE)
-        return pltpu.make_async_copy(
-            result.at[:, :, rows, :], out.at[:, :, rows, :], sem.at[block]
-        )
+        return [
+            pltpu.make_async_copy(
+                result.at[c, some, rows, :], out.at[c, some, rows, :], sem.at[block, 2 * c + half]
+            )
+            for c in range(2)
+            for half, some in enumerate((pl.ds(0, levels // 2), pl.ds(levels // 2, levels // 2)))
+        ]
 
     half_cor = time_step * lat_coriolis(width)
     keep = 1.0 - 4.0 * time_step * viscosity - time_step * drag_col
@@ -366,13 +370,15 @@
                 result[0, :, x, :] = u_new
                 result[1, :, x, :] = v_new
                 if x % TILE == TILE - 1:
-                    copy_out(x // TILE).start()
+                    for copy in copies_out(x // TILE):
+                        copy.start()
             else:
                 target[at, :levels] = u_new
                 target[at, levels:chans] = v_new
         source, target = target, source
     for block in range(cells_x // TILE):
-        copy_out(block).wait()
+        for copy in copies_out(block):
+            copy.wait()
 
 
 def wave_groups(cells_x, width, early_pairs):
@@ -522,7 +528,9 @@
                     if seam and at == SEAM_GROUP:
                         advect_seam(n)
             finish(at - 1, piece)
-        send(at - 1)
+            if piece == blocks - 1 and height_of(at - 1) == rows_of(groups[at - 1]) == 2 * width:
+                send(at - 1, 0)
+        send(at - 1, 1)
 
 
 def inner_kernel(
@@ -548,7 +556,7 @@
     wave_body(
         groups, (None, None), (), None, inter_copies,
         f_own, f_oth, courant_own, courant_oth, mask, inter,
-        wave, lambda n: None,
+        wave, lambda n, part: None,
         (adv_a, adv_b), (sea_a, sea_b), moved,
     )
 
@@ -575,8 +583,9 @@
     send(wave, [(x, TILE_ROWS, width - TILE_ROWS) for x in seam])
     rims = [(0, TILE_ROWS), (width - TILE_ROWS, width)]
 
-    def sent(n):
-        send(slots, groups[n])
+    def sent(n, part):
+        whole = n == SEAM_GROUP or len(groups[n]) == 1
+        send(slots, groups[n] if whole else groups[n][part : part + 1])
         if n == SEAM_GROUP:
             send(slots, [(x, first, last) for x in seam for first, last in rims])
 
@@ -744,7 +753,7 @@
             pltpu.VMEM((cells_x + 2 * SUBSTEPS, chans, 2 * cells_y), F32),
             pltpu.VMEM((cells_x + 2 * SUBSTEPS - 2, chans, 2 * cells_y), F32),
             pltpu.VMEM(currents.shape, F32),
-            DMA((cells_x // TILE,)),
+            DMA((cells_x // TILE, 4)),
         ],
         10**8,
         4 * MIB,

time: 29.8 us -> 29.9 us (level)
  no operation moved by 1% of the time
where the time goes in v8:
time: 29.9 us; the launch traced here: 29.7 us
  Pallas kernels  16.7 us (56%)
  starting transfers between devices  11.8 us (39%)
  between operations  0.78 us (3%)
  waiting for transfers between devices  0.35 us (1%)
    pallas_call x1, Pallas kernels, local(): call(functools.partial(outer_kernel, outer, inner), 'outer', (wave_type,...  5.18 us
    pallas_call x1, Pallas kernels, local(): call(momentum_kernel, 'momentum', jax.ShapeDtypeStruct(currents.shape, F3...  3.91 us
    pallas_call x1, Pallas kernels, local(): call(functools.partial(inner_kernel, inner), 'inner', (wave_type, jax.Sha...  3.35 us
    ppermute x1, starting transfers between devices, local(): sides_oth = lax.ppermute(sides_own, 'comp', swap)  2.54 us
    ppermute x1, starting transfers between devices, local(): east_own = lax.ppermute(to_w, 'gx', west)  2.09 us
    ppermute x1, starting transfers between devices, local(): from_b = lax.ppermute(to_b, 'gy', pairing('gy', 1))  2.09 us
    pallas_call x1, Pallas kernels, local(): call(project_kernel, 'project', (jax.ShapeDtypeStruct((cells_x + 2, chans...  2.05 us
    ppermute x1, starting transfers between devices, local(): beside_b = lax.ppermute(to_b, 'gx', pairing('gx', 1, True))  1.66 us
  transfers between devices with their start and end apart: 9, of which 2 were waited for; matrix products, arithmetic and copies ran while one was open for 0% of the time, Pallas kernels for 41%

profile of v8, /device:TPU:5, one launch (start us, length us, event | category | flops | bytes accessed | tf_op | source)
XLA Modules:
  0.0 29.7 jit_solution(16387747697432926886)
XLA Ops:
  0.6 0.0 copy-start
  0.6 0.0 copy-start.3
  0.7 0.0 copy-start.2
  0.7 0.0 copy-start.1
  0.7 0.7 %collective-permute-start = (bf16[16,128,512]{2,1,0:T(8,128)(2,1)}, bf16[16,128,512]{2,1,0:T(8,128)(2,1)S(1)}, u32[]{:S(2)}, u32[]{:S(2)}) collective-permute-start(bf16[16,128,512]{2,1,0:T(8,128)(2,1)} %f_own.5), channel_id=1, source_target_pairs={{0,1},{1,0},{2,3},{3,2},{4,5},{5,4},{6,7},{7,6},{8,9},{9,8},{10,11... | collective-permute-start | bytes 6291464 | tf_op jit(solution)/shard_map/ppermute | solution.py:636
  1.4 0.1 collective-permute-start.1
  1.5 1.5 %outgoing.1 = (bf16[752,128]{1,0:T(8,128)(2,1)S(1)}, bf16[752,128]{1,0:T(8,128)(2,1)S(1)}, bf16[2,64,1024]{2,1,0:T(8,128)(2,1)S(1)}) custom-call(bf16[16,128,512]{2,1,0:T(8,128)(2,1)} %f_own.5, f32[2,32,16,128]{3,2,1,0:T(8,128)} %currents.3, s32[16,128]{1,0:T(8,128)} %mask.5, bf16[2,64,1024]{2,1,0:T(8,128)(2,1)} %bitcast.1), custom_call_target="tpu_custom_call" | custom-call | flops 1000000 | bytes 1048576 | tf_op jit(solution)/shard_map/outgoing/pallas_call | solution.py:641
  3.0 1.3 %collective-permute-start.4 = (bf16[752,128]{1,0:T(8,128)(2,1)S(1)}, bf16[752,128]{1,0:T(8,128)(2,1)S(1)}, u32[]{:S(2)}, u32[]{:S(2)}) collective-permute-start(bf16[752,128]{1,0:T(8,128)(2,1)S(1)} %get-tuple-element.26), channel_id=1, source_target_pairs={{0,8},{8,16},{16,24},{24,0},{1,9},{9,17},{17,25},{25,1},{2,10},{10... | collective-permute-start | bytes 577544 | tf_op jit(solution)/shard_map/ppermute | solution.py:657
  4.3 2.1 %collective-permute-start.5 = (bf16[752,128]{1,0:T(8,128)(2,1)S(1)}, bf16[752,128]{1,0:T(8,128)(2,1)S(1)}, u32[]{:S(2)}, u32[]{:S(2)}) collective-permute-start(bf16[752,128]{1,0:T(8,128)(2,1)S(1)} %get-tuple-element.27), channel_id=1, source_target_pairs={{8,0},{16,8},{24,16},{0,24},{9,1},{17,9},{25,17},{1,25},{10,2},{18... | collective-permute-start | bytes 577544 | tf_op jit(solution)/shard_map/ppermute | solution.py:658
  6.4 0.0 collective-permute-done.1.courant_oth
  6.4 0.0 collective-permute-done.f_oth
  6.4 0.0 copy-done
  6.4 0.0 copy-done.3
  6.4 0.0 copy-done.2
  6.4 0.0 copy-done.1
  6.4 2.0 %project.1 = (f32[18,64,128]{2,1,0:T(8,128)S(1)}, f32[16,64,128]{2,1,0:T(8,128)S(1)}, f32[6,64,256]{2,1,0:T(8,128)S(1)}, f32[16,80,128]{2,1,0:T(8,128)S(1)}, bf1...) custom-call(bf16[16,128,512]{2,1,0:T(8,128)(2,1)S(1)} %copy-done, ...), custom_call_target="tpu_custom_call" | custom-call | flops 3000000000 | bytes 8388608 | tf_op jit(solution)/shard_map/project/pallas_call | solution.py:661
  8.5 1.3 %collective-permute-start.2 = (bf16[144,128]{1,0:T(8,128)(2,1)S(1)}, bf16[144,128]{1,0:T(8,128)(2,1)S(1)}, u32[]{:S(2)}, u32[]{:S(2)}) collective-permute-start(bf16[144,128]{1,0:T(8,128)(2,1)S(1)} %get-tuple-element.24), channel_id=1, source_target_pairs={{0,2},{4,6},{2,0},{6,4},{1,3},{5,7},{3,1},{7,5},{8,10},{12,14},{10... | collective-permute-start | bytes 110600 | tf_op jit(solution)/shard_map/ppermute | solution.py:686
  9.8 2.1 %collective-permute-start.3 = (bf16[144,128]{1,0:T(8,128)(2,1)S(1)}, bf16[144,128]{1,0:T(8,128)(2,1)S(1)}, u32[]{:S(2)}, u32[]{:S(2)}) collective-permute-start(bf16[144,128]{1,0:T(8,128)(2,1)S(1)} %get-tuple-element.25), channel_id=1, source_target_pairs={{2,4},{4,2},{3,5},{5,3},{10,12},{12,10},{11,13},{13,11},{18,20},{2... | collective-permute-start | bytes 110600 | tf_op jit(solution)/shard_map/ppermute | solution.py:687
  11.9 3.4 %inner.1 = (bf16[16,128,512]{2,1,0:T(8,128)(2,1)S(1)}, bf16[1024,512]{1,0:T(8,128)(2,1)S(1)}, f32[8,128]{1,0:T(8,128)S(1)}) custom-call(bf16[16,128,512]{2,1,0:T(8,128)(2,1)S(1)} %copy-done, bf16[16,128,512]{2,1,0:T(8,128)(2,1)S(1)} %collective-permute-done.f_oth, f32[2,512]{1,0:T(2,128)S(1)} %copy-done.3, f32[2,512]{1,0:T(2,128)S(1)} %collective-permute-done.1.courant_oth, ...), custom_call_target="tpu_custom_call" | custom-call | flops 2000000000 | bytes 5242880 | tf_op jit(solution)/shard_map/inner/pallas_call | solution.py:700
  15.2 0.0 collective-permute-done.4.side_w
  15.2 0.0 collective-permute-done.5.side_e
  15.3 0.0 collective-permute-done.2.from_a
  15.3 0.1 collective-permute-done.3.from_b
  15.4 0.7 %relay.1 = (bf16[272,128]{1,0:T(8,128)(2,1)S(1)}, bf16[272,128]{1,0:T(8,128)(2,1)S(1)}, bf16[1152,128]{1,0:T(8,128)(2,1)S(1)}) custom-call(f32[6,64,256]{2,1,0:T(8,128)S(1)} %get-tuple-element.23.s_edge, bf16[144,128]{1,0:T(8,128)(2,1)S(1)} %collective-permute-done.2.from_a, bf16[144,128]{1,0:T(8,128)(2,1)S(1)} %collective-permute-done.3.from_b, ...), custom_call_target="tpu_custom_call" | custom-call | flops 1000000 | bytes 1048576 | tf_op jit(solution)/shard_map/relay/pallas_call | solution.py:712
  16.1 2.5 %collective-permute-start.6 = (bf16[1152,128]{1,0:T(8,128)(2,1)S(1)}, bf16[1152,128]{1,0:T(8,128)(2,1)S(1)}, u32[]{:S(2)}, u32[]{:S(2)}) collective-permute-start(bf16[1152,128]{1,0:T(8,128)(2,1)S(1)} %get-tuple-element.29.sides_own), channel_id=1, source_target_pairs={{0,1},{1,0},{2,3},{3,2},{4,5},{5,4},{6,7},{7,6},{8,9},{9,8},{10,11... | collective-permute-start | bytes 884744 | tf_op jit(solution)/shard_map/ppermute | solution.py:724
  18.6 1.7 %collective-permute-start.7 = (bf16[272,128]{1,0:T(8,128)(2,1)S(1)}, bf16[272,128]{1,0:T(8,128)(2,1)S(1)}, u32[]{:S(2)}, u32[]{:S(2)}) collective-permute-start(bf16[272,128]{1,0:T(8,128)(2,1)S(1)} %get-tuple-element.35), channel_id=1, source_target_pairs={{8,16},{24,0},{16,8},{0,24},{9,17},{25,1},{17,9},{1,25},{10,18},{2... | collective-permute-start | bytes 208904 | tf_op jit(solution)/shard_map/ppermute | solution.py:725
  20.3 0.0 collective-permute-start.8
  20.3 0.0 collective-permute-done.6.sides_oth
  20.3 5.2 %outer.1 = (bf16[16,128,512]{2,1,0:T(8,128)(2,1)}, f32[8,128]{1,0:T(8,128)S(1)}) custom-call(bf16[16,128,512]{2,1,0:T(8,128)(2,1)S(1)} %copy-done, bf16[16,128,512]{2,1,0:T(8,128)(2,1)S(1)} %collective-permute-done.f_oth, f32[2,512]{1,0:T(2,128)S(1)} %copy-done.3, f32[2,512]{1,0:T(2,128)S(1)} %collective-permute-done.1.courant_oth, s32[16,128]{1,0:T(8,128)S(1)} %copy-done.2, ...), custom_call_target="tpu_custom_call" | custom-call | flops 2000000000 | bytes 5242880 | tf_op jit(solution)/shard_map/outer/pallas_call | solution.py:728
  25.5 0.0 collective-permute-done.7.beside_b
  25.5 0.2 collective-permute-done.8.beside_a
  25.8 3.9 %momentum.1 = f32[2,32,16,128]{3,2,1,0:T(8,128)} custom-call(f32[18,64,128]{2,1,0:T(8,128)S(1)} %get-tuple-element.32.s_main, f32[16,64,128]{2,1,0:T(8,128)S(1)} %get-tuple-element.33.s_aux, f32[16,80,128]{2,1,0:T(8,128)S(1)} %get-tuple-element.34.state, bf16[752,128]{1,0:T(8,128)(2,1)S(1)} %collective-permute-done.4.side_w, ...), custom_call_target="tpu_custom_call" | custom-call | flops 100000000 | bytes 4194304 | tf_op jit(solution)/shard_map/momentum/pallas_call | solution.py:745
  (2 shorter events, 0.0 us)
Async XLA Ops:
  0.6 5.8 %copy-start = (bf16[16,128,512]{2,1,0:T(8,128)(2,1)S(1)}, bf16[16,128,512]{2,1,0:T(8,128)(2,1)}, u32[]{:S(2)}) copy-start(bf16[16,128,512]{2,1,0:T(8,128)(2,1)} %f_own.5) | copy-start | bytes 6291460
  0.6 5.8 %copy-start.3 = (f32[2,512]{1,0:T(2,128)S(1)}, f32[2,512]{1,0:T(2,128)}, u32[]{:S(2)}) copy-start(f32[2,512]{1,0:T(2,128)} %courant_own.5) | copy-start | bytes 12292
  0.7 5.8 %copy-start.2 = (s32[16,128]{1,0:T(8,128)S(1)}, s32[16,128]{1,0:T(8,128)}, u32[]{:S(2)}) copy-start(s32[16,128]{1,0:T(8,128)} %mask.5) | copy-start | bytes 24580
  0.7 5.8 %copy-start.1 = (f32[2,32,16,128]{3,2,1,0:T(8,128)S(1)}, f32[2,32,16,128]{3,2,1,0:T(8,128)}, u32[]{:S(2)}) copy-start(f32[2,32,16,128]{3,2,1,0:T(8,128)} %currents.3) | copy-start | bytes 1572868
  0.7 5.7 %collective-permute-start = (bf16[16,128,512]{2,1,0:T(8,128)(2,1)}, bf16[16,128,512]{2,1,0:T(8,128)(2,1)S(1)}, u32[]{:S(2)}, u32[]{:S(2)}) collective-permute-start(bf16[16,128,512]{2,1,0:T(8,128)(2,1)} %f_own.5), channel_id=1, source_target_pairs={{0,1},{1,0},{2,3},{3,2},{4,5},{5,4},{6,7},{7,6},{8,9},{9,8},{10,11... | collective-permute-start | bytes 6291464 | tf_op jit(solution)/shard_map/ppermute | solution.py:636
  1.4 5.0 %collective-permute-start.1 = (f32[2,512]{1,0:T(2,128)}, f32[2,512]{1,0:T(2,128)S(1)}, u32[]{:S(2)}, u32[]{:S(2)}) collective-permute-start(f32[2,512]{1,0:T(2,128)} %courant_own.5), channel_id=1, source_target_pairs={{0,1},{1,0},{2,3},{3,2},{4,5},{5,4},{6,7},{7,6},{8,9},{9,8},{10,11... | collective-permute-start | bytes 12296 | tf_op jit(solution)/shard_map/ppermute | solution.py:637
  3.0 12.3 %collective-permute-start.4 = (bf16[752,128]{1,0:T(8,128)(2,1)S(1)}, bf16[752,128]{1,0:T(8,128)(2,1)S(1)}, u32[]{:S(2)}, u32[]{:S(2)}) collective-permute-start(bf16[752,128]{1,0:T(8,128)(2,1)S(1)} %get-tuple-element.26), channel_id=1, source_target_pairs={{0,8},{8,16},{16,24},{24,0},{1,9},{9,17},{17,25},{25,1},{2,10},{10... | collective-permute-start | bytes 577544 | tf_op jit(solution)/shard_map/ppermute | solution.py:657
  4.3 10.9 %collective-permute-start.5 = (bf16[752,128]{1,0:T(8,128)(2,1)S(1)}, bf16[752,128]{1,0:T(8,128)(2,1)S(1)}, u32[]{:S(2)}, u32[]{:S(2)}) collective-permute-start(bf16[752,128]{1,0:T(8,128)(2,1)S(1)} %get-tuple-element.27), channel_id=1, source_target_pairs={{8,0},{16,8},{24,16},{0,24},{9,1},{17,9},{25,17},{1,25},{10,2},{18... | collective-permute-start | bytes 577544 | tf_op jit(solution)/shard_map/ppermute | solution.py:658
  8.5 6.8 %collective-permute-start.2 = (bf16[144,128]{1,0:T(8,128)(2,1)S(1)}, bf16[144,128]{1,0:T(8,128)(2,1)S(1)}, u32[]{:S(2)}, u32[]{:S(2)}) collective-permute-start(bf16[144,128]{1,0:T(8,128)(2,1)S(1)} %get-tuple-element.24), channel_id=1, source_target_pairs={{0,2},{4,6},{2,0},{6,4},{1,3},{5,7},{3,1},{7,5},{8,10},{12,14},{10... | collective-permute-start | bytes 110600 | tf_op jit(solution)/shard_map/ppermute | solution.py:686
  9.8 5.6 %collective-permute-start.3 = (bf16[144,128]{1,0:T(8,128)(2,1)S(1)}, bf16[144,128]{1,0:T(8,128)(2,1)S(1)}, u32[]{:S(2)}, u32[]{:S(2)}) collective-permute-start(bf16[144,128]{1,0:T(8,128)(2,1)S(1)} %get-tuple-element.25), channel_id=1, source_target_pairs={{2,4},{4,2},{3,5},{5,3},{10,12},{12,10},{11,13},{13,11},{18,20},{2... | collective-permute-start | bytes 110600 | tf_op jit(solution)/shard_map/ppermute | solution.py:687
  16.1 4.2 %collective-permute-start.6 = (bf16[1152,128]{1,0:T(8,128)(2,1)S(1)}, bf16[1152,128]{1,0:T(8,128)(2,1)S(1)}, u32[]{:S(2)}, u32[]{:S(2)}) collective-permute-start(bf16[1152,128]{1,0:T(8,128)(2,1)S(1)} %get-tuple-element.29.sides_own), channel_id=1, source_target_pairs={{0,1},{1,0},{2,3},{3,2},{4,5},{5,4},{6,7},{7,6},{8,9},{9,8},{10,11... | collective-permute-start | bytes 884744 | tf_op jit(solution)/shard_map/ppermute | solution.py:724
  18.6 6.9 %collective-permute-start.7 = (bf16[272,128]{1,0:T(8,128)(2,1)S(1)}, bf16[272,128]{1,0:T(8,128)(2,1)S(1)}, u32[]{:S(2)}, u32[]{:S(2)}) collective-permute-start(bf16[272,128]{1,0:T(8,128)(2,1)S(1)} %get-tuple-element.35), channel_id=1, source_target_pairs={{8,16},{24,0},{16,8},{0,24},{9,17},{25,1},{17,9},{1,25},{10,18},{2... | collective-permute-start | bytes 208904 | tf_op jit(solution)/shard_map/ppermute | solution.py:725
  20.3 5.4 %collective-permute-start.8 = (bf16[272,128]{1,0:T(8,128)(2,1)S(1)}, bf16[272,128]{1,0:T(8,128)(2,1)S(1)}, u32[]{:S(2)}, u32[]{:S(2)}) collective-permute-start(bf16[272,128]{1,0:T(8,128)(2,1)S(1)} %get-tuple-element.36), channel_id=1, source_target_pairs={{0,8},{16,24},{8,0},{24,16},{1,9},{17,25},{9,1},{25,17},{2,10},{18... | collective-permute-start | bytes 208904 | tf_op jit(solution)/shard_map/ppermute | solution.py:726
  20.3 5.4 %copy-start.4 = (f32[32]{0:T(128)S(1)}, f32[32]{0:T(128)}, u32[]{:S(2)}) copy-start(f32[32]{0:T(128)} %drag.1) | copy-start | bytes 388

commit v9 on v7

--- a/solution.py
+++ b/solution.py
@@ -241,32 +241,33 @@
     lane = lane_of(chans, width)
     lane_f = lane_of(fields, width)
     tile_s, tile_n = from_sides(from_a, from_b, slice(0, fields))
-    def build(east, west):
-        for msg, first, first_cur, first_edge in (
-            (east, cells_x - 2, cells_x - EDGE, EDGE),
-            (west, -1, 0, 0),
-        ):
-            tile = jnp.zeros((chans, width), F32)
-            cur_tile = jnp.zeros((fields, width), F32)
-            for i in range(EDGE):
-                edge = s_edge[first_edge + i]
-                start = stokes_lane(first + i)
-                main, aux = stokes_row(
-                    edge[:, :width], edge[:, width:], tile_s[:chans], tile_n[:chans], start, lane, width
-                )
-                msg[i * chans : (i + 1) * chans] = main.astype(BF16)
-                at = SLOT * i
-                tile = jnp.where(between(lane, at, at + 6), pltpu.roll(aux, at + 3, 1), tile)
-                ring = current_halo(tile_s, tile_n, first_cur + i, cells_x, lane_f, width)
-                at += half
-                cur_tile = jnp.where(between(lane_f, at, at + 6), pltpu.roll(ring, at + 3, 1), cur_tile)
-            base = EDGE * chans
-            msg[base : base + chans] = (tile + cur_tile[:chans]).astype(BF16)
-            msg[base + chans : base + fields] = cur_tile[chans:].astype(BF16)
+    def build(first, first_cur, first_edge):
+        pieces = []
+        tile = jnp.zeros((chans, width), F32)
+        cur_tile = jnp.zeros((fields, width), F32)
+        for i in range(EDGE):
+            edge = s_edge[first_edge + i]
+            start = stokes_lane(first + i)
+            main, aux = stokes_row(
+                edge[:, :width], edge[:, width:], tile_s[:chans], tile_n[:chans], start, lane, width
+            )
+            pieces.append((slice(i * chans, (i + 1) * chans), main))
+            at = SLOT * i
+            tile = jnp.where(between(lane, at, at + 6), pltpu.roll(aux, at + 3, 1), tile)
+            ring = current_halo(tile_s, tile_n, first_cur + i, cells_x, lane_f, width)
+            at += half
+            cur_tile = jnp.where(between(lane_f, at, at + 6), pltpu.roll(ring, at + 3, 1), cur_tile)
+        base = EDGE * chans
+        pieces.append((slice(base, base + chans), tile + cur_tile[:chans]))
+        pieces.append((slice(base + chans, base + fields), cur_tile[chans:]))
+        return pieces
 
     even = is_even("gx")
-    pl.when(even)(functools.partial(build, msg_a, msg_b))
-    pl.when(~even)(functools.partial(build, msg_b, msg_a))
+    east = build(cells_x - 2, cells_x - EDGE, EDGE)
+    west = build(-1, 0, 0)
+    for (rows, to_east), (_, to_west) in zip(east, west, strict=True):
+        msg_a[rows] = jnp.where(even, to_east, to_west).astype(BF16)
+        msg_b[rows] = jnp.where(even, to_west, to_east).astype(BF16)
 
 
 def lat_coriolis(cells_y):

time: 29.8 us -> 29.8 us (level)
  no operation moved by 1% of the time
where the time goes in v9:
time: 29.8 us; the launch traced here: 29.5 us
  Pallas kernels  16.6 us (56%)
  starting transfers between devices  11.8 us (40%)
  between operations  0.78 us (3%)
  waiting for transfers between devices  0.3 us (1%)
    pallas_call x1, Pallas kernels, local(): call(functools.partial(outer_kernel, outer, inner), 'outer', (wave_type,...  5.23 us
    pallas_call x1, Pallas kernels, local(): call(momentum_kernel, 'momentum', jax.ShapeDtypeStruct(currents.shape, F3...  3.87 us
    pallas_call x1, Pallas kernels, local(): call(functools.partial(inner_kernel, inner), 'inner', (wave_type, jax.Sha...  3.35 us
    ppermute x1, starting transfers between devices, local(): sides_oth = lax.ppermute(sides_own, 'comp', swap)  2.54 us
    ppermute x1, starting transfers between devices, local(): east_own = lax.ppermute(to_w, 'gx', west)  2.09 us
    ppermute x1, starting transfers between devices, local(): from_b = lax.ppermute(to_b, 'gy', pairing('gy', 1))  2.09 us
    pallas_call x1, Pallas kernels, local(): call(project_kernel, 'project', (jax.ShapeDtypeStruct((cells_x + 2, chans...  2.05 us
    ppermute x1, starting transfers between devices, local(): beside_b = lax.ppermute(to_b, 'gx', pairing('gx', 1, True))  1.66 us
  transfers between devices with their start and end apart: 9, of which 2 were waited for; matrix products, arithmetic and copies ran while one was open for 0% of the time, Pallas kernels for 41%

profile of v9, /device:TPU:5, one launch (start us, length us, event | category | flops | bytes accessed | tf_op | source)
XLA Modules:
  0.0 29.5 jit_solution(6626485162546645714)
XLA Ops:
  0.6 0.0 copy-start
  0.6 0.0 copy-start.3
  0.7 0.0 copy-start.2
  0.7 0.0 copy-start.1
  0.7 0.7 %collective-permute-start = (bf16[16,128,512]{2,1,0:T(8,128)(2,1)}, bf16[16,128,512]{2,1,0:T(8,128)(2,1)S(1)}, u32[]{:S(2)}, u32[]{:S(2)}) collective-permute-start(bf16[16,128,512]{2,1,0:T(8,128)(2,1)} %f_own.5), channel_id=1, source_target_pairs={{0,1},{1,0},{2,3},{3,2},{4,5},{5,4},{6,7},{7,6},{8,9},{9,8},{10,11... | collective-permute-start | bytes 6291464 | tf_op jit(solution)/shard_map/ppermute | solution.py:628
  1.4 0.1 collective-permute-start.1
  1.5 1.5 %outgoing.1 = (bf16[752,128]{1,0:T(8,128)(2,1)S(1)}, bf16[752,128]{1,0:T(8,128)(2,1)S(1)}, bf16[2,64,1024]{2,1,0:T(8,128)(2,1)S(1)}) custom-call(bf16[16,128,512]{2,1,0:T(8,128)(2,1)} %f_own.5, f32[2,32,16,128]{3,2,1,0:T(8,128)} %currents.3, s32[16,128]{1,0:T(8,128)} %mask.5, bf16[2,64,1024]{2,1,0:T(8,128)(2,1)} %bitcast.1), custom_call_target="tpu_custom_call" | custom-call | flops 1000000 | bytes 1048576 | tf_op jit(solution)/shard_map/outgoing/pallas_call | solution.py:633
  3.0 1.3 %collective-permute-start.4 = (bf16[752,128]{1,0:T(8,128)(2,1)S(1)}, bf16[752,128]{1,0:T(8,128)(2,1)S(1)}, u32[]{:S(2)}, u32[]{:S(2)}) collective-permute-start(bf16[752,128]{1,0:T(8,128)(2,1)S(1)} %get-tuple-element.26), channel_id=1, source_target_pairs={{0,8},{8,16},{16,24},{24,0},{1,9},{9,17},{17,25},{25,1},{2,10},{10... | collective-permute-start | bytes 577544 | tf_op jit(solution)/shard_map/ppermute | solution.py:649
  4.3 2.1 %collective-permute-start.5 = (bf16[752,128]{1,0:T(8,128)(2,1)S(1)}, bf16[752,128]{1,0:T(8,128)(2,1)S(1)}, u32[]{:S(2)}, u32[]{:S(2)}) collective-permute-start(bf16[752,128]{1,0:T(8,128)(2,1)S(1)} %get-tuple-element.27), channel_id=1, source_target_pairs={{8,0},{16,8},{24,16},{0,24},{9,1},{17,9},{25,17},{1,25},{10,2},{18... | collective-permute-start | bytes 577544 | tf_op jit(solution)/shard_map/ppermute | solution.py:650
  6.4 0.0 collective-permute-done.1.courant_oth
  6.4 0.0 collective-permute-done.f_oth
  6.4 0.0 copy-done
  6.4 0.0 copy-done.3
  6.4 0.0 copy-done.2
  6.4 2.0 %project.1 = (f32[18,64,128]{2,1,0:T(8,128)S(1)}, f32[16,64,128]{2,1,0:T(8,128)S(1)}, f32[6,64,256]{2,1,0:T(8,128)S(1)}, f32[16,80,128]{2,1,0:T(8,128)S(1)}, bf1...) custom-call(bf16[16,128,512]{2,1,0:T(8,128)(2,1)S(1)} %copy-done, ...), custom_call_target="tpu_custom_call" | custom-call | flops 3000000000 | bytes 8388608 | tf_op jit(solution)/shard_map/project/pallas_call | solution.py:653
  8.5 1.3 %collective-permute-start.2 = (bf16[144,128]{1,0:T(8,128)(2,1)S(1)}, bf16[144,128]{1,0:T(8,128)(2,1)S(1)}, u32[]{:S(2)}, u32[]{:S(2)}) collective-permute-start(bf16[144,128]{1,0:T(8,128)(2,1)S(1)} %get-tuple-element.24), channel_id=1, source_target_pairs={{0,2},{4,6},{2,0},{6,4},{1,3},{5,7},{3,1},{7,5},{8,10},{12,14},{10... | collective-permute-start | bytes 110600 | tf_op jit(solution)/shard_map/ppermute | solution.py:678
  9.8 2.1 %collective-permute-start.3 = (bf16[144,128]{1,0:T(8,128)(2,1)S(1)}, bf16[144,128]{1,0:T(8,128)(2,1)S(1)}, u32[]{:S(2)}, u32[]{:S(2)}) collective-permute-start(bf16[144,128]{1,0:T(8,128)(2,1)S(1)} %get-tuple-element.25), channel_id=1, source_target_pairs={{2,4},{4,2},{3,5},{5,3},{10,12},{12,10},{11,13},{13,11},{18,20},{2... | collective-permute-start | bytes 110600 | tf_op jit(solution)/shard_map/ppermute | solution.py:679
  11.9 3.4 %inner.1 = (bf16[16,128,512]{2,1,0:T(8,128)(2,1)S(1)}, bf16[1024,512]{1,0:T(8,128)(2,1)S(1)}, f32[8,128]{1,0:T(8,128)S(1)}) custom-call(bf16[16,128,512]{2,1,0:T(8,128)(2,1)S(1)} %copy-done, bf16[16,128,512]{2,1,0:T(8,128)(2,1)S(1)} %collective-permute-done.f_oth, f32[2,512]{1,0:T(2,128)S(1)} %copy-done.3, f32[2,512]{1,0:T(2,128)S(1)} %collective-permute-done.1.courant_oth, ...), custom_call_target="tpu_custom_call" | custom-call | flops 2000000000 | bytes 5242880 | tf_op jit(solution)/shard_map/inner/pallas_call | solution.py:692
  15.2 0.0 collective-permute-done.4.side_w
  15.2 0.0 collective-permute-done.5.side_e
  15.3 0.0 collective-permute-done.2.from_a
  15.3 0.1 collective-permute-done.3.from_b
  15.4 0.7 %relay.1 = (bf16[272,128]{1,0:T(8,128)(2,1)S(1)}, bf16[272,128]{1,0:T(8,128)(2,1)S(1)}, bf16[1152,128]{1,0:T(8,128)(2,1)S(1)}) custom-call(f32[6,64,256]{2,1,0:T(8,128)S(1)} %get-tuple-element.23.s_edge, bf16[144,128]{1,0:T(8,128)(2,1)S(1)} %collective-permute-done.2.from_a, bf16[144,128]{1,0:T(8,128)(2,1)S(1)} %collective-permute-done.3.from_b, ...), custom_call_target="tpu_custom_call" | custom-call | flops 1000000 | bytes 1048576 | tf_op jit(solution)/shard_map/relay/pallas_call | solution.py:704
  16.0 2.5 %collective-permute-start.6 = (bf16[1152,128]{1,0:T(8,128)(2,1)S(1)}, bf16[1152,128]{1,0:T(8,128)(2,1)S(1)}, u32[]{:S(2)}, u32[]{:S(2)}) collective-permute-start(bf16[1152,128]{1,0:T(8,128)(2,1)S(1)} %get-tuple-element.29.sides_own), channel_id=1, source_target_pairs={{0,1},{1,0},{2,3},{3,2},{4,5},{5,4},{6,7},{7,6},{8,9},{9,8},{10,11... | collective-permute-start | bytes 884744 | tf_op jit(solution)/shard_map/ppermute | solution.py:716
  18.6 1.7 %collective-permute-start.7 = (bf16[272,128]{1,0:T(8,128)(2,1)S(1)}, bf16[272,128]{1,0:T(8,128)(2,1)S(1)}, u32[]{:S(2)}, u32[]{:S(2)}) collective-permute-start(bf16[272,128]{1,0:T(8,128)(2,1)S(1)} %get-tuple-element.35), channel_id=1, source_target_pairs={{8,16},{24,0},{16,8},{0,24},{9,17},{25,1},{17,9},{1,25},{10,18},{2... | collective-permute-start | bytes 208904 | tf_op jit(solution)/shard_map/ppermute | solution.py:717
  20.2 0.0 collective-permute-start.8
  20.2 0.0 collective-permute-done.6.sides_oth
  20.2 5.2 %outer.1 = (bf16[16,128,512]{2,1,0:T(8,128)(2,1)}, f32[8,128]{1,0:T(8,128)S(1)}) custom-call(bf16[16,128,512]{2,1,0:T(8,128)(2,1)S(1)} %copy-done, bf16[16,128,512]{2,1,0:T(8,128)(2,1)S(1)} %collective-permute-done.f_oth, f32[2,512]{1,0:T(2,128)S(1)} %copy-done.3, f32[2,512]{1,0:T(2,128)S(1)} %collective-permute-done.1.courant_oth, s32[16,128]{1,0:T(8,128)S(1)} %copy-done.2, ...), custom_call_target="tpu_custom_call" | custom-call | flops 2000000000 | bytes 5242880 | tf_op jit(solution)/shard_map/outer/pallas_call | solution.py:720
  25.5 0.0 collective-permute-done.7.beside_b
  25.5 0.2 collective-permute-done.8.beside_a
  25.7 0.0 copy-done.4
  25.7 3.9 %momentum.1 = f32[2,32,16,128]{3,2,1,0:T(8,128)} custom-call(f32[18,64,128]{2,1,0:T(8,128)S(1)} %get-tuple-element.32.s_main, f32[16,64,128]{2,1,0:T(8,128)S(1)} %get-tuple-element.33.s_aux, f32[16,80,128]{2,1,0:T(8,128)S(1)} %get-tuple-element.34.state, bf16[752,128]{1,0:T(8,128)(2,1)S(1)} %collective-permute-done.4.side_w, ...), custom_call_target="tpu_custom_call" | custom-call | flops 100000000 | bytes 4194304 | tf_op jit(solution)/shard_map/momentum/pallas_call | solution.py:737
  (2 shorter events, 0.0 us)
Async XLA Ops:
  0.6 5.8 %copy-start = (bf16[16,128,512]{2,1,0:T(8,128)(2,1)S(1)}, bf16[16,128,512]{2,1,0:T(8,128)(2,1)}, u32[]{:S(2)}) copy-start(bf16[16,128,512]{2,1,0:T(8,128)(2,1)} %f_own.5) | copy-start | bytes 6291460
  0.6 5.8 %copy-start.3 = (f32[2,512]{1,0:T(2,128)S(1)}, f32[2,512]{1,0:T(2,128)}, u32[]{:S(2)}) copy-start(f32[2,512]{1,0:T(2,128)} %courant_own.5) | copy-start | bytes 12292
  0.7 5.8 %copy-start.2 = (s32[16,128]{1,0:T(8,128)S(1)}, s32[16,128]{1,0:T(8,128)}, u32[]{:S(2)}) copy-start(s32[16,128]{1,0:T(8,128)} %mask.5) | copy-start | bytes 24580
  0.7 5.8 %copy-start.1 = (f32[2,32,16,128]{3,2,1,0:T(8,128)S(1)}, f32[2,32,16,128]{3,2,1,0:T(8,128)}, u32[]{:S(2)}) copy-start(f32[2,32,16,128]{3,2,1,0:T(8,128)} %currents.3) | copy-start | bytes 1572868
  0.7 5.7 %collective-permute-start = (bf16[16,128,512]{2,1,0:T(8,128)(2,1)}, bf16[16,128,512]{2,1,0:T(8,128)(2,1)S(1)}, u32[]{:S(2)}, u32[]{:S(2)}) collective-permute-start(bf16[16,128,512]{2,1,0:T(8,128)(2,1)} %f_own.5), channel_id=1, source_target_pairs={{0,1},{1,0},{2,3},{3,2},{4,5},{5,4},{6,7},{7,6},{8,9},{9,8},{10,11... | collective-permute-start | bytes 6291464 | tf_op jit(solution)/shard_map/ppermute | solution.py:628
  1.4 5.0 %collective-permute-start.1 = (f32[2,512]{1,0:T(2,128)}, f32[2,512]{1,0:T(2,128)S(1)}, u32[]{:S(2)}, u32[]{:S(2)}) collective-permute-start(f32[2,512]{1,0:T(2,128)} %courant_own.5), channel_id=1, source_target_pairs={{0,1},{1,0},{2,3},{3,2},{4,5},{5,4},{6,7},{7,6},{8,9},{9,8},{10,11... | collective-permute-start | bytes 12296 | tf_op jit(solution)/shard_map/ppermute | solution.py:629
  3.0 12.3 %collective-permute-start.4 = (bf16[752,128]{1,0:T(8,128)(2,1)S(1)}, bf16[752,128]{1,0:T(8,128)(2,1)S(1)}, u32[]{:S(2)}, u32[]{:S(2)}) collective-permute-start(bf16[752,128]{1,0:T(8,128)(2,1)S(1)} %get-tuple-element.26), channel_id=1, source_target_pairs={{0,8},{8,16},{16,24},{24,0},{1,9},{9,17},{17,25},{25,1},{2,10},{10... | collective-permute-start | bytes 577544 | tf_op jit(solution)/shard_map/ppermute | solution.py:649
  4.3 10.9 %collective-permute-start.5 = (bf16[752,128]{1,0:T(8,128)(2,1)S(1)}, bf16[752,128]{1,0:T(8,128)(2,1)S(1)}, u32[]{:S(2)}, u32[]{:S(2)}) collective-permute-start(bf16[752,128]{1,0:T(8,128)(2,1)S(1)} %get-tuple-element.27), channel_id=1, source_target_pairs={{8,0},{16,8},{24,16},{0,24},{9,1},{17,9},{25,17},{1,25},{10,2},{18... | collective-permute-start | bytes 577544 | tf_op jit(solution)/shard_map/ppermute | solution.py:650
  8.5 6.8 %collective-permute-start.2 = (bf16[144,128]{1,0:T(8,128)(2,1)S(1)}, bf16[144,128]{1,0:T(8,128)(2,1)S(1)}, u32[]{:S(2)}, u32[]{:S(2)}) collective-permute-start(bf16[144,128]{1,0:T(8,128)(2,1)S(1)} %get-tuple-element.24), channel_id=1, source_target_pairs={{0,2},{4,6},{2,0},{6,4},{1,3},{5,7},{3,1},{7,5},{8,10},{12,14},{10... | collective-permute-start | bytes 110600 | tf_op jit(solution)/shard_map/ppermute | solution.py:678
  9.8 5.6 %collective-permute-start.3 = (bf16[144,128]{1,0:T(8,128)(2,1)S(1)}, bf16[144,128]{1,0:T(8,128)(2,1)S(1)}, u32[]{:S(2)}, u32[]{:S(2)}) collective-permute-start(bf16[144,128]{1,0:T(8,128)(2,1)S(1)} %get-tuple-element.25), channel_id=1, source_target_pairs={{2,4},{4,2},{3,5},{5,3},{10,12},{12,10},{11,13},{13,11},{18,20},{2... | collective-permute-start | bytes 110600 | tf_op jit(solution)/shard_map/ppermute | solution.py:679
  16.0 4.2 %collective-permute-start.6 = (bf16[1152,128]{1,0:T(8,128)(2,1)S(1)}, bf16[1152,128]{1,0:T(8,128)(2,1)S(1)}, u32[]{:S(2)}, u32[]{:S(2)}) collective-permute-start(bf16[1152,128]{1,0:T(8,128)(2,1)S(1)} %get-tuple-element.29.sides_own), channel_id=1, source_target_pairs={{0,1},{1,0},{2,3},{3,2},{4,5},{5,4},{6,7},{7,6},{8,9},{9,8},{10,11... | collective-permute-start | bytes 884744 | tf_op jit(solution)/shard_map/ppermute | solution.py:716
  18.6 6.9 %collective-permute-start.7 = (bf16[272,128]{1,0:T(8,128)(2,1)S(1)}, bf16[272,128]{1,0:T(8,128)(2,1)S(1)}, u32[]{:S(2)}, u32[]{:S(2)}) collective-permute-start(bf16[272,128]{1,0:T(8,128)(2,1)S(1)} %get-tuple-element.35), channel_id=1, source_target_pairs={{8,16},{24,0},{16,8},{0,24},{9,17},{25,1},{17,9},{1,25},{10,18},{2... | collective-permute-start | bytes 208904 | tf_op jit(solution)/shard_map/ppermute | solution.py:717
  20.2 5.4 %collective-permute-start.8 = (bf16[272,128]{1,0:T(8,128)(2,1)S(1)}, bf16[272,128]{1,0:T(8,128)(2,1)S(1)}, u32[]{:S(2)}, u32[]{:S(2)}) collective-permute-start(bf16[272,128]{1,0:T(8,128)(2,1)S(1)} %get-tuple-element.36), channel_id=1, source_target_pairs={{0,8},{16,24},{8,0},{24,16},{1,9},{17,25},{9,1},{25,17},{2,10},{18... | collective-permute-start | bytes 208904 | tf_op jit(solution)/shard_map/ppermute | solution.py:718
  20.2 5.4 %copy-start.4 = (f32[32]{0:T(128)S(1)}, f32[32]{0:T(128)}, u32[]{:S(2)}) copy-start(f32[32]{0:T(128)} %drag.1) | copy-start | bytes 388
